TPU v7x, 32 devices: a whole 2x2x4 slice. The times are simulated.
32 devices in a mesh: section: 2 (over core), dp: 4 (over y, x), seq: 4 (over z).
Axes of the slice: x: 2, y: 2, z: 4, core: 2. Of those that a mesh axis runs over, the one named last changes fastest.
Arguments:
- inputs: bfloat16 [2, 4, 1280, 1024], P(None, 'dp', 'seq'), may hold values from -6 to 6
- cotangent: bfloat16 [2, 4, 1280, 1024], P(None, 'dp', 'seq'), may hold values from -6 to 6
- view_tokens: int32 [2, 4, 6], P(None, 'dp'), may hold values from 0 to 128, as said below
- ln1_gain: bfloat16 [2, 1024], P('section'), may hold values from 0.099609375 to 1.8984375
- ln1_bias: bfloat16 [2, 1024], P('section'), may hold values from -3 to 3
- w_qkv: bfloat16 [2, 1024, 3072], P('section'), may hold values from -0.1875 to 0.1875
- b_query: bfloat16 [2, 1024], P('section'), may hold values from -3 to 3
- b_value: bfloat16 [2, 1024], P('section'), may hold values from -0.29882812 to 0.29882812
- w_out: bfloat16 [2, 1024, 1024], P('section'), may hold values from -3 to 3
- b_out: bfloat16 [2, 1024], P('section'), may hold values from -3 to 3
- ln2_gain: bfloat16 [2, 1024], P('section'), may hold values from 0.099609375 to 1.8984375
- ln2_bias: bfloat16 [2, 1024], P('section'), may hold values from -3 to 3
- w_up: bfloat16 [2, 1024, 4096], P('section'), may hold values from -0.1875 to 0.1875
- b_up: bfloat16 [2, 4096], P('section'), may hold values from -3 to 3
- w_down: bfloat16 [2, 4096, 1024], P('section'), may hold values from -0.09375 to 0.09375
- b_down: bfloat16 [2, 1024], P('section'), may hold values from -3 to 3
Outputs:
- activations: bfloat16 [2, 2, 4, 1280, 1024], P('section', None, 'dp', 'seq')
- input_grad: bfloat16 [2, 2, 4, 1280, 1024], P('section', None, 'dp', 'seq')
- g_ln1_gain: float32 [2, 1024], P('section', ('dp', 'seq'))
- g_ln1_bias: float32 [2, 1024], P('section', ('dp', 'seq'))
- g_w_qkv: float32 [2, 1024, 3072], P('section', None, ('dp', 'seq'))
- g_b_query: float32 [2, 1024], P('section', ('dp', 'seq'))
- g_b_value: float32 [2, 1024], P('section', ('dp', 'seq'))
- g_w_out: float32 [2, 1024, 1024], P('section', None, ('dp', 'seq'))
- g_b_out: float32 [2, 1024], P('section', ('dp', 'seq'))
- g_ln2_gain: float32 [2, 1024], P('section', ('dp', 'seq'))
- g_ln2_bias: float32 [2, 1024], P('section', ('dp', 'seq'))
- g_w_up: float32 [2, 1024, 4096], P('section', None, ('dp', 'seq'))
- g_b_up: float32 [2, 4096], P('section', ('dp', 'seq'))
- g_w_down: float32 [2, 4096, 1024], P('section', None, ('dp', 'seq'))
- g_b_down: float32 [2, 1024], P('section', ('dp', 'seq'))
Inputs may be any that keep to these rules, and one draw needn't show every extreme that they name: view_tokens[m, s, i] counts the valid tokens of view i of scene s in micro-batch m; its 128 slots follow the 512 triplane tokens and the slots of earlier views, and its valid tokens come first. A scene has 2 to 6 views, which take the first slots; a present view has 32 to 128 valid tokens, the first view of each scene exactly 128; absent views hold 0.
All inputs are finite; a program needn't handle non-finite values.
Results may differ from a plain program's by a relative error of at most 0.015.
Values may be sent and summed in bfloat16 or wider, within the bound.
A program may use at most 448 MiB of HBM per device.

v0:
```python
import math

import jax
import jax.numpy as jnp
from jax import lax
from jax.sharding import PartitionSpec as P

D = 1024
H = 16
DH = 64
FF = 4096
VIEWS = 6
TRI = 512
VSLOT = 128
MICRO = 2
LEN = 1280


def passed_along(value, axis, steps):
    count = lax.axis_size(axis)
    initial, last = (max(0, -steps), min(count, count - steps))
    return lax.ppermute(value, axis, [(source, source + steps) for source in range(initial, last)])


def layer_norm(values, norm_gain, norm_bias):
    average = jnp.mean(values, axis=-1, keepdims=True)
    centered = values - average
    variance = jnp.mean(centered * centered, axis=-1, keepdims=True)
    return centered * lax.rsqrt(variance + 1e-05) * norm_gain + norm_bias


def gelu_tanh(upper):
    return jax.nn.gelu(upper, approximate=True)


def key_valid(counts):
    places = jnp.arange(LEN, dtype=jnp.int32)
    offset = jnp.maximum(places - TRI, 0)
    view_index = offset // VSLOT
    inside = offset - view_index * VSLOT
    match = view_index[:, None] == jnp.arange(VIEWS, dtype=jnp.int32)[None, :]
    limits = jnp.sum(jnp.where(match, counts[None, :], 0), axis=1)
    return (places < TRI) | (inside < limits)


def pack_grads(grads, groups):
    pieces = []
    for grad in grads:
        leading = grad.shape[:-1]
        width = grad.shape[-1]
        split = grad.reshape(leading + (groups, width // groups))
        split = jnp.moveaxis(split, -2, 0)
        pieces.append(split.reshape(groups, -1))
    return jnp.concatenate(pieces, axis=1)


def unpack_grads(packed, shapes, groups):
    outputs = []
    offset = 0
    for shape in shapes:
        shard_shape = tuple(shape[:-1]) + (shape[-1] // groups,)
        length = math.prod(shard_shape)
        outputs.append(packed[0, offset : offset + length].reshape(shard_shape))
        offset = offset + length
    return tuple(outputs)


def weight_grads_from(records, small_terms):

    def joined(index):
        return jnp.concatenate([r[index] for r in records], axis=0)

    normed, d_joint, mixed, d_branch, normed_two, d_upper, gated, d_output = (
        joined(i) for i in range(8)
    )
    g_joint = jnp.einsum("td,tc->dc", normed, d_joint, preferred_element_type=jnp.float32)
    g_query = jnp.sum(d_joint[:, :D].astype(jnp.float32), axis=0)
    g_value = jnp.sum(d_joint[:, 2 * D :].astype(jnp.float32), axis=0)
    g_proj = jnp.einsum("td,te->de", mixed, d_branch, preferred_element_type=jnp.float32)
    g_proj_bias = jnp.sum(d_branch.astype(jnp.float32), axis=0)
    g_upper = jnp.einsum("td,tf->df", normed_two, d_upper, preferred_element_type=jnp.float32)
    g_upper_bias = jnp.sum(d_upper.astype(jnp.float32), axis=0)
    g_lower = jnp.einsum("tf,td->fd", gated, d_output, preferred_element_type=jnp.float32)
    g_lower_bias = jnp.sum(d_output.astype(jnp.float32), axis=0)
    g_gain_one = sum((s[0] for s in small_terms))
    g_bias_one = sum((s[1] for s in small_terms))
    g_gain_two = sum((s[2] for s in small_terms))
    g_bias_two = sum((s[3] for s in small_terms))
    return (
        g_gain_one,
        g_bias_one,
        g_joint,
        g_query,
        g_value,
        g_proj,
        g_proj_bias,
        g_gain_two,
        g_bias_two,
        g_upper,
        g_upper_bias,
        g_lower,
        g_lower_bias,
    )


def shards(
    inputs,
    cotangent,
    view_tokens,
    ln1_gain,
    ln1_bias,
    w_qkv,
    b_query,
    b_value,
    w_out,
    b_out,
    ln2_gain,
    ln2_bias,
    w_up,
    b_up,
    w_down,
    b_down,
):
    section = lax.axis_index("section")
    groups = lax.axis_size(("dp", "seq"))
    rows = inputs.shape[2]
    scale = DH ** (-0.5)
    gain_one = ln1_gain[0].astype(jnp.float32)
    shift_one = ln1_bias[0].astype(jnp.float32)
    w_joint = w_qkv[0]
    bias_query = b_query[0].astype(jnp.float32)
    bias_value = b_value[0].astype(jnp.float32)
    w_proj = w_out[0]
    bias_proj = b_out[0].astype(jnp.float32)
    gain_two = ln2_gain[0].astype(jnp.float32)
    shift_two = ln2_bias[0].astype(jnp.float32)
    w_upper = w_up[0]
    bias_upper = b_up[0].astype(jnp.float32)
    w_lower = w_down[0]
    bias_lower = b_down[0].astype(jnp.float32)
    scene_counts = view_tokens[:, 0]
    grad_shapes = (
        (D,),
        (D,),
        (D, 3 * D),
        (D,),
        (D,),
        (D, D),
        (D,),
        (D,),
        (D,),
        (D, FF),
        (FF,),
        (FF, D),
        (D,),
    )

    def counts_of(micro):
        return lax.dynamic_index_in_dim(
            scene_counts, jnp.clip(micro, 0, MICRO - 1), 0, keepdims=False
        )

    def score_rows(queries, keys_all, valid):
        scores = (
            jnp.einsum(
                "qhd,khd->hqk",
                queries.reshape(rows, H, DH),
                keys_all.reshape(-1, H, DH),
                preferred_element_type=jnp.float32,
            )
            * scale
        )
        return jnp.where(valid[None, None, :], scores, -1e30)

    zero_rows = jnp.zeros((rows, D), jnp.bfloat16)
    received = zero_rows
    saved = []
    forward_outs = []
    for tick in range(MICRO + 1):
        micro = tick - section
        valid = key_valid(counts_of(micro))
        own_rows = inputs[min(tick, MICRO - 1), 0]
        layer_in = jnp.where(section == 0, own_rows, received)
        start = layer_in.astype(jnp.float32)
        normed = layer_norm(start, gain_one, shift_one).astype(jnp.bfloat16)
        joined = jnp.dot(normed, w_joint, preferred_element_type=jnp.float32)
        project_queries = (joined[:, :D] + bias_query).astype(jnp.bfloat16)
        keys_local = joined[:, D : 2 * D].astype(jnp.bfloat16)
        values_local = (joined[:, 2 * D :] + bias_value).astype(jnp.bfloat16)
        normed, queries, keys_local, values_local = (
            normed,
            project_queries,
            keys_local,
            values_local,
        )
        keys_all, values_all = (
            lax.all_gather(keys_local, "seq", axis=0, tiled=True),
            lax.all_gather(values_local, "seq", axis=0, tiled=True),
        )
        finish_scores = score_rows(queries, keys_all, valid)
        row_max = jnp.max(finish_scores, axis=-1, keepdims=True)
        exponent = jnp.exp(finish_scores - row_max)
        total = jnp.sum(exponent, axis=-1, keepdims=True)
        finish_probs = exponent / total
        log_total = row_max + jnp.log(total)
        mixed = (
            jnp.einsum(
                "hqk,khd->qhd",
                finish_probs.astype(jnp.bfloat16),
                values_all.reshape(-1, H, DH),
                preferred_element_type=jnp.float32,
            )
            .reshape(rows, D)
            .astype(jnp.bfloat16)
        )
        hidden = (
            layer_in.astype(jnp.float32)
            + jnp.dot(mixed, w_proj, preferred_element_type=jnp.float32)
            + bias_proj
        )
        normed_two = layer_norm(hidden, gain_two, shift_two).astype(jnp.bfloat16)
        upper = jnp.dot(normed_two, w_upper, preferred_element_type=jnp.float32) + bias_upper
        gated = gelu_tanh(upper).astype(jnp.bfloat16)
        output = hidden + jnp.dot(gated, w_lower, preferred_element_type=jnp.float32) + bias_lower
        log_total, mixed, hidden, normed_two, upper, gated, output = (
            log_total,
            mixed,
            hidden,
            normed_two,
            upper,
            gated,
            output,
        )
        sent = output.astype(jnp.bfloat16)
        forward_outs.append(sent)
        saved.append(
            (
                layer_in,
                normed,
                queries,
                keys_local,
                values_local,
                log_total,
                mixed,
                hidden,
                normed_two,
                upper,
                gated,
            )
        )
        if tick < MICRO:
            received = passed_along(sent, "section", 1)
    stacked = tuple((jnp.stack(field) for field in zip(*saved)))
    incoming = zero_rows
    grads_back = []
    records = []
    small_terms = []
    shard_totals = None
    for tick in range(MICRO + 1):
        micro = tick - 1 + section
        valid = key_valid(counts_of(micro))
        live_flag = ((micro >= 0) & (micro < MICRO)).astype(jnp.bfloat16)
        forward_tick = jnp.clip(tick - 1 + 2 * section, 0, MICRO)
        kept = tuple(
            (lax.dynamic_index_in_dim(a, forward_tick, 0, keepdims=False) for a in stacked)
        )
        own_cot = cotangent[min(tick, MICRO - 1), 0]
        d_output = jnp.where(section == 1, own_cot, incoming) * live_flag
        (
            layer_in,
            normed,
            queries,
            keys_local,
            values_local,
            log_total,
            mixed,
            hidden,
            normed_two,
            upper,
            gated,
        ) = kept
        keys_all, values_all = (
            lax.all_gather(keys_local, "seq", axis=0, tiled=True),
            lax.all_gather(values_local, "seq", axis=0, tiled=True),
        )
        d_gated = jnp.einsum("td,fd->tf", d_output, w_lower, preferred_element_type=jnp.float32)
        unused_gelu, gelu_pull = jax.vjp(gelu_tanh, upper)
        d_upper = gelu_pull(d_gated)[0].astype(jnp.bfloat16)
        d_normed_two = jnp.einsum("tf,df->td", d_upper, w_upper, preferred_element_type=jnp.float32)
        unused_two, norm_two_pull = jax.vjp(layer_norm, hidden, gain_two, shift_two)
        d_hidden_norm, d_gain_two, d_shift_two = norm_two_pull(d_normed_two)
        d_hidden = d_output.astype(jnp.float32) + d_hidden_norm
        d_branch = d_hidden.astype(jnp.bfloat16)
        d_mixed = jnp.einsum(
            "te,de->td", d_branch, w_proj, preferred_element_type=jnp.float32
        ).astype(jnp.bfloat16)
        scores = score_rows(queries, keys_all, valid)
        probs = jnp.exp(scores - log_total)
        heads_grad = d_mixed.reshape(rows, H, DH)
        d_probs = jnp.einsum(
            "qhd,khd->hqk",
            heads_grad,
            values_all.reshape(-1, H, DH),
            preferred_element_type=jnp.float32,
        )
        row_term = jnp.sum(probs * d_probs, axis=-1, keepdims=True)
        d_scores = (probs * (d_probs - row_term)).astype(jnp.bfloat16)
        d_queries = (
            (
                jnp.einsum(
                    "hqk,khd->qhd",
                    d_scores,
                    keys_all.reshape(-1, H, DH),
                    preferred_element_type=jnp.float32,
                )
                * scale
            )
            .reshape(rows, D)
            .astype(jnp.bfloat16)
        )
        queries_heads = queries.reshape(rows, H, DH)
        probs_low = probs.astype(jnp.bfloat16)
        grad_keys = (
            jnp.einsum("hqk,qhd->khd", d_scores, queries_heads, preferred_element_type=jnp.float32)
            * scale
        )
        grad_values = jnp.einsum(
            "hqk,qhd->khd", probs_low, heads_grad, preferred_element_type=jnp.float32
        )
        key_sums = lax.psum_scatter(
            jnp.concatenate(
                [
                    grad_keys.reshape(rows * lax.axis_size("seq"), D),
                    grad_values.reshape(rows * lax.axis_size("seq"), D),
                ],
                axis=1,
            ).astype(jnp.bfloat16),
            "seq",
            scatter_dimension=0,
            tiled=True,
        ).astype(jnp.float32)
        d_keys = key_sums[:, :D].astype(jnp.bfloat16)
        d_values = key_sums[:, D:].astype(jnp.bfloat16)
        d_joint = jnp.concatenate([d_queries, d_keys, d_values], axis=1)
        d_normed = jnp.einsum("tc,dc->td", d_joint, w_joint, preferred_element_type=jnp.float32)
        unused_one, norm_one_pull = jax.vjp(
            layer_norm, layer_in.astype(jnp.float32), gain_one, shift_one
        )
        d_in_norm, d_gain_one, d_shift_one = norm_one_pull(d_normed)
        d_in = (d_hidden + d_in_norm).astype(jnp.bfloat16)
        grads_back.append(d_in)
        record = (normed, d_joint, mixed, d_branch, normed_two, d_upper, gated, d_output)
        small = (d_gain_one, d_shift_one, d_gain_two, d_shift_two)
        records.append(record)
        small_terms.append(small)
        if tick < MICRO:
            incoming = passed_along(d_in, "section", -1)
    all_sums = pack_grads(weight_grads_from(records, small_terms), groups)
    shard_totals = lax.psum_scatter(all_sums, ("dp", "seq"), scatter_dimension=0, tiled=True)
    grad_shards = unpack_grads(shard_totals, grad_shapes, groups)
    acts_rows = jnp.stack(
        [jnp.where(section == 0, forward_outs[m], forward_outs[m + 1]) for m in range(MICRO)]
    )
    grad_rows = jnp.stack(
        [jnp.where(section == 0, grads_back[m + 1], grads_back[m]) for m in range(MICRO)]
    )
    activations = acts_rows[None, :, None]
    input_grad = grad_rows[None, :, None]
    outs = tuple((g[None] for g in grad_shards))
    return (
        activations,
        input_grad,
        outs[0],
        outs[1],
        outs[2],
        outs[3],
        outs[4],
        outs[5],
        outs[6],
        outs[7],
        outs[8],
        outs[9],
        outs[10],
        outs[11],
        outs[12],
    )


def solution(mesh):
    placed = (
        P(None, "dp", "seq", None),
        P(None, "dp", "seq", None),
        P(None, "dp", None),
        P("section", None),
        P("section", None),
        P("section", None, None),
        P("section", None),
        P("section", None),
        P("section", None, None),
        P("section", None),
        P("section", None),
        P("section", None),
        P("section", None, None),
        P("section", None),
        P("section", None, None),
        P("section", None),
    )
    return jax.shard_map(
        shards,
        mesh=mesh,
        in_specs=placed,
        out_specs=(
            P("section", None, "dp", "seq", None),
            P("section", None, "dp", "seq", None),
            P("section", ("dp", "seq")),
            P("section", ("dp", "seq")),
            P("section", None, ("dp", "seq")),
            P("section", ("dp", "seq")),
            P("section", ("dp", "seq")),
            P("section", None, ("dp", "seq")),
            P("section", ("dp", "seq")),
            P("section", ("dp", "seq")),
            P("section", ("dp", "seq")),
            P("section", None, ("dp", "seq")),
            P("section", ("dp", "seq")),
            P("section", None, ("dp", "seq")),
            P("section", ("dp", "seq")),
        ),
        check_vma=False,
    )
```

profile of v0, /device:TPU:9, one launch (start us, length us, event | category | flops | bytes accessed | tf_op | source)
XLA Modules:
  0.0 2888.9 jit_solution(15197749061872489220)
XLA Ops:
  27.4 46.4 %all-gather.21.cloned.1.call-done = bf16[1280,1024]{1,0:T(8,128)(2,1)} async-done(((bf16[320,1024]{1,0:T(8,128)(2,1)}), bf16[1280,1024]{1,0:T(8,128)(2,1)}) %all-gather.21.cloned.1.call-update) | async-done | bytes 2621456 | tf_op jit(solution)/shard_map/all_gather | solution.py:197
  78.3 14.8 fusion
  102.8 26.9 all-gather.19.cloned.1.call-done
  172.2 49.2 %all-gather.25.cloned.1.call-done = bf16[1280,1024]{1,0:T(8,128)(2,1)} async-done(((bf16[320,1024]{1,0:T(8,128)(2,1)}), bf16[1280,1024]{1,0:T(8,128)(2,1)}) %all-gather.25.cloned.1.call-update) | async-done | bytes 2621456 | tf_op jit(solution)/shard_map/all_gather | solution.py:197
  226.2 14.6 fusion.1
  250.6 26.5 all-gather.23.cloned.1.call-done
  345.6 22.7 all-gather.29.cloned.1.call-done
  372.8 14.9 fusion.2
  397.5 26.4 all-gather.27.cloned.1.call-done
  500.6 33.7 %all-gather.31.cloned.1.call-done = bf16[1,1280,1024]{2,1,0:T(8,128)(2,1)} async-done(((bf16[1,320,1024]{2,1,0:T(8,128)(2,1)}), bf16[1,1280,1024]{2,1,0:T(8,128)(2,1)}) %all-gather.31.cloned.1.call-update) | async-done | bytes 2621456 | tf_op jit(solution)/shard_map/all_gather | solution.py:283
  538.7 18.4 multiply_reduce_fusion.2
  568.2 16.7 multiply_convert_fusion.2
  611.7 83.4 %reduce-scatter.10.cloned.1.call-done = bf16[320,2048]{1,0:T(8,128)(2,1)} async-done(((bf16[1280,2048]{1,0:T(8,128)(2,1)}), bf16[320,2048]{1,0:T(8,128)(2,1)}) %reduce-scatter.10.cloned.1.call-update) | async-done | bytes 1310736
  714.7 35.0 %all-gather.35.cloned.1.call-done = bf16[1,1280,1024]{2,1,0:T(8,128)(2,1)} async-done(((bf16[1,320,1024]{2,1,0:T(8,128)(2,1)}), bf16[1,1280,1024]{2,1,0:T(8,128)(2,1)}) %all-gather.35.cloned.1.call-update) | async-done | bytes 2621456 | tf_op jit(solution)/shard_map/all_gather | solution.py:283
  754.5 50.4 %all-gather.37.cloned.1.call-done = bf16[1,1280,1024]{2,1,0:T(8,128)(2,1)} async-done(((bf16[1,320,1024]{2,1,0:T(8,128)(2,1)}), bf16[1,1280,1024]{2,1,0:T(8,128)(2,1)}) %all-gather.37.cloned.1.call-update) | async-done | bytes 2621456 | tf_op jit(solution)/shard_map/all_gather | solution.py:284
  847.0 18.3 multiply_reduce_fusion.1
  876.4 16.7 multiply_convert_fusion.1
  920.7 83.8 %reduce-scatter.12.cloned.1.call-done = bf16[320,2048]{1,0:T(8,128)(2,1)} async-done(((bf16[1280,2048]{1,0:T(8,128)(2,1)}), bf16[320,2048]{1,0:T(8,128)(2,1)}) %reduce-scatter.12.cloned.1.call-update) | async-done | bytes 1310736
  1026.0 33.4 %all-gather.39.cloned.1.call-done = bf16[1,1280,1024]{2,1,0:T(8,128)(2,1)} async-done(((bf16[1,320,1024]{2,1,0:T(8,128)(2,1)}), bf16[1,1280,1024]{2,1,0:T(8,128)(2,1)}) %all-gather.39.cloned.1.call-update) | async-done | bytes 2621456 | tf_op jit(solution)/shard_map/all_gather | solution.py:283
  1063.7 50.6 %all-gather.41.cloned.1.call-done = bf16[1,1280,1024]{2,1,0:T(8,128)(2,1)} async-done(((bf16[1,320,1024]{2,1,0:T(8,128)(2,1)}), bf16[1,1280,1024]{2,1,0:T(8,128)(2,1)}) %all-gather.41.cloned.1.call-update) | async-done | bytes 2621456 | tf_op jit(solution)/shard_map/all_gather | solution.py:284
  1159.4 19.1 multiply_reduce_fusion
  1189.7 16.7 multiply_convert_fusion
  1267.4 15.4 fusion.144
  1314.3 23.3 copy.148
  1337.6 27.5 reshape.835
  1394.3 16.2 fusion.45
  1410.5 15.9 copy.145
  1426.4 19.4 reshape.825
  1469.9 46.9 %dynamic-update-slice.9 = f32[16,787200]{1,0:T(8,128)} dynamic-update-slice(f32[16,787200]{1,0:T(8,128)} %dynamic-update-slice.8, f32[16,262144]{1,0:T(8,128)} %bitcast.544, s32[]{} %constant.259, s32[]{} %constant.268) | dynamic-update-slice | bytes 33554436
  1518.3 46.4 %dynamic-update-slice.11 = f32[16,787200]{1,0:T(8,128)} dynamic-update-slice(f32[16,787200]{1,0:T(8,128)} %dynamic-update-slice.10, f32[16,262144]{1,0:T(8,128)} %reshape.835, s32[]{} %constant.259, s32[]{} %constant.270) | dynamic-update-slice | bytes 33554436
  1582.2 1255.1 %all-reduce.3.cloned.1.call-done = f32[16,787200]{1,0:T(8,128)} async-done(((f32[16,787200]{1,0:T(8,128)}), f32[16,787200]{1,0:T(8,128)}) %all-reduce.3.cloned.1.call-update) | async-done | bytes 50380816
  2855.8 16.2 dynamic-slice_reduce_fusion.3
  (656 shorter events, 671.4 us)
Async XLA Ops:
  7.2 139.4 %copy-start = (bf16[1,1024,1024]{2,1,0:T(8,128)(2,1)S(1)}, bf16[1,1024,1024]{2,1,0:T(8,128)(2,1)}, u32[]{:S(2)}) copy-start(bf16[1,1024,1024]{2,1,0:T(8,128)(2,1)} %param.24) | copy-start | bytes 6291460
  7.2 66.7 %all-gather.21.cloned.1.call-start = ((), (), s32[]{:S(2)}) async-start(), calls=%async_computation.4 | async-start | bytes 3276800 | tf_op jit(solution)/shard_map/all_gather | solution.py:197
  10.9 315.5 %copy-start.79 = (f32[1,1024]{1,0:T(1,128)}, f32[1,1024]{1,0:T(1,128)S(1)}, u32[]{:S(2)}) copy-start(f32[1,1024]{1,0:T(1,128)S(1)} %mul.861) | copy-start | bytes 12292
  19.8 109.8 %all-gather.19.cloned.1.call-start = ((), (), s32[]{:S(2)}) async-start(), calls=%async_computation.3 | async-start | bytes 3276800 | tf_op jit(solution)/shard_map/all_gather | solution.py:198
  22.8 55.5 %copy-start.43 = (bf16[320,1024]{1,0:T(8,128)(2,1)}, bf16[320,1024]{1,0:T(8,128)(2,1)S(1)}, u32[]{:S(2)}) copy-start(bf16[320,1024]{1,0:T(8,128)(2,1)S(1)} %get-tuple-element.146) | copy-start | bytes 1966084
  22.8 198.6 %all-gather.25.cloned.1.call-start = ((), (), s32[]{:S(2)}) async-start(), calls=%async_computation.6 | async-start | bytes 3276800 | tf_op jit(solution)/shard_map/all_gather | solution.py:197
  158.0 4.1 collective-permute-start
  168.1 109.0 %all-gather.23.cloned.1.call-start = ((), (), s32[]{:S(2)}) async-start(), calls=%async_computation.5 | async-start | bytes 3276800 | tf_op jit(solution)/shard_map/all_gather | solution.py:198
  171.0 55.2 %copy-start.44 = (bf16[320,1024]{1,0:T(8,128)(2,1)}, bf16[320,1024]{1,0:T(8,128)(2,1)S(1)}, u32[]{:S(2)}) copy-start(bf16[320,1024]{1,0:T(8,128)(2,1)S(1)} %get-tuple-element.144) | copy-start | bytes 1966084
  171.1 197.2 %all-gather.29.cloned.1.call-start = ((), (), s32[]{:S(2)}) async-start(), calls=%async_computation.8 | async-start | bytes 3276800 | tf_op jit(solution)/shard_map/all_gather | solution.py:197
  304.8 4.0 collective-permute-start.1
  314.9 109.0 %all-gather.27.cloned.1.call-start = ((), (), s32[]{:S(2)}) async-start(), calls=%async_computation.7 | async-start | bytes 3276800 | tf_op jit(solution)/shard_map/all_gather | solution.py:198
  318.1 163.2 %all-gather.33.cloned.1.call-start = ((), (), s32[]{:S(2)}) async-start(), calls=%async_computation.10 | async-start | bytes 3276800 | tf_op jit(solution)/shard_map/all_gather | solution.py:284
  321.3 212.9 %all-gather.31.cloned.1.call-start = ((), (), s32[]{:S(2)}) async-start(), calls=%async_computation.9 | async-start | bytes 3276800 | tf_op jit(solution)/shard_map/all_gather | solution.py:283
  342.5 352.5 %reduce-scatter.10.cloned.1.call-start = ((), (), s32[]{:S(2)}) async-start(), calls=%async_computation.15 | async-start | bytes 6553600
  600.3 149.4 %all-gather.35.cloned.1.call-start = ((), (), s32[]{:S(2)}) async-start(), calls=%async_computation.11 | async-start | bytes 3276800 | tf_op jit(solution)/shard_map/all_gather | solution.py:283
  600.8 204.0 %all-gather.37.cloned.1.call-start = ((), (), s32[]{:S(2)}) async-start(), calls=%async_computation.12 | async-start | bytes 3276800 | tf_op jit(solution)/shard_map/all_gather | solution.py:284
  601.6 402.9 %reduce-scatter.12.cloned.1.call-start = ((), (), s32[]{:S(2)}) async-start(), calls=%async_computation.16 | async-start | bytes 6553600
  611.7 86.0 %copy-start.80 = (f32[1,1024]{1,0:T(1,128)S(1)}, f32[1,1024]{1,0:T(1,128)}, u32[]{:S(2)}) copy-start(f32[1,1024]{1,0:T(1,128)} %copy-done.79) | copy-start | bytes 12292
  708.5 100.8 %collective-permute-start.2 = (bf16[320,1024]{1,0:T(8,128)(2,1)}, bf16[320,1024]{1,0:T(8,128)(2,1)}, u32[]{:S(2)}, u32[]{:S(2)}) collective-permute-start(bf16[320,1024]{1,0:T(8,128)(2,1)} %get-tuple-element.176), channel_id=1, source_target_pairs={{16,0},{17,1},{18,2},{19,3},{20,4},{21,5},{22,6},{23,7},{24,8},{25... | collective-permute-start | bytes 1966088 | tf_op jit(solution)/shard_map/ppermute | solution.py:22
  754.5 54.8 %copy-start.139 = (f32[320]{0:T(512)S(1)}, f32[320]{0:T(512)}, u32[]{:S(2)}) copy-start(f32[320]{0:T(512)} %get-tuple-element.215) | copy-start | bytes 3844
  754.5 54.8 %copy-start.140 = (f32[320]{0:T(512)S(1)}, f32[320]{0:T(512)}, u32[]{:S(2)}) copy-start(f32[320]{0:T(512)} %get-tuple-element.86) | copy-start | bytes 3844
  908.7 150.7 %all-gather.39.cloned.1.call-start = ((), (), s32[]{:S(2)}) async-start(), calls=%async_computation.13 | async-start | bytes 3276800 | tf_op jit(solution)/shard_map/all_gather | solution.py:283
  909.4 205.0 %all-gather.41.cloned.1.call-start = ((), (), s32[]{:S(2)}) async-start(), calls=%async_computation.14 | async-start | bytes 3276800 | tf_op jit(solution)/shard_map/all_gather | solution.py:284
  910.0 465.1 %reduce-scatter.14.cloned.1.call-start = ((), (), s32[]{:S(2)}) async-start(), calls=%async_computation.17 | async-start | bytes 6553600
  910.6 110.2 %slice-start.6 = ((s8[5242880]{0:T(1024)(128)(4,1)}), s8[1048576]{0:T(1024)(128)(4,1)S(1)}, s32[]{:S(2)}) async-start(s8[5242880]{0:T(1024)(128)(4,1)} %bitcast.567), calls=%async_computation.25 | async-start | bytes 2097152
  1018.6 100.2 %collective-permute-start.3 = (bf16[320,1024]{1,0:T(8,128)(2,1)}, bf16[320,1024]{1,0:T(8,128)(2,1)}, u32[]{:S(2)}, u32[]{:S(2)}) collective-permute-start(bf16[320,1024]{1,0:T(8,128)(2,1)} %get-tuple-element.120), channel_id=1, source_target_pairs={{16,0},{17,1},{18,2},{19,3},{20,4},{21,5},{22,6},{23,7},{24,8},{25... | collective-permute-start | bytes 1966088 | tf_op jit(solution)/shard_map/ppermute | solution.py:22
  1063.7 55.0 %copy-start.141 = (f32[320]{0:T(512)S(1)}, f32[320]{0:T(512)}, u32[]{:S(2)}) copy-start(f32[320]{0:T(512)} %get-tuple-element.85) | copy-start | bytes 3844
  1119.9 182.0 %copy-start.29 = (bf16[320,1024]{1,0:T(8,128)(2,1)}, bf16[320,1024]{1,0:T(8,128)(2,1)S(1)}, u32[]{:S(2)}) copy-start(bf16[320,1024]{1,0:T(8,128)(2,1)S(1)} %fusion.303) | copy-start | bytes 1966084
  1221.7 1615.6 %all-reduce.3.cloned.1.call-start = ((), (), s32[]{:S(2)}) async-start(), calls=%async_computation.18 | async-start | bytes 100761600
  1469.9 46.9 %copy-start.97 = (f32[16,256]{1,0:T(8,128)S(1)}, f32[16,256]{1,0:T(8,128)}, u32[]{:S(2)}) copy-start(f32[16,256]{1,0:T(8,128)} %reshape.833) | copy-start | bytes 49156
  1518.3 46.4 %copy-start.107 = (f32[16,64]{1,0:T(8,128)S(1)}, f32[16,64]{1,0:T(8,128)}, u32[]{:S(2)}) copy-start(f32[16,64]{1,0:T(8,128)} %reshape.836) | copy-start | bytes 12292
  (174 other events, 1277.6 us)
Sparse Core Ops, SparseCore 0:
  19.9 53.9 all-gather.20
  76.0 53.5 all-gather.18
  168.2 53.1 all-gather.24
  223.4 53.5 all-gather.22
  315.0 53.1 all-gather.28
  370.3 53.5 all-gather.26
  425.4 53.5 all-gather.32
  480.6 53.5 all-gather.30
  600.4 94.6 reduce-scatter.9
  696.4 53.2 all-gather.34
  751.3 53.5 all-gather.36
  908.8 95.6 reduce-scatter.11
  1006.1 53.2 all-gather.38
  1060.8 53.5 all-gather.40
  1221.8 94.8 reduce-scatter.13
  1566.2 1270.9 all-reduce.2
where the time goes:
time: 2900 us; the launch traced here: 2890 us
  waiting for transfers between devices  1830 us (63%)
  local copies, waits for them, and re-layouts  431 us (15%)
  matrix products  427 us (15%)
  other arithmetic  174 us (6%)
    unnamed x20, waiting for transfers between devices  1420 us
    all_gather x6, waiting for transfers between devices, shards(): lax.all_gather(keys_local, 'seq', axis=0, tiled=True)  220 us
    unnamed x395, local copies, waits for them, and re-layouts  194 us
    all_gather x6, waiting for transfers between devices, shards(): lax.all_gather(values_local, 'seq', axis=0, tiled=True)  181 us
    dot_general x6, matrix products, score_rows(): jnp.einsum('qhd,khd->hqk', queries.reshape(rows, H, DH), keys_all.reshape...  100 us
    reshape x4, local copies, waits for them, and re-layouts, pack_grads(): pieces.append(split.reshape(groups, -1))  61 us
  transfers between devices with their start and end apart: 20, of which 16 were waited for; matrix products, arithmetic and copies ran while one was open for 15% of the time, Pallas kernels for 0%

commit v1 on v0

v1 whole, which is shorter than its diff:
```python
import functools
import math

import jax
import jax.numpy as jnp
from jax import lax
from jax.experimental import pallas as pl
from jax.experimental.pallas import tpu as pltpu
from jax.sharding import PartitionSpec as P

D = 1024
H = 16
DH = 64
FF = 4096
VIEWS = 6
TRI = 512
VSLOT = 128
MICRO = 2
LEN = 1280
BQ = 256
NCH = 8
FC = FF // NCH
SCALE2 = DH ** (-0.5) * math.log2(math.e)
F32 = jnp.float32
BF16 = jnp.bfloat16
VMEM_LIMIT = 56 * 2**20


def params():
    return pltpu.CompilerParams(vmem_limit_bytes=VMEM_LIMIT)


def mm(a, b):
    return lax.dot_general(a, b, (((1,), (0,)), ((), ())), preferred_element_type=F32)


def mm_nt(a, b):
    return lax.dot_general(a, b, (((1,), (1,)), ((), ())), preferred_element_type=F32)


def mm_tn(a, b):
    return lax.dot_general(a, b, (((0,), (0,)), ((), ())), preferred_element_type=F32)


def norm_stats(values):
    average = jnp.mean(values, axis=-1, keepdims=True)
    centered = values - average
    variance = jnp.mean(centered * centered, axis=-1, keepdims=True)
    inverse = lax.rsqrt(variance + 1e-05)
    return centered * inverse, inverse


def qkv_kernel(x_ref, w_ref, bias_ref, gain_ref, shift_ref, a_ref, q_ref, k_ref, v_ref):
    width = q_ref.shape[1]
    normal, _ = norm_stats(x_ref[...].astype(F32))
    a = (normal * gain_ref[...] + shift_ref[...]).astype(BF16)
    a_ref[...] = a
    joined = mm(a, w_ref[...]) + bias_ref[...]
    q_ref[...] = joined[:, :width].astype(BF16)
    k_ref[...] = joined[:, width : 2 * width].astype(BF16)
    v_ref[...] = joined[:, 2 * width :].astype(BF16)


def qkv_call(x_all, weights, bias, gain, shift):
    length = x_all.shape[0]
    width = weights.shape[1] // 3
    row = lambda i: (i, 0)
    whole = lambda i: (0, 0)
    return pl.pallas_call(
        qkv_kernel,
        grid=(length // BQ,),
        in_specs=[
            pl.BlockSpec((BQ, D), row),
            pl.BlockSpec((D, 3 * width), whole),
            pl.BlockSpec((1, 3 * width), whole),
            pl.BlockSpec((1, D), whole),
            pl.BlockSpec((1, D), whole),
        ],
        out_specs=[pl.BlockSpec((BQ, D), row)] + [pl.BlockSpec((BQ, width), row)] * 3,
        out_shape=[jax.ShapeDtypeStruct((length, D), BF16)]
        + [jax.ShapeDtypeStruct((length, width), BF16)] * 3,
        compiler_params=params(),
        cost_estimate=pl.CostEstimate(
            flops=2 * length * D * 3 * width, bytes_accessed=8 * 2**20, transcendentals=0
        ),
    )(x_all, weights, bias, gain, shift)


def head_lanes(shape, head):
    lane = lax.broadcasted_iota(jnp.int32, shape, 1)
    return (lane >= head * DH) & (lane < (head + 1) * DH)


def attend_kernel(q_ref, k_ref, v_ref, mask_ref, o_ref, lse_ref):
    width = q_ref.shape[1]
    heads = width // DH
    q = q_ref[...]
    keys = k_ref[...]
    values = v_ref[...]
    mask = mask_ref[...]
    mixed = jnp.zeros((BQ, width), F32)
    totals = jnp.zeros((BQ, 128), F32)
    lane = lax.broadcasted_iota(jnp.int32, (BQ, 128), 1)
    for head in range(heads):
        mine = head_lanes((BQ, width), head)
        scores = mm_nt(jnp.where(mine, q, jnp.zeros_like(q)), keys) * SCALE2 + mask
        top = jnp.max(scores, axis=-1, keepdims=True)
        weights = jnp.exp2(scores - top)
        total = jnp.sum(weights, axis=-1, keepdims=True)
        part = mm(weights.astype(BF16), values) / total
        mixed = jnp.where(mine, part, mixed)
        totals = jnp.where(lane == head, top + jnp.log2(total), totals)
    o_ref[...] = mixed.astype(BF16)
    lse_ref[...] = totals


def attend_call(q, k, v, mask):
    length, width = q.shape
    row = lambda i: (i, 0)
    whole = lambda i: (0, 0)
    return pl.pallas_call(
        attend_kernel,
        grid=(length // BQ,),
        in_specs=[
            pl.BlockSpec((BQ, width), row),
            pl.BlockSpec((length, width), whole),
            pl.BlockSpec((length, width), whole),
            pl.BlockSpec((1, length), whole),
        ],
        out_specs=[pl.BlockSpec((BQ, width), row), pl.BlockSpec((BQ, 128), row)],
        out_shape=[
            jax.ShapeDtypeStruct((length, width), BF16),
            jax.ShapeDtypeStruct((length, 128), F32),
        ],
        compiler_params=params(),
        cost_estimate=pl.CostEstimate(
            flops=16 * length * length * width,
            bytes_accessed=4 * 2**20,
            transcendentals=length * length * width // DH,
        ),
    )(q, k, v, mask)


def attend_back_kernel(
    q_ref, do_ref, k_ref, v_ref, lse_ref, mask_ref, dj_ref, sums_ref, dk_acc, dv_acc
):
    step = pl.program_id(0)
    width = q_ref.shape[1]
    heads = width // DH
    scale = DH ** (-0.5)

    @pl.when(step == 0)
    def _():
        dk_acc[...] = jnp.zeros_like(dk_acc)
        dv_acc[...] = jnp.zeros_like(dv_acc)
        sums_ref[...] = jnp.zeros_like(sums_ref)

    q = q_ref[...]
    grad = do_ref[...]
    keys = k_ref[...]
    values = v_ref[...]
    mask = mask_ref[...]
    totals = lse_ref[...]
    d_q = jnp.zeros((BQ, width), F32)
    for head in range(heads):
        mine = head_lanes((BQ, width), head)
        q_head = jnp.where(mine, q, jnp.zeros_like(q))
        grad_head = jnp.where(mine, grad, jnp.zeros_like(grad))
        scores = mm_nt(q_head, keys) * SCALE2 + mask
        probs = jnp.exp2(scores - totals[:, head : head + 1])
        d_probs = mm_nt(grad_head, values)
        term = jnp.sum(probs * d_probs, axis=-1, keepdims=True)
        d_scores = (probs * (d_probs - term)).astype(BF16)
        dv_acc[...] += mm_tn(probs.astype(BF16), grad_head)
        dk_acc[...] += mm_tn(d_scores, q_head)
        d_q = jnp.where(mine, mm(d_scores, keys), d_q)
    low = (d_q * scale).astype(BF16)
    dj_ref[pl.ds(pl.multiple_of(step * BQ, BQ), BQ), :width] = low
    sums_ref[0:1, :] += jnp.sum(low.astype(F32), axis=0, keepdims=True)

    @pl.when(step == pl.num_programs(0) - 1)
    def _():
        dj_ref[:, width : 2 * width] = (dk_acc[...] * scale).astype(BF16)
        low_v = dv_acc[...].astype(BF16)
        dj_ref[:, 2 * width :] = low_v
        sums_ref[1:2, :] = jnp.sum(low_v.astype(F32), axis=0, keepdims=True)


def attend_back_call(q, d_o, k, v, lse, mask):
    length, width = q.shape
    row = lambda i: (i, 0)
    whole = lambda i: (0, 0)
    return pl.pallas_call(
        attend_back_kernel,
        grid=(length // BQ,),
        in_specs=[
            pl.BlockSpec((BQ, width), row),
            pl.BlockSpec((BQ, width), row),
            pl.BlockSpec((length, width), whole),
            pl.BlockSpec((length, width), whole),
            pl.BlockSpec((BQ, 128), row),
            pl.BlockSpec((1, length), whole),
        ],
        out_specs=[
            pl.BlockSpec((length, 3 * width), whole),
            pl.BlockSpec((8, width), whole),
        ],
        out_shape=[
            jax.ShapeDtypeStruct((length, 3 * width), BF16),
            jax.ShapeDtypeStruct((8, width), F32),
        ],
        scratch_shapes=[pltpu.VMEM((length, width), F32), pltpu.VMEM((length, width), F32)],
        compiler_params=params(),
        cost_estimate=pl.CostEstimate(
            flops=40 * length * length * width,
            bytes_accessed=6 * 2**20,
            transcendentals=length * length * width // DH,
        ),
    )(q, d_o, k, v, lse, mask)


GELU_A = math.sqrt(2.0 / math.pi)
GELU_B = 0.044715


def mlp_kernel(
    sel_ref,
    o_ref,
    x_ref,
    wo_ref,
    vec_ref,
    bup_ref,
    up0_ref,
    up1_ref,
    down0_ref,
    down1_ref,
    h_ref,
    a_ref,
    u_ref,
    g_ref,
    y_ref,
    acc,
):
    step = pl.program_id(0)
    groups, _, width = o_ref.shape

    @pl.when(step == 0)
    def _():
        hidden = x_ref[...].astype(F32) + vec_ref[0:1, :]
        for group in range(groups):
            hidden += mm(o_ref[group], wo_ref[group * width : (group + 1) * width, :])
        h_ref[...] = hidden
        normal, _ = norm_stats(hidden)
        a_ref[...] = (normal * vec_ref[1:2, :] + vec_ref[2:3, :]).astype(BF16)
        acc[...] = hidden + vec_ref[3:4, :]

    def part(up_ref, down_ref):
        upper = mm(a_ref[...], up_ref[...]) + bup_ref[...]
        u_ref[...] = upper
        inner = GELU_A * (upper + GELU_B * upper * upper * upper)
        gated = (0.5 * upper * (1.0 + jnp.tanh(inner))).astype(BF16)
        g_ref[...] = gated
        acc[...] += mm(gated, down_ref[...])

    pl.when(sel_ref[0] == 0)(lambda: part(up0_ref, down0_ref))
    pl.when(sel_ref[0] == 1)(lambda: part(up1_ref, down1_ref))

    @pl.when(step == pl.num_programs(0) - 1)
    def _():
        y_ref[...] = acc[...].astype(BF16)


def mlp_call(sel, o_all, x_own, wo, vecs, bup, ups, downs):
    rows = x_own.shape[0]
    groups, _, width = o_all.shape
    whole = lambda i, s: (0, 0)
    col = lambda which: (lambda i, s: (0, jnp.where(s[0] == which, i, 0)))
    line = lambda which: (lambda i, s: (jnp.where(s[0] == which, i, 0), 0))
    chunk = lambda i, s: (0, i)
    return pl.pallas_call(
        mlp_kernel,
        grid_spec=pltpu.PrefetchScalarGridSpec(
            num_scalar_prefetch=1,
            grid=(NCH,),
            in_specs=[
                pl.BlockSpec((groups, rows, width), lambda i, s: (0, 0, 0)),
                pl.BlockSpec((rows, D), whole),
                pl.BlockSpec((D, D), whole),
                pl.BlockSpec((8, D), whole),
                pl.BlockSpec((1, FC), chunk),
                pl.BlockSpec((D, FC), col(0)),
                pl.BlockSpec((D, FC), col(1)),
                pl.BlockSpec((FC, D), line(0)),
                pl.BlockSpec((FC, D), line(1)),
            ],
            out_specs=[
                pl.BlockSpec((rows, D), whole),
                pl.BlockSpec((rows, D), whole),
                pl.BlockSpec((rows, FC), chunk),
                pl.BlockSpec((rows, FC), chunk),
                pl.BlockSpec((rows, D), whole),
            ],
            scratch_shapes=[pltpu.VMEM((rows, D), F32)],
        ),
        out_shape=[
            jax.ShapeDtypeStruct((rows, D), F32),
            jax.ShapeDtypeStruct((rows, D), BF16),
            jax.ShapeDtypeStruct((rows, FF), F32),
            jax.ShapeDtypeStruct((rows, FF), BF16),
            jax.ShapeDtypeStruct((rows, D), BF16),
        ],
        compiler_params=params(),
        cost_estimate=pl.CostEstimate(
            flops=2 * rows * D * (D + 2 * FF), bytes_accessed=30 * 2**20, transcendentals=rows * FF
        ),
    )(sel, o_all, x_own, wo, vecs, bup, ups[0], ups[1], downs[0], downs[1])


def mlp_back_kernel(
    sel_ref,
    dy_ref,
    h_ref,
    wo_ref,
    vec_ref,
    u_ref,
    up0_ref,
    up1_ref,
    down0_ref,
    down1_ref,
    du_ref,
    gbup_ref,
    dh_ref,
    dr_ref,
    do_ref,
    sums_ref,
    acc,
):
    step = pl.program_id(0)
    groups, _, width = do_ref.shape

    @pl.when(step == 0)
    def _():
        acc[...] = jnp.zeros_like(acc)

    def part(up_ref, down_ref):
        d_gated = mm_nt(dy_ref[...], down_ref[...])
        upper = u_ref[...]
        square = upper * upper
        turn = jnp.tanh(GELU_A * upper * (1.0 + GELU_B * square))
        slope = 0.5 * (1.0 + turn) + (0.5 * GELU_A) * upper * (1.0 - turn * turn) * (
            1.0 + (3.0 * GELU_B) * square
        )
        d_upper = (d_gated * slope).astype(BF16)
        du_ref[...] = d_upper
        gbup_ref[...] = jnp.sum(d_upper.astype(F32), axis=0, keepdims=True)
        acc[...] += mm_nt(d_upper, up_ref[...])

    pl.when(sel_ref[0] == 0)(lambda: part(up0_ref, down0_ref))
    pl.when(sel_ref[0] == 1)(lambda: part(up1_ref, down1_ref))

    @pl.when(step == pl.num_programs(0) - 1)
    def _():
        normal, inverse = norm_stats(h_ref[...])
        d_out = dy_ref[...].astype(F32)
        d_normed = acc[...]
        sums_ref[...] = jnp.zeros_like(sums_ref)
        sums_ref[0:1, :] = jnp.sum(d_normed * normal, axis=0, keepdims=True)
        sums_ref[1:2, :] = jnp.sum(d_normed, axis=0, keepdims=True)
        d_normal = d_normed * vec_ref[1:2, :]
        d_hidden = d_out + inverse * (
            d_normal
            - jnp.mean(d_normal, axis=-1, keepdims=True)
            - normal * jnp.mean(d_normal * normal, axis=-1, keepdims=True)
        )
        dh_ref[...] = d_hidden
        d_branch = d_hidden.astype(BF16)
        dr_ref[...] = d_branch
        sums_ref[2:3, :] = jnp.sum(d_branch.astype(F32), axis=0, keepdims=True)
        sums_ref[3:4, :] = jnp.sum(d_out, axis=0, keepdims=True)
        for group in range(groups):
            do_ref[group] = mm_nt(
                d_branch, wo_ref[group * width : (group + 1) * width, :]
            ).astype(BF16)


def mlp_back_call(sel, dy, hidden, wo, vecs, upper, ups, downs, groups):
    rows = dy.shape[0]
    width = D // groups
    whole = lambda i, s: (0, 0)
    col = lambda which: (lambda i, s: (0, jnp.where(s[0] == which, i, 0)))
    line = lambda which: (lambda i, s: (jnp.where(s[0] == which, i, 0), 0))
    chunk = lambda i, s: (0, i)
    return pl.pallas_call(
        mlp_back_kernel,
        grid_spec=pltpu.PrefetchScalarGridSpec(
            num_scalar_prefetch=1,
            grid=(NCH,),
            in_specs=[
                pl.BlockSpec((rows, D), whole),
                pl.BlockSpec((rows, D), whole),
                pl.BlockSpec((D, D), whole),
                pl.BlockSpec((8, D), whole),
                pl.BlockSpec((rows, FC), chunk),
                pl.BlockSpec((D, FC), col(0)),
                pl.BlockSpec((D, FC), col(1)),
                pl.BlockSpec((FC, D), line(0)),
                pl.BlockSpec((FC, D), line(1)),
            ],
            out_specs=[
                pl.BlockSpec((rows, FC), chunk),
                pl.BlockSpec((1, FC), chunk),
                pl.BlockSpec((rows, D), whole),
                pl.BlockSpec((rows, D), whole),
                pl.BlockSpec((groups, rows, width), lambda i, s: (0, 0, 0)),
                pl.BlockSpec((8, D), whole),
            ],
            scratch_shapes=[pltpu.VMEM((rows, D), F32)],
        ),
        out_shape=[
            jax.ShapeDtypeStruct((rows, FF), BF16),
            jax.ShapeDtypeStruct((1, FF), F32),
            jax.ShapeDtypeStruct((rows, D), F32),
            jax.ShapeDtypeStruct((rows, D), BF16),
            jax.ShapeDtypeStruct((groups, rows, width), BF16),
            jax.ShapeDtypeStruct((8, D), F32),
        ],
        compiler_params=params(),
        cost_estimate=pl.CostEstimate(
            flops=2 * rows * D * (D + 2 * FF), bytes_accessed=30 * 2**20, transcendentals=rows * FF
        ),
    )(sel, dy, hidden, wo, vecs, upper, ups[0], ups[1], downs[0], downs[1])


def norm_back_kernel(mine_ref, other_ref, x_ref, dh_ref, gain_ref, dx_ref, sums_ref):
    d_normed = mine_ref[...].astype(F32) + other_ref[...].astype(F32)
    normal, inverse = norm_stats(x_ref[...].astype(F32))
    sums_ref[...] = jnp.zeros_like(sums_ref)
    sums_ref[0:1, :] = jnp.sum(d_normed * normal, axis=0, keepdims=True)
    sums_ref[1:2, :] = jnp.sum(d_normed, axis=0, keepdims=True)
    d_normal = d_normed * gain_ref[...]
    dx_ref[...] = (
        dh_ref[...]
        + inverse
        * (
            d_normal
            - jnp.mean(d_normal, axis=-1, keepdims=True)
            - normal * jnp.mean(d_normal * normal, axis=-1, keepdims=True)
        )
    ).astype(BF16)


def norm_back_call(mine, other, x_own, d_hidden, gain):
    return pl.pallas_call(
        norm_back_kernel,
        out_shape=[
            jax.ShapeDtypeStruct(x_own.shape, BF16),
            jax.ShapeDtypeStruct((8, D), F32),
        ],
        compiler_params=params(),
        cost_estimate=pl.CostEstimate(
            flops=20 * x_own.size, bytes_accessed=10 * x_own.size, transcendentals=0
        ),
    )(mine, other, x_own, d_hidden, gain)


def swap(value, axis, mask):
    count = lax.axis_size(axis)
    return lax.ppermute(value, axis, [(i, i ^ mask) for i in range(count)])


def take(value, index, dim):
    return lax.dynamic_index_in_dim(value, index, dim, keepdims=False)


def ordered(bit, mine, other, dim):
    return jnp.where(
        bit == 0,
        jnp.stack([mine, other], axis=dim),
        jnp.stack([other, mine], axis=dim),
    )


def key_bias(counts, rotate):
    places = jnp.arange(LEN, dtype=jnp.int32)
    places = jnp.where(rotate, (places + LEN // 2) % LEN, places)
    offset = jnp.maximum(places - TRI, 0)
    view_index = offset // VSLOT
    inside = offset - view_index * VSLOT
    match = view_index[:, None] == jnp.arange(VIEWS, dtype=jnp.int32)[None, :]
    limits = jnp.sum(jnp.where(match, counts[None, :], 0), axis=1)
    valid = (places < TRI) | (inside < limits)
    return jnp.where(valid, 0.0, -1e30).astype(F32)[None, :]


def shards(
    inputs,
    cotangent,
    view_tokens,
    ln1_gain,
    ln1_bias,
    w_qkv,
    b_query,
    b_value,
    w_out,
    b_out,
    ln2_gain,
    ln2_bias,
    w_up,
    b_up,
    w_down,
    b_down,
):
    core = lax.axis_index("section")
    place = lax.axis_index("seq")
    dp_index = lax.axis_index("dp")
    count = lax.axis_size("seq")
    dp_count = lax.axis_size("dp")
    groups = dp_count * count
    half = count // 2
    micro = place // half
    low = place % half
    low_bits = half.bit_length() - 1
    rows = inputs.shape[2]
    width = D // count
    rank = core * half + low

    def swap_core(value):
        return swap(value, "section", 1)

    def swap_seq(value, bit):
        return swap(value, "seq", 1 << bit)

    def low_bit(bit):
        return (place >> bit) & 1

    def own_rows(local):
        chunks = local[:, 0]
        far = lax.ppermute(
            take(chunks, 1 - micro, 0),
            ("section", "seq"),
            [(count + z, count + (z ^ half)) for z in range(count)],
        )
        return jnp.where(core == 0, take(chunks, micro, 0), far)

    def gather_rows(own):
        value = own[None]
        for bit in range(low_bits):
            other = swap_seq(value, bit)
            value = ordered(low_bit(bit), value, other, 0).reshape((-1,) + own.shape)
        value = ordered(core, value, swap_core(value), 0)
        return value.reshape((-1,) + own.shape[1:])

    def exchange(value):
        tail = value.shape[1:]
        value = value.reshape((2,) * (low_bits + 1) + tail)
        for bit in range(low_bits):
            dim = low_bits - bit
            mine = take(value, low_bit(bit), dim)
            other = swap_seq(take(value, 1 - low_bit(bit), dim), bit)
            value = ordered(low_bit(bit), mine, other, dim)
        mine = take(value, core, 0)
        other = swap_core(take(value, 1 - core, 0))
        return ordered(core, mine, other, 0).reshape((count,) + tail)

    def to_section(own, layer):
        first = own
        if layer == 1:
            first = lax.ppermute(
                own, ("section", "seq"), [(z, count + z) for z in range(count)]
            )
        second = lax.ppermute(
            own,
            ("section", "seq"),
            [(count + z, layer * count + (z ^ half)) for z in range(count)],
        )
        return ordered(micro, first, second, 0)

    def both_vectors(value):
        return jnp.stack([value, value])

    vectors = jnp.concatenate(
        [v[0].astype(F32) for v in (ln1_gain, ln1_bias, b_query, b_value, b_out, ln2_gain, ln2_bias, b_down, b_up)]
    )
    vector_pair = ordered(core, vectors, swap_core(vectors), 0)

    def vector(layer, index):
        size = FF if index == 8 else D
        return vector_pair[layer, index * D : index * D + size]

    joint = w_qkv[0].reshape(D, 3, count, width)
    joint_mine = take(joint, rank, 2).reshape(D, 3 * width)
    joint_other = swap_core(take(joint, (1 - core) * half + low, 2).reshape(D, 3 * width))
    out_other = swap_core(w_out[0])
    up_other = swap_core(w_up[0])
    down_other = swap_core(w_down[0])
    ups = (w_up[0], up_other)
    downs = (w_down[0], down_other)

    bias_mask = key_bias(take(view_tokens[:, 0], micro, 0), micro == 1)

    saved = []
    layer_in = own_rows(inputs)
    acts = []
    for layer in range(2):
        sel = jnp.where(core == layer, 0, 1).astype(jnp.int32)[None]
        w_joint = jnp.where(core == layer, joint_mine, joint_other)
        w_proj = jnp.where(core == layer, w_out[0], out_other)
        zero = jnp.zeros((width,), F32)
        slice_of = lambda v: lax.dynamic_slice_in_dim(v, rank * width, width)
        bias = jnp.concatenate([slice_of(vector(layer, 2)), zero, slice_of(vector(layer, 3))])
        vecs = jnp.concatenate(
            [
                jnp.stack([vector(layer, 4), vector(layer, 5), vector(layer, 6), vector(layer, 7)]),
                jnp.zeros((4, D), F32),
            ]
        )
        x_all = gather_rows(layer_in)
        a1, q, k, v = qkv_call(
            x_all, w_joint, bias[None], vector(layer, 0)[None], vector(layer, 1)[None]
        )
        mixed, lse = attend_call(q, k, v, bias_mask)
        o_own = exchange(mixed.reshape(count, rows, width))
        hidden, a2, upper, gated, output = mlp_call(
            sel, o_own, layer_in, w_proj, vecs, vector(layer, 8)[None], ups, downs
        )
        acts.append(output)
        saved.append(
            (sel, w_joint, w_proj, vecs, layer_in, a1, q, k, v, lse, o_own, hidden, a2, upper, gated)
        )
        layer_in = output

    dp_bits = dp_count.bit_length() - 1
    seq_bits = count.bit_length() - 1
    bits = [("dp", dp_bits - 1 - i) for i in range(dp_bits)]
    bits += [("seq", seq_bits - 1 - i) for i in range(seq_bits)]
    dp_dims = list(range(dp_bits))
    seq_dims = list(range(dp_bits, dp_bits + seq_bits))[::-1]
    orders = (
        dp_dims[::-1] + seq_dims,
        dp_dims + seq_dims,
        seq_dims[:1] + dp_dims + seq_dims[1:],
        seq_dims[:1] + dp_dims[::-1] + seq_dims[1:],
    )

    def reduce_one(value, order):
        tail = value.shape[1:]
        value = value.reshape((2,) * len(bits) + tail)
        left = list(range(len(bits)))
        for dim in order:
            axis, bit = bits[dim]
            index = (lax.axis_index(axis) >> bit) & 1
            at = left.index(dim)
            left.remove(dim)
            other = swap(take(value, 1 - index, at), axis, 1 << bit)
            total = take(value, index, at).astype(F32) + other.astype(F32)
            value = total.astype(value.dtype) if left else total
        return value

    def reduce_parts(value, cuts):
        outs = []
        start = 0
        for order, size in zip(orders, cuts):
            if size:
                outs.append(reduce_one(value[..., start : start + size], order))
            start += size
        return jnp.concatenate(outs, axis=-1)

    def halves(value):
        split = value.reshape(rows, groups, 2, FF // groups // 2)
        mine = take(split, core, 2).reshape(rows, FF // 2)
        return mine, take(split, 1 - core, 2).reshape(rows, FF // 2)

    def joined(mine, other):
        return jnp.concatenate([mine, other], axis=0)

    def give(value, layer):
        return lax.ppermute(value, "section", [(1 - layer, layer)])

    smalls = []
    results = []
    grads_in = []
    d_out = own_rows(cotangent)
    for layer in (1, 0):
        sel, w_joint, w_proj, vecs, x_own, a1, q, k, v, lse, o_own, hidden, a2, upper, gated = saved[layer]
        gated_mine, gated_send = halves(gated)
        gated_all = joined(gated_mine, swap_core(gated_send))
        a2_all = joined(a2, swap_core(a2))
        d_out_all = joined(d_out, swap_core(d_out))
        g_down = mm_tn(d_out_all, gated_all).astype(BF16).reshape(groups, D // groups, FF // 2)
        r_down = reduce_parts(g_down, (640, 640, 384, 384))
        d_upper, g_bup, d_hidden, d_branch, d_heads, sums_two = mlp_back_call(
            sel, d_out, hidden, w_proj, vecs, upper, ups, downs, count
        )
        upper_mine, upper_send = halves(d_upper)
        upper_all = joined(upper_mine, swap_core(upper_send))
        g_up = mm_tn(upper_all, a2_all).astype(BF16).reshape(groups, FF // groups // 2, D)
        r_up = reduce_parts(g_up, (384, 384, 128, 128))
        d_mixed = exchange(d_heads).reshape(LEN, width)
        o_split = o_own.reshape(2, half, rows, width)
        flat = lambda t: jnp.swapaxes(t, 0, 1).reshape(rows, half * width)
        o_all = joined(flat(take(o_split, core, 0)), swap_core(flat(take(o_split, 1 - core, 0))))
        branch_all = joined(d_branch, swap_core(d_branch))
        g_out = mm_tn(branch_all, o_all).astype(BF16).reshape(groups, D // groups, D // 2)
        r_out = reduce_parts(g_out, (128, 128, 128, 128))
        d_joint, sums_qv = attend_back_call(q, d_mixed, k, v, lse, bias_mask)
        d_normed = mm_nt(d_joint, w_joint).astype(BF16).reshape((2,) * (low_bits + 1) + (rows, D))
        other = swap_core(take(d_normed, 1 - core, 0))
        mine = take(d_normed, core, 0)
        for bit in range(low_bits):
            total = (mine.astype(F32) + other.astype(F32)).astype(BF16)
            dim = low_bits - 1 - bit
            other = swap_seq(take(total, 1 - low_bit(bit), dim), bit)
            mine = take(total, low_bit(bit), dim)
        d_in, sums_one = norm_back_call(mine, other, x_own, d_hidden, vector(layer, 0)[None])
        g_joint = mm_tn(d_joint, a1).astype(BF16).reshape(3, width, 2, D // 2)
        g_joint = ordered(core, take(g_joint, core, 2), swap_core(take(g_joint, 1 - core, 2)), 1)
        spread = jnp.stack(
            [jnp.where(low == i, g_joint, jnp.zeros_like(g_joint)) for i in range(half)], axis=2
        )
        r_joint = reduce_parts(spread.reshape(groups, 3 * D // groups, D // 2), (128, 128, 128, 128))
        mine_at = jnp.zeros((2, count, width), F32)
        mine_at = lax.dynamic_update_slice(mine_at, sums_qv[0:2, None, :], (0, rank, 0))
        smalls.append(
            jnp.concatenate(
                [
                    piece.reshape(groups, -1)
                    for piece in (
                        sums_one[0],
                        sums_one[1],
                        mine_at[0].reshape(-1),
                        mine_at[1].reshape(-1),
                        sums_two[2],
                        sums_two[0],
                        sums_two[1],
                        g_bup[0],
                        sums_two[3],
                    )
                ],
                axis=1,
            )
        )
        parts = []
        for piece in (r_down, r_out, r_joint, r_up):
            parts.append((piece, give(piece, layer)))
        results.append(parts)
        grads_in.append(d_in)
        d_out = d_in

    results = results[::-1]
    grads_in = grads_in[::-1]
    small_pair = jnp.stack(smalls[::-1])
    small = take(small_pair, core, 0) + swap_core(take(small_pair, 1 - core, 0))
    small = reduce_one(small, orders[0])

    acts_rows = jnp.where(core == 0, to_section(acts[0], 0), to_section(acts[1], 1))
    grad_rows = jnp.where(core == 0, to_section(grads_in[0], 0), to_section(grads_in[1], 1))

    def choose(index):
        first = jnp.where(core == 0, results[0][index][0], results[1][index][1])
        second = jnp.where(core == 0, results[0][index][1], results[1][index][0])
        return first, second

    down_0, down_1 = choose(0)
    d_down = jnp.stack([down_0.reshape(-1, groups, FF // groups // 2), down_1.reshape(-1, groups, FF // groups // 2)], axis=2)
    g_w_down = d_down.reshape(-1, FF).T
    out_0, out_1 = choose(1)
    g_w_out = jnp.concatenate([out_0, out_1], axis=1).T
    joint_0, joint_1 = choose(2)
    g_w_qkv = jnp.concatenate([joint_0, joint_1], axis=1).T
    up_0, up_1 = choose(3)
    g_w_up = jnp.concatenate([up_0, up_1], axis=0).T

    unit = D // groups
    pieces = []
    start = 0
    for size in (unit, unit, unit, unit, unit, unit, unit, FF // groups, unit):
        pieces.append(small[start : start + size])
        start += size
    g_ln1g, g_ln1b, g_bq, g_bv, g_bo, g_ln2g, g_ln2b, g_bup, g_bd = pieces
    outs = (
        g_ln1g,
        g_ln1b,
        g_w_qkv,
        g_bq,
        g_bv,
        g_w_out,
        g_bo,
        g_ln2g,
        g_ln2b,
        g_w_up,
        g_bup,
        g_w_down,
        g_bd,
    )
    return (acts_rows[None, :, None], grad_rows[None, :, None]) + tuple(g[None] for g in outs)


def solution(mesh):
    rows = P(None, "dp", "seq", None)
    vector = P("section", None)
    matrix = P("section", None, None)
    placed = (
        rows,
        rows,
        P(None, "dp", None),
        vector,
        vector,
        matrix,
        vector,
        vector,
        matrix,
        vector,
        vector,
        vector,
        matrix,
        vector,
        matrix,
        vector,
    )
    both = P("section", None, "dp", "seq", None)
    line = P("section", ("dp", "seq"))
    table = P("section", None, ("dp", "seq"))
    return jax.shard_map(
        shards,
        mesh=mesh,
        in_specs=placed,
        out_specs=(
            both,
            both,
            line,
            line,
            table,
            line,
            line,
            table,
            line,
            line,
            line,
            table,
            line,
            table,
            line,
        ),
        check_vma=False,
    )
```

time: 2900 us -> 1220 us (0.42)
  waiting for transfers between devices: 1830 us -> 399 us
  matrix products: 427 us -> 39.9 us
  starting transfers between devices: 9.07 us -> 321 us
  local copies, waits for them, and re-layouts: 431 us -> 191 us
  Pallas kernels: 0 us -> 183 us
  other arithmetic: 174 us -> 73.4 us
    unnamed x20 -> x0, waiting for transfers between devices: 1420 us -> none
    all_gather x12 -> x0, waiting for transfers between devices: 401 us -> none  [the longest x6 220 us: shards(): lax.all_gather(keys_local, 'seq', axis=0, tiled=True)]
    ppermute x4 -> x184, waiting for transfers between devices: 5.39 us -> 399 us  [the longest x168 397 us: swap(): return lax.ppermute(value, axis, [(i, i ^ mask) for i in range(count)])]
    dot_general x49 -> x10, matrix products: 427 us -> 39.9 us  [the longest x8 32.2 us: mm_tn(): lax.dot_general(a, b, (((0,), (0,)), ((), ())), preferred_element_type=F32)]
    ppermute x4 -> x184, starting transfers between devices: 8.25 us -> 321 us  [the longest x168 243 us: swap(): return lax.ppermute(value, axis, [(i, i ^ mask) for i in range(count)])]
    pallas_call x0 -> x12, Pallas kernels: none -> 183 us  [the longest x2 56.4 us: attend_back_call(): pl.pallas_call(attend_back_kernel, grid=(length // BQ,), in_specs=[pl.Blo...]
    unnamed x395 -> x245, local copies, waits for them, and re-layouts: 194 us -> 35 us
    dynamic_slice x6 -> x63, local copies, waits for them, and re-layouts: 10.7 us -> 87 us  [the longest x61 87 us: take(): return lax.dynamic_index_in_dim(value, index, dim, keepdims=False)]
  transfers between devices with their start and end apart: 20 -> 184, of which waited for: 16 -> 121; matrix products, arithmetic and copies ran while one was open for 15% -> 24% of each run, Pallas kernels for 0% -> 14%
where the time goes in v1:
time: 1220 us; the launch traced here: 1210 us
  waiting for transfers between devices  399 us (33%)
  starting transfers between devices  321 us (26%)
  local copies, waits for them, and re-layouts  191 us (16%)
  Pallas kernels  183 us (15%)
  other arithmetic  73.4 us (6%)
  matrix products  39.9 us (3%)
    ppermute x168, waiting for transfers between devices, swap(): return lax.ppermute(value, axis, [(i, i ^ mask) for i in range(count)])  397 us
    ppermute x168, starting transfers between devices, swap(): return lax.ppermute(value, axis, [(i, i ^ mask) for i in range(count)])  243 us
    dynamic_slice x61, local copies, waits for them, and re-layouts, take(): return lax.dynamic_index_in_dim(value, index, dim, keepdims=False)  87 us
    pallas_call x2, Pallas kernels, attend_back_call(): pl.pallas_call(attend_back_kernel, grid=(length // BQ,), in_specs=[pl.Blo...  56.4 us
    ppermute x8, starting transfers between devices, give(): return lax.ppermute(value, 'section', [(1 - layer, layer)])  49.1 us
    pallas_call x2, Pallas kernels, mlp_back_call(): pl.pallas_call(mlp_back_kernel, grid_spec=pltpu.PrefetchScalarGridSpec(nu...  39 us
    pallas_call x2, Pallas kernels, mlp_call(): pl.pallas_call(mlp_kernel, grid_spec=pltpu.PrefetchScalarGridSpec(num_sca...  36.6 us
    unnamed x245, local copies, waits for them, and re-layouts  35 us
  transfers between devices with their start and end apart: 184, of which 121 were waited for; matrix products, arithmetic and copies ran while one was open for 24% of the time, Pallas kernels for 14%

profile of v1, /device:TPU:9, one launch (start us, length us, event | category | flops | bytes accessed | tf_op | source)
XLA Modules:
  0.0 1211.8 jit_solution(17931225046587240005)
XLA Ops:
  1.5 8.6 copy.177
  40.0 8.7 collective-permute-done.1
  56.4 7.2 shard_map.271
  63.6 14.3 %shard_map.272 = (bf16[1280,256]{1,0:T(8,128)(2,1)}, f32[1280,128]{1,0:T(8,128)}) custom-call(bf16[1280,256]{1,0:T(8,128)(2,1)} %get-tuple-element.57.q_ref, bf16[1280,256]{1,0:T(8,128)(2,1)} %get-tuple-element.58.k_ref, bf16[1280,256]{1,0:T(8,128)(2,1)} %get-tuple-element.59.v_ref, f32[1,1280]{1,0:T(1,128)} %or_select_fusion.mask_ref), custom_call_target="tpu_custom_call" | custom-call | flops 6710886400 | bytes 4194304 | tf_op jit(solution)/shard_map/pallas_call | solution.py:121
  94.2 17.8 %shard_map.273 = (f32[320,1024]{1,0:T(8,128)}, bf16[320,1024]{1,0:T(8,128)(2,1)}, f32[320,4096]{1,0:T(8,128)}, bf16[320,4096]{1,0:T(8,128)(2,1)}, bf16[320,1024]{1,0:T(8,128)(2,1)}) custom-call(s32[1]{0:T(128)} %bitcast.sel_ref, bf16[4,320,256]{2,1,0:T(8,128)(2,1)} %bitcast.1105, bf16[320,1024]{1,0:T(8,128)(2,1)} %copy-done.2, ...), custom_call_target="tpu_custom_call" | custom-call | flops 6039797760 | bytes 31457280 | tf_op jit(solution)/shard_map/pallas_call | solution.py:280
  113.6 14.4 %collective-permute-done.11 = bf16[1,320,1024]{2,1,0:T(8,128)(2,1)S(1)} collective-permute-done((bf16[1,320,1024]{2,1,0:T(8,128)(2,1)}, bf16[1,320,1024]{2,1,0:T(8,128)(2,1)S(1)}, u32[]{:S(2)}, u32[]{:S(2)}) %collective-permute-start.11) | collective-permute-done | bytes 655392 | tf_op jit(solution)/shard_map/ppermute | solution.py:468
  143.5 7.2 shard_map.274
  150.7 14.3 %shard_map.275 = (bf16[1280,256]{1,0:T(8,128)(2,1)}, f32[1280,128]{1,0:T(8,128)}) custom-call(bf16[1280,256]{1,0:T(8,128)(2,1)} %get-tuple-element.62.q_ref, bf16[1280,256]{1,0:T(8,128)(2,1)} %get-tuple-element.63.k_ref, bf16[1280,256]{1,0:T(8,128)(2,1)} %get-tuple-element.64.v_ref, f32[1,1280]{1,0:T(1,128)} %or_select_fusion.mask_ref), custom_call_target="tpu_custom_call" | custom-call | flops 6710886400 | bytes 4194304 | tf_op jit(solution)/shard_map/pallas_call | solution.py:121
  176.7 15.8 %dynamic-slice_reduce_fusion.3 = (bf16[320,16,128]{2,1,0:T(8,128)(2,1)S(1)}, bf16[320,16,128]{2,1,0:T(8,128)(2,1)S(1)}) fusion(bf16[320,16,2,128]{3,2,1,0:T(2,128)(2,1)S(1)} %reshape.1312, s32[]{:T(128)S(6)} %select_n.891, s32[]{:T(128)S(6)} %select_n.892), kind=kLoop, calls=%fused_computation.29 | loop fusion | bytes 5242888 | tf_op jit(solution)/shard_map/jit(dynamic_index_in_dim)/dynamic_slice | solution.py:472
  196.2 18.9 %shard_map.276 = (f32[320,1024]{1,0:T(8,128)}, bf16[320,1024]{1,0:T(8,128)(2,1)}, f32[320,4096]{1,0:T(8,128)}, bf16[320,4096]{1,0:T(8,128)(2,1)}, bf16[320,1024]{1,0:T(8,128)(2,1)}) custom-call(s32[1]{0:T(128)} %bitcast.27.sel_ref, bf16[4,320,256]{2,1,0:T(8,128)(2,1)} %bitcast.1106, bf16[320,1024]{1,0:T(8,128)(2,1)} %get-tuple-element.61.x_ref, ...), custom_call_target="tpu_custom_call" | custom-call | flops 6039797760 | bytes 31457280 | tf_op jit(solution)/shard_map/pallas_call | solution.py:280
  215.1 19.8 %shard_map.277 = (bf16[320,4096]{1,0:T(8,128)(2,1)}, f32[1,4096]{1,0:T(1,128)}, f32[320,1024]{1,0:T(8,128)}, bf16[320,1024]{1,0:T(8,128)(2,1)}, bf16[4,320,256]{2,1,0:T(8,128)(2,1)}, /*index=5*/f32[8,1024]{1,0:T(8,128)}) custom-call(s32[1]{0:T(128)} %bitcast.27.sel_ref, bf16[320,1024]{1,0:T(8,128)(2,1)} %bitcast_select_fusion.dy_ref, ...), custom_call_target="tpu_custom_call" | custom-call | flops 6039797760 | bytes 31457280 | tf_op jit(solution)/shard_map/pallas_call | solution.py:393
  242.5 17.1 %dynamic-slice_reduce_fusion.1 = (bf16[320,16,128]{2,1,0:T(8,128)(2,1)}, bf16[320,16,128]{2,1,0:T(8,128)(2,1)}) fusion(bf16[320,16,2,128]{3,2,1,0:T(2,128)(2,1)S(1)} %reshape.1320, s32[]{:T(128)S(6)} %select_n.891, s32[]{:T(128)S(6)} %select_n.892), kind=kLoop, calls=%fused_computation.27 | loop fusion | bytes 5242888 | tf_op jit(solution)/shard_map/jit(dynamic_index_in_dim)/dynamic_slice | solution.py:472
  264.0 16.0 %dynamic-slice_reduce_fusion.5 = (bf16[320,16,128]{2,1,0:T(8,128)(2,1)S(1)}, bf16[320,16,128]{2,1,0:T(8,128)(2,1)S(1)}) fusion(bf16[320,16,2,128]{3,2,1,0:T(2,128)(2,1)S(1)} %reshape.1304, s32[]{:T(128)S(6)} %select_n.891, s32[]{:T(128)S(6)} %select_n.892), kind=kLoop, calls=%fused_computation.31 | loop fusion | bytes 5242888 | tf_op jit(solution)/shard_map/jit(dynamic_index_in_dim)/dynamic_slice | solution.py:472
  306.2 28.0 %shard_map.278 = (bf16[1280,768]{1,0:T(8,128)(2,1)}, f32[8,256]{1,0:T(8,128)}) custom-call(bf16[1280,256]{1,0:T(8,128)(2,1)} %get-tuple-element.62.q_ref, bf16[1280,256]{1,0:T(8,128)(2,1)} %bitcast.1199, bf16[1280,256]{1,0:T(8,128)(2,1)} %get-tuple-element.63.k_ref, bf16[1280,256]{1,0:T(8,128)(2,1)} %get-tuple-element.64.v_ref, ...), custom_call_target="tpu_custom_call" | custom-call | flops 16777216000 | bytes 6291456 | tf_op jit(solution)/shard_map/pallas_call | solution.py:193
  411.7 16.8 %collective-permute-start.126 = (bf16[320,2048]{1,0:T(8,128)(2,1)S(1)}, bf16[320,2048]{1,0:T(8,128)(2,1)S(1)}, u32[]{:S(2)}, u32[]{:S(2)}) collective-permute-start(bf16[320,2048]{1,0:T(8,128)(2,1)S(1)} %bitcast.1167), channel_id=1, source_target_pairs={{0,16},{16,0},{1,17},{17,1},{2,18},{18,2},{3,19},{19,3},{4,20},{20... | collective-permute-start | bytes 3932168 | tf_op jit(solution)/shard_map/ppermute | solution.py:468
  446.1 6.8 collective-permute-done.136
  516.6 8.3 collective-permute-done.170
  531.4 11.7 collective-permute-done.180
  571.7 20.4 %collective-permute-start.109 = (bf16[320,1024]{1,0:T(8,128)(2,1)}, bf16[320,1024]{1,0:T(8,128)(2,1)}, u32[]{:S(2)}, u32[]{:S(2)}) collective-permute-start(bf16[320,1024]{1,0:T(8,128)(2,1)} %get-tuple-element.94), channel_id=1, source_target_pairs={{0,16},{16,0},{1,17},{17,1},{2,18},{18,2},{3,19},{19,3},{4,20},{20... | collective-permute-start | bytes 1966088 | tf_op jit(solution)/shard_map/ppermute | solution.py:468
  666.9 19.2 %shard_map.280 = (bf16[320,4096]{1,0:T(8,128)(2,1)}, f32[1,4096]{1,0:T(1,128)}, f32[320,1024]{1,0:T(8,128)}, bf16[320,1024]{1,0:T(8,128)(2,1)}, bf16[4,320,256]{2,1,0:T(8,128)(2,1)}, /*index=5*/f32[8,1024]{1,0:T(8,128)}) custom-call(s32[1]{0:T(128)} %bitcast.sel_ref, bf16[320,1024]{1,0:T(8,128)(2,1)} %get-tuple-element.73.dy_ref, ...), custom_call_target="tpu_custom_call" | custom-call | flops 6039797760 | bytes 31457280 | tf_op jit(solution)/shard_map/pallas_call | solution.py:393
  690.4 15.8 %dynamic-slice_reduce_fusion.7 = (bf16[320,16,128]{2,1,0:T(8,128)(2,1)S(1)}, bf16[320,16,128]{2,1,0:T(8,128)(2,1)S(1)}) fusion(bf16[320,16,2,128]{3,2,1,0:T(2,128)(2,1)S(1)} %reshape.1296, s32[]{:T(128)S(6)} %select_n.891, s32[]{:T(128)S(6)} %select_n.892), kind=kLoop, calls=%fused_computation.33 | loop fusion | bytes 5242888 | tf_op jit(solution)/shard_map/jit(dynamic_index_in_dim)/dynamic_slice | solution.py:472
  726.8 22.9 %collective-permute-start.23 = (bf16[2,320,256]{2,1,0:T(8,128)(2,1)S(1)}, bf16[2,320,256]{2,1,0:T(8,128)(2,1)S(1)}, u32[]{:S(2)}, u32[]{:S(2)}) collective-permute-start(bf16[2,320,256]{2,1,0:T(8,128)(2,1)S(1)} %get-tuple-element.249), channel_id=1, source_target_pairs={{0,16},{16,0},{1,17},{17,1},{2,18},{18,2},{3,19},{19,3},{4,20},{20... | collective-permute-start | bytes 983048 | tf_op jit(solution)/shard_map/ppermute | solution.py:468
  752.3 28.5 %shard_map.281 = (bf16[1280,768]{1,0:T(8,128)(2,1)}, f32[8,256]{1,0:T(8,128)}) custom-call(bf16[1280,256]{1,0:T(8,128)(2,1)} %get-tuple-element.57.q_ref, bf16[1280,256]{1,0:T(8,128)(2,1)} %bitcast.1198, bf16[1280,256]{1,0:T(8,128)(2,1)} %get-tuple-element.58.k_ref, bf16[1280,256]{1,0:T(8,128)(2,1)} %get-tuple-element.59.v_ref, ...), custom_call_target="tpu_custom_call" | custom-call | flops 16777216000 | bytes 6291456 | tf_op jit(solution)/shard_map/pallas_call | solution.py:193
  866.6 19.1 %collective-permute-start.107 = (f32[64,512]{1,0:T(8,128)S(1)}, f32[64,512]{1,0:T(8,128)S(1)}, u32[]{:S(2)}, u32[]{:S(2)}) collective-permute-start(f32[64,512]{1,0:T(8,128)S(1)} %get-tuple-element.285), channel_id=1, source_target_pairs={{16,0},{17,1},{18,2},{19,3},{20,4},{21,5},{22,6},{23,7},{24,8},{25... | collective-permute-start | bytes 393224 | tf_op jit(solution)/shard_map/ppermute | solution.py:677
  888.2 8.7 collective-permute-done.156
  897.2 8.0 collective-permute-done.160
  928.8 10.3 collective-permute-done.152
  960.5 7.4 collective-permute-done.122
  1017.2 17.2 %collective-permute-start.24 = (bf16[2,320,1024]{2,1,0:T(8,128)(2,1)}, bf16[2,320,1024]{2,1,0:T(8,128)(2,1)}, u32[]{:S(2)}, u32[]{:S(2)}) collective-permute-start(bf16[2,320,1024]{2,1,0:T(8,128)(2,1)} %dynamic-slice_bitcast_fusion), channel_id=1, source_target_pairs={{0,16},{16,0},{1,17},{17,1},{2,18},{18,2},{3,19},{19,3},{4,20},{20... | collective-permute-start | bytes 3932168 | tf_op jit(solution)/shard_map/ppermute | solution.py:468
  1054.6 9.8 collective-permute-done.36
  1083.9 8.9 collective-permute-start.183
  1143.2 9.0 collective-permute-start.69
  (1045 shorter events, 750.2 us)
Async XLA Ops:
  0.7 93.5 %collective-permute-start.8 = (bf16[1024,4096]{1,0:T(8,128)(2,1)}, bf16[1024,4096]{1,0:T(8,128)(2,1)}, u32[]{:S(2)}, u32[]{:S(2)}) collective-permute-start(bf16[1024,4096]{1,0:T(8,128)(2,1)} %bitcast.1078), channel_id=1, source_target_pairs={{0,16},{16,0},{1,17},{17,1},{2,18},{18,2},{3,19},{19,3},{4,20},{20... | collective-permute-start | bytes 25165832 | tf_op jit(solution)/shard_map/ppermute | solution.py:468
  1.4 92.8 %collective-permute-start.9 = (bf16[4096,1024]{1,0:T(8,128)(2,1)}, bf16[4096,1024]{1,0:T(8,128)(2,1)}, u32[]{:S(2)}, u32[]{:S(2)}) collective-permute-start(bf16[4096,1024]{1,0:T(8,128)(2,1)} %bitcast.1083), channel_id=1, source_target_pairs={{0,16},{16,0},{1,17},{17,1},{2,18},{18,2},{3,19},{19,3},{4,20},{20... | collective-permute-start | bytes 25165832 | tf_op jit(solution)/shard_map/ppermute | solution.py:468
  16.2 34.8 %collective-permute-start.3 = (bf16[1024,768]{1,0:T(8,128)(2,1)}, bf16[1024,768]{1,0:T(8,128)(2,1)}, u32[]{:S(2)}, u32[]{:S(2)}) collective-permute-start(bf16[1024,768]{1,0:T(8,128)(2,1)} %copy.178), channel_id=1, source_target_pairs={{0,16},{16,0},{1,17},{17,1},{2,18},{18,2},{3,19},{19,3},{4,20},{20... | collective-permute-start | bytes 4718600 | tf_op jit(solution)/shard_map/ppermute | solution.py:468
  48.6 40.8 %collective-permute-start.7 = (bf16[1024,1024]{1,0:T(8,128)(2,1)}, bf16[1024,1024]{1,0:T(8,128)(2,1)}, u32[]{:S(2)}, u32[]{:S(2)}) collective-permute-start(bf16[1024,1024]{1,0:T(8,128)(2,1)} %bitcast.1156), channel_id=1, source_target_pairs={{0,16},{16,0},{1,17},{17,1},{2,18},{18,2},{3,19},{19,3},{4,20},{20... | collective-permute-start | bytes 6291464 | tf_op jit(solution)/shard_map/ppermute | solution.py:468
  168.3 260.9 %collective-permute-start.164 = (bf16[320,1024]{1,0:T(8,128)(2,1)}, bf16[320,1024]{1,0:T(8,128)(2,1)}, u32[]{:S(2)}, u32[]{:S(2)}) collective-permute-start(bf16[320,1024]{1,0:T(8,128)(2,1)} %bitcast_select_fusion.dy_ref), channel_id=1, source_target_pairs={{0,16},{16,0},{1,17},{17,1},{2,18},{18,2},{3,19},{19,3},{4,20},{20... | collective-permute-start | bytes 1966088 | tf_op jit(solution)/shard_map/ppermute | solution.py:468
  169.5 637.6 %collective-permute-start.71 = (bf16[320,512]{1,0:T(8,128)(2,1)}, bf16[320,512]{1,0:T(8,128)(2,1)}, u32[]{:S(2)}, u32[]{:S(2)}) collective-permute-start(bf16[320,512]{1,0:T(8,128)(2,1)} %bitcast.565), channel_id=1, source_target_pairs={{0,16},{16,0},{1,17},{17,1},{2,18},{18,2},{3,19},{19,3},{4,20},{20... | collective-permute-start | bytes 983048 | tf_op jit(solution)/shard_map/ppermute | solution.py:468
  236.8 54.9 %collective-permute-start.18 = (bf16[2,320,256]{2,1,0:T(8,128)(2,1)}, bf16[2,320,256]{2,1,0:T(8,128)(2,1)S(1)}, u32[]{:S(2)}, u32[]{:S(2)}) collective-permute-start(bf16[2,320,256]{2,1,0:T(8,128)(2,1)} %get-tuple-element.255), channel_id=1, source_target_pairs={{0,1},{1,0},{2,3},{3,2},{4,5},{5,4},{6,7},{7,6},{8,9},{9,8},{10,11... | collective-permute-start | bytes 983048 | tf_op jit(solution)/shard_map/ppermute | solution.py:468
  291.7 64.1 %collective-permute-start.10 = (bf16[320,1024]{1,0:T(8,128)(2,1)S(1)}, bf16[320,1024]{1,0:T(8,128)(2,1)}, u32[]{:S(2)}, u32[]{:S(2)}) collective-permute-start(bf16[320,1024]{1,0:T(8,128)(2,1)S(1)} %copy-done.4), channel_id=1, source_target_pairs={{16,2},{17,3},{18,0},{19,1},{20,6},{21,7},{22,4},{23,5},{24,10},{2... | collective-permute-start | bytes 1966088 | tf_op jit(solution)/shard_map/ppermute | solution.py:571
  294.5 61.3 %collective-permute-start.15 = (bf16[320,1024]{1,0:T(8,128)(2,1)}, bf16[320,1024]{1,0:T(8,128)(2,1)}, u32[]{:S(2)}, u32[]{:S(2)}) collective-permute-start(bf16[320,1024]{1,0:T(8,128)(2,1)} %get-tuple-element.66), channel_id=1, source_target_pairs={{0,16},{1,17},{2,18},{3,19},{4,20},{5,21},{6,22},{7,23},{8,24},{9,... | collective-permute-start | bytes 1966088 | tf_op jit(solution)/shard_map/ppermute | solution.py:568
  301.0 55.3 %collective-permute-start.16 = (bf16[320,1024]{1,0:T(8,128)(2,1)}, bf16[320,1024]{1,0:T(8,128)(2,1)}, u32[]{:S(2)}, u32[]{:S(2)}) collective-permute-start(bf16[320,1024]{1,0:T(8,128)(2,1)} %get-tuple-element.66), channel_id=1, source_target_pairs={{16,18},{17,19},{18,16},{19,17},{20,22},{21,23},{22,20},{23,21},{2... | collective-permute-start | bytes 1966088 | tf_op jit(solution)/shard_map/ppermute | solution.py:571
  355.7 441.7 %collective-permute-start.147 = (bf16[320,2048]{1,0:T(8,128)(2,1)}, bf16[320,2048]{1,0:T(8,128)(2,1)}, u32[]{:S(2)}, u32[]{:S(2)}) collective-permute-start(bf16[320,2048]{1,0:T(8,128)(2,1)} %bitcast.1048), channel_id=1, source_target_pairs={{0,16},{16,0},{1,17},{17,1},{2,18},{18,2},{3,19},{19,3},{4,20},{20... | collective-permute-start | bytes 3932168 | tf_op jit(solution)/shard_map/ppermute | solution.py:468
  355.8 73.4 %collective-permute-start.165 = (bf16[320,2048]{1,0:T(8,128)(2,1)S(1)}, bf16[320,2048]{1,0:T(8,128)(2,1)S(1)}, u32[]{:S(2)}, u32[]{:S(2)}) collective-permute-start(bf16[320,2048]{1,0:T(8,128)(2,1)S(1)} %bitcast.1169), channel_id=1, source_target_pairs={{0,16},{16,0},{1,17},{17,1},{2,18},{18,2},{3,19},{19,3},{4,20},{20... | collective-permute-start | bytes 3932168 | tf_op jit(solution)/shard_map/ppermute | solution.py:468
  429.2 97.2 %collective-permute-start.20 = (bf16[2,320,1024]{2,1,0:T(8,128)(2,1)S(1)}, bf16[2,320,1024]{2,1,0:T(8,128)(2,1)S(1)}, u32[]{:S(2)}, u32[]{:S(2)}) collective-permute-start(bf16[2,320,1024]{2,1,0:T(8,128)(2,1)S(1)} %dynamic-slice_bitcast_fusion.1), channel_id=1, source_target_pairs={{0,16},{16,0},{1,17},{17,1},{2,18},{18,2},{3,19},{19,3},{4,20},{20... | collective-permute-start | bytes 3932168 | tf_op jit(solution)/shard_map/ppermute | solution.py:468
  515.1 77.0 %collective-permute-start.128 = (bf16[2,2,2,128,384]{4,3,1,2,0:T(8,128)(2,1)S(1)}, bf16[2,2,2,128,384]{4,3,1,2,0:T(8,128)(2,1)S(1)}, u32[]{:S(2)}, u32[]{:S(2)}) collective-permute-start(bf16[2,2,2,128,384]{4,3,1,2,0:T(8,128)(2,1)S(1)} %bitcast.1190), channel_id=1, source_target_pairs={{0,4},{4,0},{8,12},{12,8},{1,5},{5,1},{9,13},{13,9},{2,6},{6,2},{1... | collective-permute-start | bytes 2359304 | tf_op jit(solution)/shard_map/ppermute | solution.py:468
  524.9 69.0 %collective-permute-start.132 = (bf16[2,2,2,128,384]{4,3,1,2,0:T(8,128)(2,1)S(1)}, bf16[2,2,2,128,384]{4,3,1,2,0:T(8,128)(2,1)S(1)}, u32[]{:S(2)}, u32[]{:S(2)}) collective-permute-start(bf16[2,2,2,128,384]{4,3,1,2,0:T(8,128)(2,1)S(1)} %bitcast.1189), channel_id=1, source_target_pairs={{0,8},{4,12},{8,0},{12,4},{1,9},{5,13},{9,1},{13,5},{2,10},{6,14},... | collective-permute-start | bytes 2359304 | tf_op jit(solution)/shard_map/ppermute | solution.py:468
  571.7 348.2 %collective-permute-start.109 = (bf16[320,1024]{1,0:T(8,128)(2,1)}, bf16[320,1024]{1,0:T(8,128)(2,1)}, u32[]{:S(2)}, u32[]{:S(2)}) collective-permute-start(bf16[320,1024]{1,0:T(8,128)(2,1)} %get-tuple-element.94), channel_id=1, source_target_pairs={{0,16},{16,0},{1,17},{17,1},{2,18},{18,2},{3,19},{19,3},{4,20},{20... | collective-permute-start | bytes 1966088 | tf_op jit(solution)/shard_map/ppermute | solution.py:468
  592.1 36.2 %collective-permute-start.167 = (bf16[2,2,64,640]{3,2,0,1:T(8,128)(2,1)S(1)}, bf16[2,2,64,640]{3,2,0,1:T(8,128)(2,1)S(1)}, u32[]{:S(2)}, u32[]{:S(2)}) collective-permute-start(bf16[2,2,64,640]{3,2,0,1:T(8,128)(2,1)S(1)} %dynamic-slice_bitcast_fusion.21), channel_id=1, source_target_pairs={{0,8},{4,12},{8,0},{12,4},{1,9},{5,13},{9,1},{13,5},{2,10},{6,14},... | collective-permute-start | bytes 983048 | tf_op jit(solution)/shard_map/ppermute | solution.py:468
  660.5 53.8 %collective-permute-start.130 = (bf16[2,128,384]{2,1,0:T(8,128)(2,1)}, bf16[2,128,384]{2,1,0:T(8,128)(2,1)}, u32[]{:S(2)}, u32[]{:S(2)}) collective-permute-start(bf16[2,128,384]{2,1,0:T(8,128)(2,1)} %dynamic-slice_bitcast_fusion.39), channel_id=1, source_target_pairs={{0,1},{1,0},{2,3},{3,2},{4,5},{5,4},{6,7},{7,6},{8,9},{9,8},{10,11... | collective-permute-start | bytes 589832 | tf_op jit(solution)/shard_map/ppermute | solution.py:468
  661.4 54.8 %collective-permute-start.134 = (bf16[2,128,384]{2,1,0:T(8,128)(2,1)}, bf16[2,128,384]{2,1,0:T(8,128)(2,1)}, u32[]{:S(2)}, u32[]{:S(2)}) collective-permute-start(bf16[2,128,384]{2,1,0:T(8,128)(2,1)} %dynamic-slice_bitcast_fusion.38), channel_id=1, source_target_pairs={{0,1},{1,0},{2,3},{3,2},{4,5},{5,4},{6,7},{7,6},{8,9},{9,8},{10,11... | collective-permute-start | bytes 589832 | tf_op jit(solution)/shard_map/ppermute | solution.py:468
  721.0 144.7 %collective-permute-start.106 = (f32[64,512]{1,0:T(8,128)}, f32[64,512]{1,0:T(8,128)}, u32[]{:S(2)}, u32[]{:S(2)}) collective-permute-start(f32[64,512]{1,0:T(8,128)} %pad_maximum_fusion.10), channel_id=1, source_target_pairs={{0,16},{1,17},{2,18},{3,19},{4,20},{5,21},{6,22},{7,23},{8,24},{9,... | collective-permute-start | bytes 393224 | tf_op jit(solution)/shard_map/ppermute | solution.py:677
  751.0 48.2 %collective-permute-start.146 = (bf16[320,1024]{1,0:T(8,128)(2,1)}, bf16[320,1024]{1,0:T(8,128)(2,1)}, u32[]{:S(2)}, u32[]{:S(2)}) collective-permute-start(bf16[320,1024]{1,0:T(8,128)(2,1)} %get-tuple-element.73.dy_ref), channel_id=1, source_target_pairs={{0,16},{16,0},{1,17},{17,1},{2,18},{18,2},{3,19},{19,3},{4,20},{20... | collective-permute-start | bytes 1966088 | tf_op jit(solution)/shard_map/ppermute | solution.py:468
  797.5 332.8 %collective-permute-start.68 = (f32[192,512]{1,0:T(8,128)}, f32[192,512]{1,0:T(8,128)}, u32[]{:S(2)}, u32[]{:S(2)}) collective-permute-start(f32[192,512]{1,0:T(8,128)} %pad_maximum_fusion.8), channel_id=1, source_target_pairs={{0,16},{1,17},{2,18},{3,19},{4,20},{5,21},{6,22},{7,23},{8,24},{9,... | collective-permute-start | bytes 1179656 | tf_op jit(solution)/shard_map/ppermute | solution.py:677
  808.1 114.7 %collective-permute-start.108 = (bf16[320,2048]{1,0:T(8,128)(2,1)S(1)}, bf16[320,2048]{1,0:T(8,128)(2,1)S(1)}, u32[]{:S(2)}, u32[]{:S(2)}) collective-permute-start(bf16[320,2048]{1,0:T(8,128)(2,1)S(1)} %bitcast.1165), channel_id=1, source_target_pairs={{0,16},{16,0},{1,17},{17,1},{2,18},{18,2},{3,19},{19,3},{4,20},{20... | collective-permute-start | bytes 3932168 | tf_op jit(solution)/shard_map/ppermute | solution.py:468
  916.8 130.4 %collective-permute-start.182 = (f32[64,2048]{1,0:T(8,128)S(1)}, f32[64,2048]{1,0:T(8,128)S(1)}, u32[]{:S(2)}, u32[]{:S(2)}) collective-permute-start(f32[64,2048]{1,0:T(8,128)S(1)} %copy-done.62), channel_id=1, source_target_pairs={{0,16},{1,17},{2,18},{3,19},{4,20},{5,21},{6,22},{7,23},{8,24},{9,... | collective-permute-start | bytes 1572872 | tf_op jit(solution)/shard_map/ppermute | solution.py:677
  918.2 288.7 %collective-permute-start.27 = (bf16[320,1024]{1,0:T(8,128)(2,1)}, bf16[320,1024]{1,0:T(8,128)(2,1)}, u32[]{:S(2)}, u32[]{:S(2)}) collective-permute-start(bf16[320,1024]{1,0:T(8,128)(2,1)} %get-tuple-element.73.dy_ref), channel_id=1, source_target_pairs={{0,16},{1,17},{2,18},{3,19},{4,20},{5,21},{6,22},{7,23},{8,24},{9,... | collective-permute-start | bytes 1966088 | tf_op jit(solution)/shard_map/ppermute | solution.py:568
  968.5 41.7 %collective-permute-start.35 = (bf16[2,2,2,192,128]{4,3,2,1,0:T(8,128)(2,1)S(1)}, bf16[2,2,2,192,128]{4,3,2,1,0:T(8,128)(2,1)S(1)}, u32[]{:S(2)}, u32[]{:S(2)}) collective-permute-start(bf16[2,2,2,192,128]{4,3,2,1,0:T(8,128)(2,1)S(1)} %dynamic-slice_bitcast_fusion.19), channel_id=1, source_target_pairs={{0,4},{4,0},{8,12},{12,8},{1,5},{5,1},{9,13},{13,9},{2,6},{6,2},{1... | collective-permute-start | bytes 1179656 | tf_op jit(solution)/shard_map/ppermute | solution.py:468
  1047.1 36.7 %collective-permute-start.110 = (bf16[2,2,2,128,384]{4,3,2,1,0:T(8,128)(2,1)}, bf16[2,2,2,128,384]{4,3,2,1,0:T(8,128)(2,1)}, u32[]{:S(2)}, u32[]{:S(2)}) collective-permute-start(bf16[2,2,2,128,384]{4,3,2,1,0:T(8,128)(2,1)} %dynamic-slice_bitcast_fusion.2), channel_id=1, source_target_pairs={{0,4},{4,0},{8,12},{12,8},{1,5},{5,1},{9,13},{13,9},{2,6},{6,2},{1... | collective-permute-start | bytes 2359304 | tf_op jit(solution)/shard_map/ppermute | solution.py:468
  1047.2 47.8 %collective-permute-start.114 = (bf16[2,2,2,128,384]{4,3,1,2,0:T(8,128)(2,1)}, bf16[2,2,2,128,384]{4,3,1,2,0:T(8,128)(2,1)}, u32[]{:S(2)}, u32[]{:S(2)}) collective-permute-start(bf16[2,2,2,128,384]{4,3,1,2,0:T(8,128)(2,1)} %bitcast.1060), channel_id=1, source_target_pairs={{0,8},{4,12},{8,0},{12,4},{1,9},{5,13},{9,1},{13,5},{2,10},{6,14},... | collective-permute-start | bytes 2359304 | tf_op jit(solution)/shard_map/ppermute | solution.py:468
  1078.7 128.2 %collective-permute-start.28 = (bf16[320,1024]{1,0:T(8,128)(2,1)}, bf16[320,1024]{1,0:T(8,128)(2,1)}, u32[]{:S(2)}, u32[]{:S(2)}) collective-permute-start(bf16[320,1024]{1,0:T(8,128)(2,1)} %get-tuple-element.73.dy_ref), channel_id=1, source_target_pairs={{16,18},{17,19},{18,16},{19,17},{20,22},{21,23},{22,20},{23,21},{2... | collective-permute-start | bytes 1966088 | tf_op jit(solution)/shard_map/ppermute | solution.py:571
  1083.9 48.8 %collective-permute-start.183 = (f32[64,2048]{1,0:T(8,128)S(1)}, f32[64,2048]{1,0:T(8,128)S(1)}, u32[]{:S(2)}, u32[]{:S(2)}) collective-permute-start(f32[64,2048]{1,0:T(8,128)S(1)} %copy-done.61), channel_id=1, source_target_pairs={{16,0},{17,1},{18,2},{19,3},{20,4},{21,5},{22,6},{23,7},{24,8},{25... | collective-permute-start | bytes 1572872 | tf_op jit(solution)/shard_map/ppermute | solution.py:677
  1128.9 68.0 %collective-permute-start.144 = (f32[128,1024]{1,0:T(8,128)}, f32[128,1024]{1,0:T(8,128)}, u32[]{:S(2)}, u32[]{:S(2)}) collective-permute-start(f32[128,1024]{1,0:T(8,128)} %pad_maximum_fusion.4), channel_id=1, source_target_pairs={{0,16},{1,17},{2,18},{3,19},{4,20},{5,21},{6,22},{7,23},{8,24},{9,... | collective-permute-start | bytes 1572872 | tf_op jit(solution)/shard_map/ppermute | solution.py:677
  1168.9 38.0 %collective-permute-start.26 = (bf16[320,1024]{1,0:T(8,128)(2,1)S(1)}, bf16[320,1024]{1,0:T(8,128)(2,1)S(1)}, u32[]{:S(2)}, u32[]{:S(2)}) collective-permute-start(bf16[320,1024]{1,0:T(8,128)(2,1)S(1)} %copy-done.54), channel_id=1, source_target_pairs={{16,2},{17,3},{18,0},{19,1},{20,6},{21,7},{22,4},{23,5},{24,10},{2... | collective-permute-start | bytes 1966088 | tf_op jit(solution)/shard_map/ppermute | solution.py:571
  (261 other events, 2737.5 us)

commit v2 on v1

--- a/solution.py
+++ b/solution.py
@@ -141,82 +141,13 @@
     )(q, k, v, mask)
 
 
-def attend_back_kernel(
-    q_ref, do_ref, k_ref, v_ref, lse_ref, mask_ref, dj_ref, sums_ref, dk_acc, dv_acc
-):
-    step = pl.program_id(0)
-    width = q_ref.shape[1]
-    heads = width // DH
-    scale = DH ** (-0.5)
-
-    @pl.when(step == 0)
-    def _():
-        dk_acc[...] = jnp.zeros_like(dk_acc)
-        dv_acc[...] = jnp.zeros_like(dv_acc)
-        sums_ref[...] = jnp.zeros_like(sums_ref)
-
-    q = q_ref[...]
-    grad = do_ref[...]
-    keys = k_ref[...]
-    values = v_ref[...]
-    mask = mask_ref[...]
-    totals = lse_ref[...]
-    d_q = jnp.zeros((BQ, width), F32)
-    for head in range(heads):
-        mine = head_lanes((BQ, width), head)
-        q_head = jnp.where(mine, q, jnp.zeros_like(q))
-        grad_head = jnp.where(mine, grad, jnp.zeros_like(grad))
-        scores = mm_nt(q_head, keys) * SCALE2 + mask
-        probs = jnp.exp2(scores - totals[:, head : head + 1])
-        d_probs = mm_nt(grad_head, values)
-        term = jnp.sum(probs * d_probs, axis=-1, keepdims=True)
-        d_scores = (probs * (d_probs - term)).astype(BF16)
-        dv_acc[...] += mm_tn(probs.astype(BF16), grad_head)
-        dk_acc[...] += mm_tn(d_scores, q_head)
-        d_q = jnp.where(mine, mm(d_scores, keys), d_q)
-    low = (d_q * scale).astype(BF16)
-    dj_ref[pl.ds(pl.multiple_of(step * BQ, BQ), BQ), :width] = low
-    sums_ref[0:1, :] += jnp.sum(low.astype(F32), axis=0, keepdims=True)
-
-    @pl.when(step == pl.num_programs(0) - 1)
-    def _():
-        dj_ref[:, width : 2 * width] = (dk_acc[...] * scale).astype(BF16)
-        low_v = dv_acc[...].astype(BF16)
-        dj_ref[:, 2 * width :] = low_v
-        sums_ref[1:2, :] = jnp.sum(low_v.astype(F32), axis=0, keepdims=True)
-
-
-def attend_back_call(q, d_o, k, v, lse, mask):
-    length, width = q.shape
-    row = lambda i: (i, 0)
-    whole = lambda i: (0, 0)
-    return pl.pallas_call(
-        attend_back_kernel,
-        grid=(length // BQ,),
-        in_specs=[
-            pl.BlockSpec((BQ, width), row),
-            pl.BlockSpec((BQ, width), row),
-            pl.BlockSpec((length, width), whole),
-            pl.BlockSpec((length, width), whole),
-            pl.BlockSpec((BQ, 128), row),
-            pl.BlockSpec((1, length), whole),
-        ],
-        out_specs=[
-            pl.BlockSpec((length, 3 * width), whole),
-            pl.BlockSpec((8, width), whole),
-        ],
-        out_shape=[
-            jax.ShapeDtypeStruct((length, 3 * width), BF16),
-            jax.ShapeDtypeStruct((8, width), F32),
-        ],
-        scratch_shapes=[pltpu.VMEM((length, width), F32), pltpu.VMEM((length, width), F32)],
-        compiler_params=params(),
-        cost_estimate=pl.CostEstimate(
-            flops=40 * length * length * width,
-            bytes_accessed=6 * 2**20,
-            transcendentals=length * length * width // DH,
-        ),
-    )(q, d_o, k, v, lse, mask)
+def shards_of():
+    return lax.axis_size("dp") * lax.axis_size("seq")
+
+
+def put_halves(ref, value, unit):
+    for at in range(value.shape[1] // unit):
+        ref[at % 2, :, at // 2 * unit : (at // 2 + 1) * unit] = value[:, at * unit : (at + 1) * unit]
 
 
 GELU_A = math.sqrt(2.0 / math.pi)
@@ -243,6 +174,7 @@
 ):
     step = pl.program_id(0)
     groups, _, width = o_ref.shape
+    unit = FF // shards_of() // 2
 
     @pl.when(step == 0)
     def _():
@@ -259,7 +191,7 @@
         u_ref[...] = upper
         inner = GELU_A * (upper + GELU_B * upper * upper * upper)
         gated = (0.5 * upper * (1.0 + jnp.tanh(inner))).astype(BF16)
-        g_ref[...] = gated
+        put_halves(g_ref, gated, unit)
         acc[...] += mm(gated, down_ref[...])
 
     pl.when(sel_ref[0] == 0)(lambda: part(up0_ref, down0_ref))
@@ -297,7 +229,7 @@
                 pl.BlockSpec((rows, D), whole),
                 pl.BlockSpec((rows, D), whole),
                 pl.BlockSpec((rows, FC), chunk),
-                pl.BlockSpec((rows, FC), chunk),
+                pl.BlockSpec((2, rows, FC // 2), lambda i, s: (0, 0, i)),
                 pl.BlockSpec((rows, D), whole),
             ],
             scratch_shapes=[pltpu.VMEM((rows, D), F32)],
@@ -306,7 +238,7 @@
             jax.ShapeDtypeStruct((rows, D), F32),
             jax.ShapeDtypeStruct((rows, D), BF16),
             jax.ShapeDtypeStruct((rows, FF), F32),
-            jax.ShapeDtypeStruct((rows, FF), BF16),
+            jax.ShapeDtypeStruct((2, rows, FF // 2), BF16),
             jax.ShapeDtypeStruct((rows, D), BF16),
         ],
         compiler_params=params(),
@@ -314,121 +246,6 @@
             flops=2 * rows * D * (D + 2 * FF), bytes_accessed=30 * 2**20, transcendentals=rows * FF
         ),
     )(sel, o_all, x_own, wo, vecs, bup, ups[0], ups[1], downs[0], downs[1])
-
-
-def mlp_back_kernel(
-    sel_ref,
-    dy_ref,
-    h_ref,
-    wo_ref,
-    vec_ref,
-    u_ref,
-    up0_ref,
-    up1_ref,
-    down0_ref,
-    down1_ref,
-    du_ref,
-    gbup_ref,
-    dh_ref,
-    dr_ref,
-    do_ref,
-    sums_ref,
-    acc,
-):
-    step = pl.program_id(0)
-    groups, _, width = do_ref.shape
-
-    @pl.when(step == 0)
-    def _():
-        acc[...] = jnp.zeros_like(acc)
-
-    def part(up_ref, down_ref):
-        d_gated = mm_nt(dy_ref[...], down_ref[...])
-        upper = u_ref[...]
-        square = upper * upper
-        turn = jnp.tanh(GELU_A * upper * (1.0 + GELU_B * square))
-        slope = 0.5 * (1.0 + turn) + (0.5 * GELU_A) * upper * (1.0 - turn * turn) * (
-            1.0 + (3.0 * GELU_B) * square
-        )
-        d_upper = (d_gated * slope).astype(BF16)
-        du_ref[...] = d_upper
-        gbup_ref[...] = jnp.sum(d_upper.astype(F32), axis=0, keepdims=True)
-        acc[...] += mm_nt(d_upper, up_ref[...])
-
-    pl.when(sel_ref[0] == 0)(lambda: part(up0_ref, down0_ref))
-    pl.when(sel_ref[0] == 1)(lambda: part(up1_ref, down1_ref))
-
-    @pl.when(step == pl.num_programs(0) - 1)
-    def _():
-        normal, inverse = norm_stats(h_ref[...])
-        d_out = dy_ref[...].astype(F32)
-        d_normed = acc[...]
-        sums_ref[...] = jnp.zeros_like(sums_ref)
-        sums_ref[0:1, :] = jnp.sum(d_normed * normal, axis=0, keepdims=True)
-        sums_ref[1:2, :] = jnp.sum(d_normed, axis=0, keepdims=True)
-        d_normal = d_normed * vec_ref[1:2, :]
-        d_hidden = d_out + inverse * (
-            d_normal
-            - jnp.mean(d_normal, axis=-1, keepdims=True)
-            - normal * jnp.mean(d_normal * normal, axis=-1, keepdims=True)
-        )
-        dh_ref[...] = d_hidden
-        d_branch = d_hidden.astype(BF16)
-        dr_ref[...] = d_branch
-        sums_ref[2:3, :] = jnp.sum(d_branch.astype(F32), axis=0, keepdims=True)
-        sums_ref[3:4, :] = jnp.sum(d_out, axis=0, keepdims=True)
-        for group in range(groups):
-            do_ref[group] = mm_nt(
-                d_branch, wo_ref[group * width : (group + 1) * width, :]
-            ).astype(BF16)
-
-
-def mlp_back_call(sel, dy, hidden, wo, vecs, upper, ups, downs, groups):
-    rows = dy.shape[0]
-    width = D // groups
-    whole = lambda i, s: (0, 0)
-    col = lambda which: (lambda i, s: (0, jnp.where(s[0] == which, i, 0)))
-    line = lambda which: (lambda i, s: (jnp.where(s[0] == which, i, 0), 0))
-    chunk = lambda i, s: (0, i)
-    return pl.pallas_call(
-        mlp_back_kernel,
-        grid_spec=pltpu.PrefetchScalarGridSpec(
-            num_scalar_prefetch=1,
-            grid=(NCH,),
-            in_specs=[
-                pl.BlockSpec((rows, D), whole),
-                pl.BlockSpec((rows, D), whole),
-                pl.BlockSpec((D, D), whole),
-                pl.BlockSpec((8, D), whole),
-                pl.BlockSpec((rows, FC), chunk),
-                pl.BlockSpec((D, FC), col(0)),
-                pl.BlockSpec((D, FC), col(1)),
-                pl.BlockSpec((FC, D), line(0)),
-                pl.BlockSpec((FC, D), line(1)),
-            ],
-            out_specs=[
-                pl.BlockSpec((rows, FC), chunk),
-                pl.BlockSpec((1, FC), chunk),
-                pl.BlockSpec((rows, D), whole),
-                pl.BlockSpec((rows, D), whole),
-                pl.BlockSpec((groups, rows, width), lambda i, s: (0, 0, 0)),
-                pl.BlockSpec((8, D), whole),
-            ],
-            scratch_shapes=[pltpu.VMEM((rows, D), F32)],
-        ),
-        out_shape=[
-            jax.ShapeDtypeStruct((rows, FF), BF16),
-            jax.ShapeDtypeStruct((1, FF), F32),
-            jax.ShapeDtypeStruct((rows, D), F32),
-            jax.ShapeDtypeStruct((rows, D), BF16),
-            jax.ShapeDtypeStruct((groups, rows, width), BF16),
-            jax.ShapeDtypeStruct((8, D), F32),
-        ],
-        compiler_params=params(),
-        cost_estimate=pl.CostEstimate(
-            flops=2 * rows * D * (D + 2 * FF), bytes_accessed=30 * 2**20, transcendentals=rows * FF
-        ),
-    )(sel, dy, hidden, wo, vecs, upper, ups[0], ups[1], downs[0], downs[1])
 
 
 def norm_back_kernel(mine_ref, other_ref, x_ref, dh_ref, gain_ref, dx_ref, sums_ref):
@@ -461,6 +278,541 @@
             flops=20 * x_own.size, bytes_accessed=10 * x_own.size, transcendentals=0
         ),
     )(mine, other, x_own, d_hidden, gain)
+
+
+MESH_AXES = ("dp", "seq")
+
+
+def axis_bits(dp_count, count):
+    bits = []
+    for axis, size in (("dp", dp_count), ("seq", count)):
+        mask = size // 2
+        while mask:
+            bits.append((axis, mask))
+            mask //= 2
+    return bits
+
+
+def stream_orders(dp_count, count):
+    dp_bits = dp_count.bit_length() - 1
+    seq_bits = count.bit_length() - 1
+    dp_dims = list(range(dp_bits))
+    seq_dims = list(range(dp_bits, dp_bits + seq_bits))[::-1]
+    return (
+        dp_dims[::-1] + seq_dims,
+        dp_dims + seq_dims,
+        seq_dims[:1] + dp_dims + seq_dims[1:],
+        seq_dims[:1] + dp_dims[::-1] + seq_dims[1:],
+    )
+
+
+def my_bit(axis, mask):
+    return lax.rem(lax.div(lax.axis_index(axis), mask), 2)
+
+
+def partner(axis, mask):
+    return lax.axis_index(axis) + mask * (1 - 2 * my_bit(axis, mask))
+
+
+def greet(bits):
+    barrier = pltpu.get_barrier_semaphore()
+    for axis, mask in bits:
+        pl.semaphore_signal(
+            barrier,
+            inc=1,
+            device_id={axis: partner(axis, mask)},
+            device_id_type=pl.DeviceIdType.MESH,
+        )
+    pl.semaphore_wait(barrier, len(bits))
+
+
+class Reducer:
+    def __init__(self, bits, order, src, cols, out, rows, compact, buffers, sems):
+        self.bits, self.order, self.src, self.cols = bits, order, src, cols
+        self.out, self.out_cols, self.buffers, self.sems = out, cols, buffers, sems
+        self.count, self.rows, self.compact = len(bits), rows, compact
+
+    @staticmethod
+    def scratch(count, rows, width):
+        shapes = [pltpu.VMEM((2,) * (count - 1) + (rows, width), BF16)]
+        for stage in range(count):
+            shapes.append(pltpu.VMEM((2,) * (count - 1 - stage) + (rows, width), BF16))
+        shapes += [
+            pltpu.SemaphoreType.DMA((count + 2,)),
+            pltpu.SemaphoreType.DMA((count + 2,)),
+            pltpu.SemaphoreType.DMA,
+        ]
+        return shapes
+
+    def place(self, stage):
+        left = [d for d in range(self.count) if d not in self.order[:stage]]
+        dim = self.order[stage]
+        return left, left.index(dim), self.bits[dim]
+
+    def cut(self, stage, index):
+        left, at, _ = self.place(stage)
+        where = [slice(None)] * len(left)
+        where[at] = index
+        return tuple(where)
+
+    def source(self, stage):
+        if stage == 0:
+            return self.src
+        return self.buffers[0] if stage == 1 else self.buffers[stage]
+
+    def copy(self, stage):
+        axis, mask = self.place(stage)[2]
+        where = self.cut(stage, 1 - my_bit(axis, mask))
+        if stage == 0:
+            where = where + (slice(None), pl.ds(*self.cols))
+        return pltpu.make_async_remote_copy(
+            src_ref=self.source(stage).at[where],
+            dst_ref=self.buffers[stage + 1],
+            send_sem=self.sems[0].at[stage],
+            recv_sem=self.sems[1].at[stage],
+            device_id={axis: partner(axis, mask)},
+            device_id_type=pl.DeviceIdType.MESH,
+        )
+
+    def load(self):
+        axis, mask = self.place(0)[2]
+        where = self.cut(0, my_bit(axis, mask)) + (slice(None), pl.ds(*self.cols))
+        return pltpu.make_async_copy(self.src.at[where], self.buffers[0], self.sems[2])
+
+    def share(self):
+        core = lax.axis_index("section")
+        return pltpu.make_async_remote_copy(
+            src_ref=self.out.at[core, :, pl.ds(*self.out_cols)],
+            dst_ref=self.out.at[core, :, pl.ds(*self.out_cols)],
+            send_sem=self.sems[0].at[self.count],
+            recv_sem=self.sems[1].at[self.count],
+            device_id={"section": 1 - core},
+            device_id_type=pl.DeviceIdType.MESH,
+        )
+
+    def trade(self):
+        third = self.rows // 3
+        core = lax.axis_index("section")
+        bit = lax.rem(lax.axis_index("seq"), 2)
+        row = pl.multiple_of((1 - bit) * 2 * third, third)
+        return pltpu.make_async_remote_copy(
+            src_ref=self.out.at[core, pl.ds(row, third), pl.ds(*self.out_cols)],
+            dst_ref=self.out.at[core, pl.ds(self.rows, third), pl.ds(*self.out_cols)],
+            send_sem=self.sems[0].at[self.count + 1],
+            recv_sem=self.sems[1].at[self.count + 1],
+            device_id={"seq": partner("seq", 1)},
+            device_id_type=pl.DeviceIdType.MESH,
+        )
+
+    def begin(self):
+        self.copy(0).start()
+        self.load().start()
+
+    def step(self, stage):
+        left, at, (axis, mask) = self.place(stage)
+        bit = my_bit(axis, mask)
+        if stage == 0:
+            self.load().wait()
+        self.copy(stage).wait_recv()
+        got = self.buffers[stage + 1]
+        rows = got.shape[-2]
+        chunk = 16
+        per = rows // chunk
+        last = stage == self.count - 1
+        core = lax.axis_index("section")
+        total = 2 ** (len(left) - 1)
+
+        def body(i, carry):
+            flat = lax.div(i, per)
+            row = pl.multiple_of(lax.rem(i, per) * chunk, chunk)
+            index = []
+            for j in range(len(left) - 1):
+                index.append(lax.rem(lax.div(flat, 2 ** (len(left) - 2 - j)), 2))
+            there = tuple(index) + (pl.ds(row, chunk), slice(None))
+            if stage == 0:
+                mine = self.buffers[0][there]
+            else:
+                own = index[:at] + [bit] + index[at:]
+                mine = self.source(stage)[tuple(own) + (pl.ds(row, chunk), slice(None))]
+            value = mine.astype(F32) + got[there].astype(F32)
+            if last:
+                self.out[core, pl.ds(row, chunk), pl.ds(*self.out_cols)] = value
+            elif stage == 0:
+                self.buffers[0][there] = value.astype(BF16)
+            else:
+                got[there] = value.astype(BF16)
+            return carry
+
+        lax.fori_loop(0, total * per, body, 0)
+        if not last:
+            self.copy(stage + 1).start()
+        elif self.compact:
+            self.trade().start()
+        else:
+            self.share().start()
+
+    def tail(self):
+        if self.compact:
+            self.trade().wait()
+            self.share().start()
+
+    def finish(self):
+        for stage in range(self.count):
+            self.copy(stage).wait_send()
+        self.share().wait()
+
+
+def part_widths(width):
+    unit = 128 if width % 128 == 0 else width
+    tiles = width // unit
+    first = -(-tiles // 3)
+    rest = tiles - 2 * first
+    if rest <= 0:
+        first = tiles // 2
+        rest = tiles - 2 * first
+    second = rest // 2
+    return tuple(unit * n for n in (first, first, rest - second, second))
+
+
+class Hosted:
+    def __init__(self, dp_count, count, shapes):
+        self.dp_count, self.count, self.shapes = dp_count, count, shapes
+        self.all_bits = axis_bits(dp_count, count)
+        self.plan = []
+        for index, (rows, width, compact) in enumerate(shapes):
+            bits = self.all_bits[:-1] if compact else self.all_bits
+            orders = stream_orders(dp_count, count)
+            widths = part_widths(width)
+            if compact:
+                last = len(bits)
+                orders = [tuple(d for d in order if d != last) for order in orders[:2]]
+                widths = (width // 2, width // 2)
+            start = 0
+            for order, size in zip(orders, widths):
+                pieces = [size] if size else []
+                if size >= 256 and not compact:
+                    first = 128 * -(-size // 256)
+                    pieces = [first, size - first]
+                for k, piece in enumerate(pieces):
+                    self.plan.append((index, tuple(order), bits, start, piece, rows, compact, k))
+                    start += piece
+        self.plan.sort(key=lambda p: (p[0], p[7]))
+        self.arrays = len(shapes)
+        self.events = []
+        for k, part in enumerate(self.plan):
+            for stage in range(len(part[2])):
+                order = 1.0 - 0.5**stage + 0.25 * part[7] + 0.02 * part[0]
+                self.events.append((order, k, stage))
+        self.events.sort()
+
+    def views(self, arrays):
+        out = []
+        for array, (_, _, compact) in zip(arrays, self.shapes):
+            depth = len(self.all_bits) - (1 if compact else 0)
+            out.append(array.reshape((2,) * depth + array.shape[1:]))
+        return out
+
+    def in_specs(self):
+        return [pl.BlockSpec(memory_space=pl.ANY)] * self.arrays
+
+    def out_shapes(self):
+        return [
+            jax.ShapeDtypeStruct((2, rows + (rows // 3 if compact else 0), width), F32)
+            for rows, width, compact in self.shapes
+        ]
+
+    def out_specs(self):
+        return [pl.BlockSpec(memory_space=pltpu.VMEM)] * self.arrays
+
+    def scratch(self):
+        shapes = [pltpu.VMEM(o.shape, F32) for o in self.out_shapes()]
+        for _, _, bits, _, size, rows, _, _ in self.plan:
+            shapes += Reducer.scratch(len(bits), rows, size)
+        return shapes
+
+    def bind(self, srcs, outs, scratch):
+        self.parts = []
+        self.outs, self.sums = outs, scratch[: self.arrays]
+        at = self.arrays
+        for index, order, bits, start, size, rows, compact, _ in self.plan:
+            depth = len(bits) + 1
+            mine = scratch[at : at + depth + 3]
+            at += depth + 3
+            self.parts.append(
+                Reducer(
+                    bits,
+                    order,
+                    srcs[index],
+                    (start, size),
+                    self.sums[index],
+                    rows,
+                    compact,
+                    mine[:depth],
+                    mine[depth:],
+                )
+            )
+    def begin(self):
+        greet(self.all_bits + [("section", 1)])
+        for part in self.parts:
+            part.begin()
+
+    def run(self, first, last):
+        for _, k, stage in self.events[first:last]:
+            self.parts[k].step(stage)
+
+    def slots(self, times, total):
+        edges = []
+        done = 0
+        for time in times:
+            while done < len(self.events) and self.expected(done) * total <= time:
+                done += 1
+            edges.append(done)
+        edges[-1] = len(self.events)
+        return list(zip([0] + edges[:-1], edges))
+
+    def expected(self, event):
+        _, k, stage = self.events[event]
+        late = self.plan[k][7]
+        return min(1.0, 0.3 + 0.25 * late + 0.5 * (1.0 - 0.5**stage))
+
+    def finish(self):
+        for part in self.parts:
+            part.tail()
+        for part in self.parts:
+            part.finish()
+        for out, value in zip(self.outs, self.sums):
+            out[...] = value[...]
+
+
+def reduce_kernel(host, *refs):
+    n = host.arrays
+    host.bind(refs[:n], refs[n : 2 * n], refs[2 * n :])
+    host.begin()
+    host.run(0, len(host.events))
+    host.finish()
+
+
+def reduce_call(host, arrays, collective_id):
+    return pl.pallas_call(
+        functools.partial(reduce_kernel, host),
+        in_specs=host.in_specs(),
+        out_specs=host.out_specs(),
+        out_shape=host.out_shapes(),
+        scratch_shapes=host.scratch(),
+        compiler_params=pltpu.CompilerParams(
+            vmem_limit_bytes=VMEM_LIMIT, collective_id=collective_id, has_side_effects=True
+        ),
+    )(*host.views(arrays))
+
+
+MLP_SLOT = 2.4
+ATT_SLOT = 1.4
+
+
+def mlp_back_kernel(layer, host, ranges, *refs):
+    n = host.arrays
+    dy_ref, h_ref, wo_ref, vec_ref, u_ref, up0_ref, up1_ref, down0_ref, down1_ref = refs[:9]
+    srcs = refs[9 : 9 + n]
+    du_ref, gbup_ref, dh_ref, dr_ref, do_ref, sums_ref = refs[9 + n : 15 + n]
+    outs = refs[15 + n : 15 + 2 * n]
+    acc = refs[15 + 2 * n]
+    host.bind(srcs, outs, refs[16 + 2 * n :])
+    step = pl.program_id(0)
+    groups, _, width = do_ref.shape
+    unit = FF // shards_of() // 2
+    own = lax.axis_index("section") == layer
+
+    @pl.when(step == 0)
+    def _():
+        host.begin()
+        acc[...] = jnp.zeros_like(acc)
+
+    def part(up_ref, down_ref):
+        d_gated = mm_nt(dy_ref[...], down_ref[...])
+        upper = u_ref[...]
+        square = upper * upper
+        turn = jnp.tanh(GELU_A * upper * (1.0 + GELU_B * square))
+        slope = 0.5 * (1.0 + turn) + (0.5 * GELU_A) * upper * (1.0 - turn * turn) * (
+            1.0 + (3.0 * GELU_B) * square
+        )
+        d_upper = (d_gated * slope).astype(BF16)
+        put_halves(du_ref, d_upper, unit)
+        gbup_ref[...] = jnp.sum(d_upper.astype(F32), axis=0, keepdims=True)
+        acc[...] += mm_nt(d_upper, up_ref[...])
+
+    pl.when(own)(lambda: part(up0_ref, down0_ref))
+    pl.when(jnp.logical_not(own))(lambda: part(up1_ref, down1_ref))
+
+    for slot, (first, last) in enumerate(ranges[:-1]):
+        if last > first:
+            pl.when(step == slot)(functools.partial(host.run, first, last))
+
+    @pl.when(step == pl.num_programs(0) - 1)
+    def _():
+        normal, inverse = norm_stats(h_ref[...])
+        d_out = dy_ref[...].astype(F32)
+        d_normed = acc[...]
+        sums_ref[...] = jnp.zeros_like(sums_ref)
+        sums_ref[0:1, :] = jnp.sum(d_normed * normal, axis=0, keepdims=True)
+        sums_ref[1:2, :] = jnp.sum(d_normed, axis=0, keepdims=True)
+        d_normal = d_normed * vec_ref[1:2, :]
+        d_hidden = d_out + inverse * (
+            d_normal
+            - jnp.mean(d_normal, axis=-1, keepdims=True)
+            - normal * jnp.mean(d_normal * normal, axis=-1, keepdims=True)
+        )
+        dh_ref[...] = d_hidden
+        d_branch = d_hidden.astype(BF16)
+        dr_ref[...] = d_branch
+        sums_ref[2:3, :] = jnp.sum(d_branch.astype(F32), axis=0, keepdims=True)
+        sums_ref[3:4, :] = jnp.sum(d_out, axis=0, keepdims=True)
+        for group in range(groups):
+            do_ref[group] = mm_nt(
+                d_branch, wo_ref[group * width : (group + 1) * width, :]
+            ).astype(BF16)
+        host.run(*ranges[-1])
+        host.finish()
+
+
+def mlp_back_call(layer, dy, hidden, wo, vecs, upper, ups, downs, groups, host, arrays, total):
+    rows = dy.shape[0]
+    width = D // groups
+    whole = lambda i: (0, 0)
+    mine = lambda i, first: jnp.where((lax.axis_index("section") == layer) == first, i, 0)
+    col = lambda first: (lambda i: (0, mine(i, first)))
+    line = lambda first: (lambda i: (mine(i, first), 0))
+    chunk = lambda i: (0, i)
+    ranges = host.slots([MLP_SLOT * (i + 1) for i in range(NCH)], total)
+    return pl.pallas_call(
+        functools.partial(mlp_back_kernel, layer, host, ranges),
+        grid=(NCH,),
+        in_specs=[
+            pl.BlockSpec((rows, D), whole),
+            pl.BlockSpec((rows, D), whole),
+            pl.BlockSpec((D, D), whole),
+            pl.BlockSpec((8, D), whole),
+            pl.BlockSpec((rows, FC), chunk),
+            pl.BlockSpec((D, FC), col(True)),
+            pl.BlockSpec((D, FC), col(False)),
+            pl.BlockSpec((FC, D), line(True)),
+            pl.BlockSpec((FC, D), line(False)),
+        ]
+        + host.in_specs(),
+        out_specs=[
+            pl.BlockSpec((2, rows, FC // 2), lambda i: (0, 0, i)),
+            pl.BlockSpec((1, FC), chunk),
+            pl.BlockSpec((rows, D), whole),
+            pl.BlockSpec((rows, D), whole),
+            pl.BlockSpec((groups, rows, width), lambda i: (0, 0, 0)),
+            pl.BlockSpec((8, D), whole),
+        ]
+        + host.out_specs(),
+        scratch_shapes=[pltpu.VMEM((rows, D), F32)] + host.scratch(),
+        out_shape=[
+            jax.ShapeDtypeStruct((2, rows, FF // 2), BF16),
+            jax.ShapeDtypeStruct((1, FF), F32),
+            jax.ShapeDtypeStruct((rows, D), F32),
+            jax.ShapeDtypeStruct((rows, D), BF16),
+            jax.ShapeDtypeStruct((groups, rows, width), BF16),
+            jax.ShapeDtypeStruct((8, D), F32),
+        ]
+        + host.out_shapes(),
+        compiler_params=pltpu.CompilerParams(
+            vmem_limit_bytes=VMEM_LIMIT, collective_id=layer, has_side_effects=True
+        ),
+    )(dy, hidden, wo, vecs, upper, ups[0], ups[1], downs[0], downs[1], *host.views(arrays))
+
+
+def attend_back_kernel(host, ranges, *refs):
+    n = host.arrays
+    q_ref, do_ref, k_ref, v_ref, lse_ref, mask_ref = refs[:6]
+    srcs = refs[6 : 6 + n]
+    dj_ref, sums_ref = refs[6 + n : 8 + n]
+    outs = refs[8 + n : 8 + 2 * n]
+    dk_acc, dv_acc = refs[8 + 2 * n : 10 + 2 * n]
+    host.bind(srcs, outs, refs[10 + 2 * n :])
+    step = pl.program_id(0)
+    width = q_ref.shape[1]
+    heads = width // DH
+    scale = DH ** (-0.5)
+
+    @pl.when(step == 0)
+    def _():
+        host.begin()
+        dk_acc[...] = jnp.zeros_like(dk_acc)
+        dv_acc[...] = jnp.zeros_like(dv_acc)
+        sums_ref[...] = jnp.zeros_like(sums_ref)
+
+    q = q_ref[...]
+    grad = do_ref[...]
+    keys = k_ref[...]
+    values = v_ref[...]
+    mask = mask_ref[...]
+    totals = lse_ref[...]
+    d_q = jnp.zeros((BQ, width), F32)
+    for head in range(heads):
+        mine = head_lanes((BQ, width), head)
+        q_head = jnp.where(mine, q, jnp.zeros_like(q))
+        grad_head = jnp.where(mine, grad, jnp.zeros_like(grad))
+        scores = mm_nt(q_head, keys) * SCALE2 + mask
+        probs = jnp.exp2(scores - totals[:, head : head + 1])
+        d_probs = mm_nt(grad_head, values)
+        term = jnp.sum(probs * d_probs, axis=-1, keepdims=True)
+        d_scores = (probs * (d_probs - term)).astype(BF16)
+        dv_acc[...] += mm_tn(probs.astype(BF16), grad_head)
+        dk_acc[...] += mm_tn(d_scores, q_head)
+        d_q = jnp.where(mine, mm(d_scores, keys), d_q)
+        for slot, (first, last) in enumerate(ranges[:-1]):
+            if last > first and slot % heads == head:
+                pl.when(step == slot // heads)(functools.partial(host.run, first, last))
+    low = (d_q * scale).astype(BF16)
+    dj_ref[pl.ds(pl.multiple_of(step * BQ, BQ), BQ), :width] = low
+    sums_ref[0:1, :] += jnp.sum(low.astype(F32), axis=0, keepdims=True)
+
+    @pl.when(step == pl.num_programs(0) - 1)
+    def _():
+        dj_ref[:, width : 2 * width] = (dk_acc[...] * scale).astype(BF16)
+        low_v = dv_acc[...].astype(BF16)
+        dj_ref[:, 2 * width :] = low_v
+        sums_ref[1:2, :] = jnp.sum(low_v.astype(F32), axis=0, keepdims=True)
+        host.run(*ranges[-1])
+        host.finish()
+
+
+def attend_back_call(q, d_o, k, v, lse, mask, host, arrays, total, collective_id):
+    length, width = q.shape
+    row = lambda i: (i, 0)
+    whole = lambda i: (0, 0)
+    slots = length // BQ * (width // DH)
+    ranges = host.slots([ATT_SLOT * (i + 1) for i in range(slots)], total)
+    return pl.pallas_call(
+        functools.partial(attend_back_kernel, host, ranges),
+        grid=(length // BQ,),
+        in_specs=[
+            pl.BlockSpec((BQ, width), row),
+            pl.BlockSpec((BQ, width), row),
+            pl.BlockSpec((length, width), whole),
+            pl.BlockSpec((length, width), whole),
+            pl.BlockSpec((BQ, 128), row),
+            pl.BlockSpec((1, length), whole),
+        ]
+        + host.in_specs(),
+        out_specs=[
+            pl.BlockSpec((length, 3 * width), whole),
+            pl.BlockSpec((8, width), whole),
+        ]
+        + host.out_specs(),
+        out_shape=[
+            jax.ShapeDtypeStruct((length, 3 * width), BF16),
+            jax.ShapeDtypeStruct((8, width), F32),
+        ]
+        + host.out_shapes(),
+        scratch_shapes=[pltpu.VMEM((length, width), F32), pltpu.VMEM((length, width), F32)]
+        + host.scratch(),
+        compiler_params=pltpu.CompilerParams(
+            vmem_limit_bytes=VMEM_LIMIT, collective_id=collective_id, has_side_effects=True
+        ),
+    )(q, d_o, k, v, lse, mask, *host.views(arrays))
 
 
 def swap(value, axis, mask):
@@ -587,10 +939,50 @@
         size = FF if index == 8 else D
         return vector_pair[layer, index * D : index * D + size]
 
-    joint = w_qkv[0].reshape(D, 3, count, width)
-    joint_mine = take(joint, rank, 2).reshape(D, 3 * width)
-    joint_other = swap_core(take(joint, (1 - core) * half + low, 2).reshape(D, 3 * width))
-    out_other = swap_core(w_out[0])
+    compact = half == 2 and D // groups == DH
+    span = half * width
+
+    def joint_of(which):
+        wide = lax.dynamic_slice_in_dim(
+            w_qkv[0].reshape(D, 3, 2, span), which, 1, 2
+        ).reshape(D, 3, span)
+        source = jnp.arange(span)[:, None]
+        target = jnp.arange(width)[None, :]
+        if compact:
+            wanted = (2 * (target // DH) + low) * DH + target % DH
+        else:
+            wanted = low * width + target
+        pick = (source == wanted).astype(BF16)
+        return lax.dot_general(
+            wide, pick, (((2,), (0,)), ((), ())), preferred_element_type=F32
+        ).astype(BF16).reshape(D, 3 * width)
+
+    def vector_of(value):
+        wide = lax.dynamic_slice_in_dim(value, core * span, span)
+        if compact:
+            return take(wide.reshape(-1, 2, DH), low, 1).reshape(width)
+        return lax.dynamic_slice_in_dim(wide, low * width, width)
+
+    def vector_to(value):
+        if compact:
+            wide = jnp.stack(
+                [jnp.where(low == i, value.reshape(-1, DH), 0.0) for i in range(2)], axis=1
+            )
+        else:
+            wide = jnp.stack([jnp.where(low == i, value, 0.0) for i in range(half)], axis=0)
+        wide = wide.reshape(span)
+        return jnp.concatenate([jnp.where(core == i, wide, 0.0) for i in range(2)])
+
+    def rank_rows(value):
+        if compact:
+            value = value.reshape(2, width // DH, 2, DH, D)
+            return jnp.swapaxes(value, 1, 2).reshape(D, D)
+        return value
+
+    joint_mine = joint_of(core)
+    joint_other = swap_core(joint_of(1 - core))
+    out_mine = rank_rows(w_out[0])
+    out_other = swap_core(out_mine)
     up_other = swap_core(w_up[0])
     down_other = swap_core(w_down[0])
     ups = (w_up[0], up_other)
@@ -604,10 +996,9 @@
     for layer in range(2):
         sel = jnp.where(core == layer, 0, 1).astype(jnp.int32)[None]
         w_joint = jnp.where(core == layer, joint_mine, joint_other)
-        w_proj = jnp.where(core == layer, w_out[0], out_other)
+        w_proj = jnp.where(core == layer, out_mine, out_other)
         zero = jnp.zeros((width,), F32)
-        slice_of = lambda v: lax.dynamic_slice_in_dim(v, rank * width, width)
-        bias = jnp.concatenate([slice_of(vector(layer, 2)), zero, slice_of(vector(layer, 3))])
+        bias = jnp.concatenate([vector_of(vector(layer, 2)), zero, vector_of(vector(layer, 3))])
         vecs = jnp.concatenate(
             [
                 jnp.stack([vector(layer, 4), vector(layer, 5), vector(layer, 6), vector(layer, 7)]),
@@ -656,53 +1047,45 @@
             value = total.astype(value.dtype) if left else total
         return value
 
-    def reduce_parts(value, cuts):
-        outs = []
-        start = 0
-        for order, size in zip(orders, cuts):
-            if size:
-                outs.append(reduce_one(value[..., start : start + size], order))
-            start += size
-        return jnp.concatenate(outs, axis=-1)
-
-    def halves(value):
-        split = value.reshape(rows, groups, 2, FF // groups // 2)
-        mine = take(split, core, 2).reshape(rows, FF // 2)
-        return mine, take(split, 1 - core, 2).reshape(rows, FF // 2)
+    def both_halves(value):
+        return jnp.concatenate([take(value, core, 0), swap_core(take(value, 1 - core, 0))], axis=0)
 
     def joined(mine, other):
         return jnp.concatenate([mine, other], axis=0)
 
-    def give(value, layer):
-        return lax.ppermute(value, "section", [(1 - layer, layer)])
+    def hosted(*arrays):
+        shapes = []
+        for array in arrays:
+            shapes.append((array.shape[1], array.shape[2], array.shape[0] != groups))
+        return Hosted(dp_count, count, tuple(shapes)), arrays
 
     smalls = []
-    results = []
+    results = [{}, {}]
     grads_in = []
+    pending = None
     d_out = own_rows(cotangent)
     for layer in (1, 0):
-        sel, w_joint, w_proj, vecs, x_own, a1, q, k, v, lse, o_own, hidden, a2, upper, gated = saved[layer]
-        gated_mine, gated_send = halves(gated)
-        gated_all = joined(gated_mine, swap_core(gated_send))
+        _, w_joint, w_proj, vecs, x_own, a1, q, k, v, lse, o_own, hidden, a2, upper, gated = saved[layer]
+        gated_all = both_halves(gated)
         a2_all = joined(a2, swap_core(a2))
         d_out_all = joined(d_out, swap_core(d_out))
         g_down = mm_tn(d_out_all, gated_all).astype(BF16).reshape(groups, D // groups, FF // 2)
-        r_down = reduce_parts(g_down, (640, 640, 384, 384))
-        d_upper, g_bup, d_hidden, d_branch, d_heads, sums_two = mlp_back_call(
-            sel, d_out, hidden, w_proj, vecs, upper, ups, downs, count
-        )
-        upper_mine, upper_send = halves(d_upper)
-        upper_all = joined(upper_mine, swap_core(upper_send))
+        host, arrays = hosted(g_down) if pending is None else hosted(*pending)
+        d_upper, g_bup, d_hidden, d_branch, d_heads, sums_two, *reduced = mlp_back_call(
+            layer, d_out, hidden, w_proj, vecs, upper, ups, downs, count, host, arrays, 32.0
+        )
+        if pending is None:
+            results[layer]["down"] = reduced[0]
+        else:
+            results[1]["out"], results[1]["joint"] = reduced
+        upper_all = both_halves(d_upper)
         g_up = mm_tn(upper_all, a2_all).astype(BF16).reshape(groups, FF // groups // 2, D)
-        r_up = reduce_parts(g_up, (384, 384, 128, 128))
         d_mixed = exchange(d_heads).reshape(LEN, width)
-        o_split = o_own.reshape(2, half, rows, width)
-        flat = lambda t: jnp.swapaxes(t, 0, 1).reshape(rows, half * width)
-        o_all = joined(flat(take(o_split, core, 0)), swap_core(flat(take(o_split, 1 - core, 0))))
-        branch_all = joined(d_branch, swap_core(d_branch))
-        g_out = mm_tn(branch_all, o_all).astype(BF16).reshape(groups, D // groups, D // 2)
-        r_out = reduce_parts(g_out, (128, 128, 128, 128))
-        d_joint, sums_qv = attend_back_call(q, d_mixed, k, v, lse, bias_mask)
+        host, arrays = hosted(g_up) if pending is None else hosted(g_down)
+        d_joint, sums_qv, reduced = attend_back_call(
+            q, d_mixed, k, v, lse, bias_mask, host, arrays, 32.0, 2 + layer
+        )
+        results[layer]["up" if pending is None else "down"] = reduced
         d_normed = mm_nt(d_joint, w_joint).astype(BF16).reshape((2,) * (low_bits + 1) + (rows, D))
         other = swap_core(take(d_normed, 1 - core, 0))
         mine = take(d_normed, core, 0)
@@ -712,14 +1095,27 @@
             other = swap_seq(take(total, 1 - low_bit(bit), dim), bit)
             mine = take(total, low_bit(bit), dim)
         d_in, sums_one = norm_back_call(mine, other, x_own, d_hidden, vector(layer, 0)[None])
+        o_split = o_own.reshape(2, half, rows, width)
+        flat = lambda t: jnp.swapaxes(t, 0, 1).reshape(rows, half * width)
+        o_all = joined(flat(take(o_split, core, 0)), swap_core(flat(take(o_split, 1 - core, 0))))
+        branch_all = joined(d_branch, swap_core(d_branch))
+        g_out = mm_tn(branch_all, o_all).astype(BF16).reshape(groups, D // groups, D // 2)
         g_joint = mm_tn(d_joint, a1).astype(BF16).reshape(3, width, 2, D // 2)
         g_joint = ordered(core, take(g_joint, core, 2), swap_core(take(g_joint, 1 - core, 2)), 1)
-        spread = jnp.stack(
-            [jnp.where(low == i, g_joint, jnp.zeros_like(g_joint)) for i in range(half)], axis=2
-        )
-        r_joint = reduce_parts(spread.reshape(groups, 3 * D // groups, D // 2), (128, 128, 128, 128))
-        mine_at = jnp.zeros((2, count, width), F32)
-        mine_at = lax.dynamic_update_slice(mine_at, sums_qv[0:2, None, :], (0, rank, 0))
+        if compact:
+            g_joint = g_joint.reshape(groups // 2, 3 * D // groups, D // 2)
+        else:
+            spread = jnp.stack(
+                [jnp.where(low == i, g_joint, jnp.zeros_like(g_joint)) for i in range(half)], axis=2
+            )
+            g_joint = spread.reshape(groups, 3 * D // groups, D // 2)
+        if pending is None:
+            pending = (g_out, g_joint)
+        else:
+            host, arrays = hosted(g_up, g_out, g_joint)
+            results[layer]["up"], results[layer]["out"], results[layer]["joint"] = reduce_call(
+                host, arrays, 4
+            )
         smalls.append(
             jnp.concatenate(
                 [
@@ -727,8 +1123,8 @@
                     for piece in (
                         sums_one[0],
                         sums_one[1],
-                        mine_at[0].reshape(-1),
-                        mine_at[1].reshape(-1),
+                        vector_to(sums_qv[0]),
+                        vector_to(sums_qv[1]),
                         sums_two[2],
                         sums_two[0],
                         sums_two[1],
@@ -739,14 +1135,9 @@
                 axis=1,
             )
         )
-        parts = []
-        for piece in (r_down, r_out, r_joint, r_up):
-            parts.append((piece, give(piece, layer)))
-        results.append(parts)
         grads_in.append(d_in)
         d_out = d_in
 
-    results = results[::-1]
     grads_in = grads_in[::-1]
     small_pair = jnp.stack(smalls[::-1])
     small = take(small_pair, core, 0) + swap_core(take(small_pair, 1 - core, 0))
@@ -755,20 +1146,28 @@
     acts_rows = jnp.where(core == 0, to_section(acts[0], 0), to_section(acts[1], 1))
     grad_rows = jnp.where(core == 0, to_section(grads_in[0], 0), to_section(grads_in[1], 1))
 
-    def choose(index):
-        first = jnp.where(core == 0, results[0][index][0], results[1][index][1])
-        second = jnp.where(core == 0, results[0][index][1], results[1][index][0])
-        return first, second
-
-    down_0, down_1 = choose(0)
-    d_down = jnp.stack([down_0.reshape(-1, groups, FF // groups // 2), down_1.reshape(-1, groups, FF // groups // 2)], axis=2)
-    g_w_down = d_down.reshape(-1, FF).T
-    out_0, out_1 = choose(1)
-    g_w_out = jnp.concatenate([out_0, out_1], axis=1).T
-    joint_0, joint_1 = choose(2)
-    g_w_qkv = jnp.concatenate([joint_0, joint_1], axis=1).T
-    up_0, up_1 = choose(3)
-    g_w_up = jnp.concatenate([up_0, up_1], axis=0).T
+    def choose(name):
+        return jnp.where(core == 0, results[0][name], results[1][name])
+
+    r_down = choose("down").reshape(2, D // groups, groups, FF // groups // 2)
+    g_w_down = jnp.transpose(r_down, (2, 0, 3, 1)).reshape(FF, D // groups)
+    r_out = choose("out")
+    if compact:
+        r_out = r_out.reshape(2, D // groups, 2, width // DH, DH)
+        g_w_out = jnp.transpose(r_out, (0, 3, 2, 4, 1)).reshape(D, D // groups)
+    else:
+        g_w_out = jnp.swapaxes(r_out, 1, 2).reshape(D, D // groups)
+    r_joint = choose("joint")
+    if compact:
+        r_joint = r_joint.reshape(2, 4, DH, D // 2)
+        r_joint = jnp.where(
+            low == 0,
+            jnp.stack([r_joint[:, 0], r_joint[:, 3], r_joint[:, 1]], axis=1),
+            jnp.stack([r_joint[:, 1], r_joint[:, 3], r_joint[:, 2]], axis=1),
+        ).reshape(2, 3 * DH, D // 2)
+    g_w_qkv = jnp.swapaxes(r_joint, 1, 2).reshape(D, 3 * D // groups)
+    r_up = choose("up")
+    g_w_up = jnp.transpose(r_up, (2, 0, 1)).reshape(D, FF // groups)
 
     unit = D // groups
     pieces = []

time: 1220 us -> 735 us (0.60)
  waiting for transfers between devices: 399 us -> 76 us
  starting transfers between devices: 321 us -> 57.3 us
  Pallas kernels: 183 us -> 382 us
  local copies, waits for them, and re-layouts: 191 us -> 110 us
  other arithmetic: 73.4 us -> 44.2 us
  matrix products: 39.9 us -> 52.7 us
    ppermute x168 -> x40, waiting for transfers between devices: 397 us -> 63 us  [swap(): return lax.ppermute(value, axis, [(i, i ^ mask) for i in range(count)])]
    ppermute x168 -> x40, starting transfers between devices: 243 us -> 33.4 us  [swap(): return lax.ppermute(value, axis, [(i, i ^ mask) for i in range(count)])]
    pallas_call x4 -> x5, Pallas kernels: 95.5 us -> 295 us  [the longest x2 113 us: attend_back_call(): pl.pallas_call(functools.partial(attend_back_kernel, host, ranges), grid=...]
    dynamic_slice x61 -> x22, local copies, waits for them, and re-layouts: 87 us -> 15.3 us  [take(): return lax.dynamic_index_in_dim(value, index, dim, keepdims=False)]
    ppermute x8 -> x0, starting transfers between devices: 49.1 us -> none  [give(): return lax.ppermute(value, 'section', [(1 - layer, layer)])]
    unnamed x245 -> x137, local copies, waits for them, and re-layouts: 35 us -> 11.3 us
    another operation x8 -> x7, local copies, waits for them, and re-layouts: 3.29 us -> 22.7 us  [the longest x1 15 us: joint_of(): w_qkv[0].reshape(D, 3, 2, span)]
    dynamic_slice x2 -> x5, local copies, waits for them, and re-layouts: 0.01 us -> 16.3 us  [the longest x1 15.6 us: joint_of(): lax.dynamic_slice_in_dim(w_qkv[0].reshape(D, 3, 2, span), which, 1, 2)]
  transfers between devices with their start and end apart: 184 -> 48, of which waited for: 121 -> 14; matrix products, arithmetic and copies ran while one was open for 24% -> 24% of each run, Pallas kernels for 14% -> 32%
where the time goes in v2:
time: 735 us; the launch traced here: 724 us
  Pallas kernels  382 us (52%)
  local copies, waits for them, and re-layouts  110 us (15%)
  waiting for transfers between devices  76 us (10%)
  starting transfers between devices  57.3 us (8%)
  matrix products  52.7 us (7%)
  other arithmetic  44.2 us (6%)
    pallas_call x2, Pallas kernels, attend_back_call(): pl.pallas_call(functools.partial(attend_back_kernel, host, ranges), grid=...  113 us
    pallas_call x2, Pallas kernels, mlp_back_call(): pl.pallas_call(functools.partial(mlp_back_kernel, layer, host, ranges), g...  105 us
    pallas_call x1, Pallas kernels, reduce_call(): pl.pallas_call(functools.partial(reduce_kernel, host), in_specs=host.in_s...  76.7 us
    ppermute x40, waiting for transfers between devices, swap(): return lax.ppermute(value, axis, [(i, i ^ mask) for i in range(count)])  63 us
    dot_general x8, matrix products, mm_tn(): lax.dot_general(a, b, (((0,), (0,)), ((), ())), preferred_element_type=F32)  39.1 us
    pallas_call x2, Pallas kernels, mlp_call(): pl.pallas_call(mlp_kernel, grid_spec=pltpu.PrefetchScalarGridSpec(num_sca...  36.3 us
    ppermute x40, starting transfers between devices, swap(): return lax.ppermute(value, axis, [(i, i ^ mask) for i in range(count)])  33.4 us
    pallas_call x2, Pallas kernels, attend_call(): pl.pallas_call(attend_kernel, grid=(length // BQ,), in_specs=[pl.BlockSpe...  28.7 us
  transfers between devices with their start and end apart: 48, of which 14 were waited for; matrix products, arithmetic and copies ran while one was open for 24% of the time, Pallas kernels for 32%

profile of v2, /device:TPU:9, one launch (start us, length us, event | category | flops | bytes accessed | tf_op | source)
XLA Modules:
  0.0 724.5 jit_solution(2654454269333911439)
XLA Ops:
  1.5 15.0 %reshape_squeeze.57 = bf16[1024,3,2,512]{3,2,1,0:T(2,128)(2,1)} reshape(bf16[1,1024,3072]{2,1,0:T(8,128)(2,1)} %param.21) | data formatting | bytes 12582912 | tf_op jit(solution)/shard_map/reshape;squeeze | solution.py:947
  16.4 15.6 %constant_dynamic-slice_fusion.31 = (bf16[1024,3,1,512]{3,2,1,0:T(2,128)(2,1)}, bf16[1024,3,1,512]{3,2,1,0:T(2,128)(2,1)}) fusion(bf16[1024,3,2,512]{3,2,1,0:T(2,128)(2,1)} %reshape_squeeze.57, s32[]{:T(128)S(6)} %select_n.729, s32[]{:T(128)S(6)} %select_n.725), kind=kLoop, calls=%fused_computation.175 | loop fusion | bytes 12582920 | tf_op jit(solution)/shard_map/dynamic_slice | solution.py:946
  38.0 4.2 collective-permute-start
  47.4 9.3 %collective-permute-done = bf16[320,1024]{1,0:T(8,128)(2,1)S(1)} collective-permute-done((bf16[320,1024]{1,0:T(8,128)(2,1)S(1)}, bf16[320,1024]{1,0:T(8,128)(2,1)S(1)}, u32[]{:S(2)}, u32[]{:S(2)}) %collective-permute-start) | collective-permute-done | bytes 655392 | tf_op jit(solution)/shard_map/ppermute | solution.py:890
  85.5 7.2 shard_map.271
  92.7 14.3 %shard_map.272 = (bf16[1280,256]{1,0:T(8,128)(2,1)}, f32[1280,128]{1,0:T(8,128)}) custom-call(bf16[1280,256]{1,0:T(8,128)(2,1)} %get-tuple-element.65.q_ref.refs_0_, bf16[1280,256]{1,0:T(8,128)(2,1)} %get-tuple-element.66.k_ref.refs_2_, bf16[1280,256]{1,0:T(8,128)(2,1)} %get-tuple-element.67.v_ref.refs_3_, f32[1,1280]{1,0:T(1,128)} %or_select_fusion.mask_ref.refs_5_), custom_call_target="tpu_custom_call" | custom-call | flops 6710886400 | bytes 4194304 | tf_op jit(solution)/shard_map/pallas_call | solution.py:121
  111.3 6.8 collective-permute-done.5
  118.9 3.9 broadcast_select_fusion
  123.7 17.8 %shard_map.273 = (f32[320,1024]{1,0:T(8,128)}, bf16[320,1024]{1,0:T(8,128)(2,1)}, f32[320,4096]{1,0:T(8,128)}, bf16[2,320,2048]{2,1,0:T(8,128)(2,1)}, bf16[320,1024]{1,0:T(8,128)(2,1)}) custom-call(s32[1]{0:T(128)} %bitcast.sel_ref, bf16[4,320,256]{2,1,0:T(8,128)(2,1)} %bitcast.273, bf16[320,1024]{1,0:T(8,128)(2,1)} %copy-done.2, ...), custom_call_target="tpu_custom_call" | custom-call | flops 6039797760 | bytes 31457280 | tf_op jit(solution)/shard_map/pallas_call | solution.py:212
  143.1 14.4 %collective-permute-done.11 = bf16[1,320,1024]{2,1,0:T(8,128)(2,1)S(1)} collective-permute-done((bf16[1,320,1024]{2,1,0:T(8,128)(2,1)}, bf16[1,320,1024]{2,1,0:T(8,128)(2,1)S(1)}, u32[]{:S(2)}, u32[]{:S(2)}) %collective-permute-start.11) | collective-permute-done | bytes 655392 | tf_op jit(solution)/shard_map/ppermute | solution.py:820
  164.9 7.2 shard_map.274
  172.1 14.4 %shard_map.275 = (bf16[1280,256]{1,0:T(8,128)(2,1)}, f32[1280,128]{1,0:T(8,128)}) custom-call(bf16[1280,256]{1,0:T(8,128)(2,1)} %get-tuple-element.70.q_ref.refs_0_, bf16[1280,256]{1,0:T(8,128)(2,1)} %get-tuple-element.71.k_ref.refs_2_, bf16[1280,256]{1,0:T(8,128)(2,1)} %get-tuple-element.72.v_ref.refs_3_, f32[1,1280]{1,0:T(1,128)} %or_select_fusion.mask_ref.refs_5_), custom_call_target="tpu_custom_call" | custom-call | flops 6710886400 | bytes 4194304 | tf_op jit(solution)/shard_map/pallas_call | solution.py:121
  189.2 7.5 %collective-permute-done.13 = bf16[2,320,256]{2,1,0:T(8,128)(2,1)S(1)} collective-permute-done((bf16[2,320,256]{2,1,0:T(8,128)(2,1)S(1)}, bf16[2,320,256]{2,1,0:T(8,128)(2,1)S(1)}, u32[]{:S(2)}, u32[]{:S(2)}) %collective-permute-start.13) | collective-permute-done | bytes 327712 | tf_op jit(solution)/shard_map/ppermute | solution.py:820
  198.1 4.4 collective-permute-start.17
  205.2 18.4 %shard_map.276 = (f32[320,1024]{1,0:T(8,128)}, bf16[320,1024]{1,0:T(8,128)(2,1)}, f32[320,4096]{1,0:T(8,128)}, bf16[2,320,2048]{2,1,0:T(8,128)(2,1)}, bf16[320,1024]{1,0:T(8,128)(2,1)}) custom-call(s32[1]{0:T(128)} %bitcast.30.sel_ref, bf16[4,320,256]{2,1,0:T(8,128)(2,1)} %bitcast.274, bf16[320,1024]{1,0:T(8,128)(2,1)} %get-tuple-element.69.x_ref, ...), custom_call_target="tpu_custom_call" | custom-call | flops 6039797760 | bytes 31457280 | tf_op jit(solution)/shard_map/pallas_call | solution.py:212
  229.7 5.1 convolution_convert_fusion.5
  234.8 52.0 %shard_map.277 = (bf16[2,320,2048]{2,1,0:T(8,128)(2,1)}, f32[1,4096]{1,0:T(1,128)}, f32[320,1024]{1,0:T(8,128)}, bf16[320,1024]{1,0:T(8,128)(2,1)}, bf16[4,320,2...) custom-call(bf16[320,1024]{1,0:T(8,128)(2,1)} %copy-done.17, f32[320,1024]{1,0:T(8,128)} %get-tuple-element.75.refs_1_, ...), custom_call_target="tpu_custom_call" | custom-call | tf_op jit(solution)/shard_map/pallas_call | solution.py:686
  291.9 7.2 collective-permute-done.20
  303.5 7.2 convolution_convert_fusion.4
  310.7 60.4 %shard_map.278 = (bf16[1280,768]{1,0:T(8,128)(2,1)}, f32[8,256]{1,0:T(8,128)}, f32[2,128,1024]{2,1,0:T(8,128)}) custom-call(bf16[1280,256]{1,0:T(8,128)(2,1)} %get-tuple-element.70.q_ref.refs_0_, bf16[1280,256]{1,0:T(8,128)(2,1)} %bitcast.288, bf16[1280,256]{1,0:T(8,128)(2,1)} %get-tuple-element.71.k_ref.refs_2_, ...), custom_call_target="tpu_custom_call" | custom-call | tf_op jit(solution)/shard_map/pallas_call | solution.py:788
  384.5 4.9 collective-permute-start.16
  398.2 4.4 constant_dynamic-slice_fusion.12
  428.7 3.9 shard_map.279
  432.6 53.5 %shard_map.280 = (bf16[2,320,2048]{2,1,0:T(8,128)(2,1)}, f32[1,4096]{1,0:T(1,128)}, f32[320,1024]{1,0:T(8,128)}, bf16[320,1024]{1,0:T(8,128)(2,1)}, bf16[4,320,2...) custom-call(bf16[320,1024]{1,0:T(8,128)(2,1)} %get-tuple-element.84.refs_0_, ...), custom_call_target="tpu_custom_call" | custom-call | tf_op jit(solution)/shard_map/pallas_call | solution.py:686
  488.6 7.9 %collective-permute-done.29 = bf16[2,320,256]{2,1,0:T(8,128)(2,1)S(1)} collective-permute-done((bf16[2,320,256]{2,1,0:T(8,128)(2,1)S(1)}, bf16[2,320,256]{2,1,0:T(8,128)(2,1)S(1)}, u32[]{:S(2)}, u32[]{:S(2)}) %collective-permute-start.29) | collective-permute-done | bytes 327712 | tf_op jit(solution)/shard_map/ppermute | solution.py:820
  505.3 7.2 convolution_convert_fusion.2
  512.5 52.4 %shard_map.281 = (bf16[1280,768]{1,0:T(8,128)(2,1)}, f32[8,256]{1,0:T(8,128)}, f32[2,64,2048]{2,1,0:T(8,128)}) custom-call(bf16[1280,256]{1,0:T(8,128)(2,1)} %get-tuple-element.65.q_ref.refs_0_, bf16[1280,256]{1,0:T(8,128)(2,1)} %bitcast.287, bf16[1280,256]{1,0:T(8,128)(2,1)} %get-tuple-element.66.k_ref.refs_2_, ...), custom_call_target="tpu_custom_call" | custom-call | tf_op jit(solution)/shard_map/pallas_call | solution.py:788
  577.1 4.4 constant_dynamic-slice_fusion
  602.7 6.9 convolution_convert_fusion
  611.2 76.7 %shard_map.283 = (f32[2,128,1024]{2,1,0:T(8,128)}, f32[2,64,512]{2,1,0:T(8,128)}, f32[2,256,512]{2,1,0:T(8,128)}) custom-call(bf16[2,2,2,2,128,1024]{5,4,3,2,1,0:T(8,128)(2,1)} %bitcast.282, bf16[2,2,2,2,64,512]{5,4,3,2,1,0:T(8,128)(2,1)} %bitcast.307, bf16[2,2,2,192,512]{4,3,2,1,0:T(8,128)(2,1)} %bitcast.272), custom_call_target="tpu_custom_call" | custom-call | tf_op jit(solution)/shard_map/pallas_call | solution.py:596
  688.8 3.9 shard_map.282
  704.7 8.2 %collective-permute-done.41 = f32[2,768]{1,0:T(2,128)S(1)} collective-permute-done((f32[2,768]{1,0:T(2,128)S(1)}, f32[2,768]{1,0:T(2,128)S(1)}, u32[]{:S(2)}, u32[]{:S(2)}) %collective-permute-start.41) | collective-permute-done | bytes 6176 | tf_op jit(solution)/shard_map/ppermute | solution.py:820
  (393 shorter events, 195.8 us)
Async XLA Ops:
  0.7 123.0 %collective-permute-start.8 = (bf16[1024,4096]{1,0:T(8,128)(2,1)}, bf16[1024,4096]{1,0:T(8,128)(2,1)}, u32[]{:S(2)}, u32[]{:S(2)}) collective-permute-start(bf16[1024,4096]{1,0:T(8,128)(2,1)} %bitcast.253), channel_id=1, source_target_pairs={{0,16},{16,0},{1,17},{17,1},{2,18},{18,2},{3,19},{19,3},{4,20},{20... | collective-permute-start | bytes 25165832 | tf_op jit(solution)/shard_map/ppermute | solution.py:820
  1.4 122.3 %collective-permute-start.9 = (bf16[4096,1024]{1,0:T(8,128)(2,1)}, bf16[4096,1024]{1,0:T(8,128)(2,1)}, u32[]{:S(2)}, u32[]{:S(2)}) collective-permute-start(bf16[4096,1024]{1,0:T(8,128)(2,1)} %bitcast.258), channel_id=1, source_target_pairs={{0,16},{16,0},{1,17},{17,1},{2,18},{18,2},{3,19},{19,3},{4,20},{20... | collective-permute-start | bytes 25165832 | tf_op jit(solution)/shard_map/ppermute | solution.py:820
  37.5 41.1 %collective-permute-start.3 = (bf16[1024,768]{1,0:T(8,128)(2,1)}, bf16[1024,768]{1,0:T(8,128)(2,1)}, u32[]{:S(2)}, u32[]{:S(2)}) collective-permute-start(bf16[1024,768]{1,0:T(8,128)(2,1)} %copy.70), channel_id=1, source_target_pairs={{0,16},{16,0},{1,17},{17,1},{2,18},{18,2},{3,19},{19,3},{4,20},{20... | collective-permute-start | bytes 4718600 | tf_op jit(solution)/shard_map/ppermute | solution.py:820
  38.0 18.7 %collective-permute-start = (bf16[320,1024]{1,0:T(8,128)(2,1)S(1)}, bf16[320,1024]{1,0:T(8,128)(2,1)S(1)}, u32[]{:S(2)}, u32[]{:S(2)}) collective-permute-start(bf16[320,1024]{1,0:T(8,128)(2,1)S(1)} %dynamic-slice_bitcast_fusion.15), channel_id=1, source_target_pairs={{16,18},{17,19},{18,16},{19,17},{20,22},{21,23},{22,20},{23,21},{2... | collective-permute-start | bytes 1966088 | tf_op jit(solution)/shard_map/ppermute | solution.py:890
  47.4 22.9 %collective-permute-start.4 = (f32[12288]{0:T(1024)}, f32[12288]{0:T(1024)}, u32[]{:S(2)}, u32[]{:S(2)}) collective-permute-start(f32[12288]{0:T(1024)} %concatenate.173), channel_id=1, source_target_pairs={{0,16},{16,0},{1,17},{17,1},{2,18},{18,2},{3,19},{19,3},{4,20},{20... | collective-permute-start | bytes 147464 | tf_op jit(solution)/shard_map/ppermute | solution.py:820
  56.8 12.3 %collective-permute-start.1 = (bf16[1,320,1024]{2,1,0:T(8,128)(2,1)S(1)}, bf16[1,320,1024]{2,1,0:T(8,128)(2,1)S(1)}, u32[]{:S(2)}, u32[]{:S(2)}) collective-permute-start(bf16[1,320,1024]{2,1,0:T(8,128)(2,1)S(1)} %bitcast.263), channel_id=1, source_target_pairs={{0,1},{1,0},{2,3},{3,2},{4,5},{5,4},{6,7},{7,6},{8,9},{9,8},{10,11... | collective-permute-start | bytes 1966088 | tf_op jit(solution)/shard_map/ppermute | solution.py:820
  69.1 49.8 %collective-permute-start.7 = (bf16[1024,1024]{1,0:T(8,128)(2,1)S(1)}, bf16[1024,1024]{1,0:T(8,128)(2,1)}, u32[]{:S(2)}, u32[]{:S(2)}) collective-permute-start(bf16[1024,1024]{1,0:T(8,128)(2,1)S(1)} %bitcast.270), channel_id=1, source_target_pairs={{0,16},{16,0},{1,17},{17,1},{2,18},{18,2},{3,19},{19,3},{4,20},{20... | collective-permute-start | bytes 6291464 | tf_op jit(solution)/shard_map/ppermute | solution.py:820
  70.3 11.7 %collective-permute-start.2 = (bf16[2,320,1024]{2,1,0:T(8,128)(2,1)}, bf16[2,320,1024]{2,1,0:T(8,128)(2,1)}, u32[]{:S(2)}, u32[]{:S(2)}) collective-permute-start(bf16[2,320,1024]{2,1,0:T(8,128)(2,1)} %maximum_select_fusion.5), channel_id=1, source_target_pairs={{0,16},{16,0},{1,17},{17,1},{2,18},{18,2},{3,19},{19,3},{4,20},{20... | collective-permute-start | bytes 3932168 | tf_op jit(solution)/shard_map/ppermute | solution.py:820
  141.5 16.0 %collective-permute-start.11 = (bf16[1,320,1024]{2,1,0:T(8,128)(2,1)}, bf16[1,320,1024]{2,1,0:T(8,128)(2,1)S(1)}, u32[]{:S(2)}, u32[]{:S(2)}) collective-permute-start(bf16[1,320,1024]{2,1,0:T(8,128)(2,1)} %bitcast.266), channel_id=1, source_target_pairs={{0,1},{1,0},{2,3},{3,2},{4,5},{5,4},{6,7},{7,6},{8,9},{9,8},{10,11... | collective-permute-start | bytes 1966088 | tf_op jit(solution)/shard_map/ppermute | solution.py:820
  198.1 27.7 %collective-permute-start.17 = (bf16[320,1024]{1,0:T(8,128)(2,1)S(1)}, bf16[320,1024]{1,0:T(8,128)(2,1)S(1)}, u32[]{:S(2)}, u32[]{:S(2)}) collective-permute-start(bf16[320,1024]{1,0:T(8,128)(2,1)S(1)} %dynamic-slice_bitcast_fusion.14), channel_id=1, source_target_pairs={{16,18},{17,19},{18,16},{19,17},{20,22},{21,23},{22,20},{23,21},{2... | collective-permute-start | bytes 1966088 | tf_op jit(solution)/shard_map/ppermute | solution.py:890
  288.8 14.7 %collective-permute-start.22 = (bf16[320,2048]{1,0:T(8,128)(2,1)S(1)}, bf16[320,2048]{1,0:T(8,128)(2,1)}, u32[]{:S(2)}, u32[]{:S(2)}) collective-permute-start(bf16[320,2048]{1,0:T(8,128)(2,1)S(1)} %get-tuple-element.193), channel_id=1, source_target_pairs={{0,16},{16,0},{1,17},{17,1},{2,18},{18,2},{3,19},{19,3},{4,20},{20... | collective-permute-start | bytes 3932168 | tf_op jit(solution)/shard_map/ppermute | solution.py:820
  291.2 12.3 %collective-permute-start.23 = (bf16[320,1024]{1,0:T(8,128)(2,1)}, bf16[320,1024]{1,0:T(8,128)(2,1)}, u32[]{:S(2)}, u32[]{:S(2)}) collective-permute-start(bf16[320,1024]{1,0:T(8,128)(2,1)} %get-tuple-element.81), channel_id=1, source_target_pairs={{0,16},{16,0},{1,17},{17,1},{2,18},{18,2},{3,19},{19,3},{4,20},{20... | collective-permute-start | bytes 1966088 | tf_op jit(solution)/shard_map/ppermute | solution.py:820
  376.1 26.7 %collective-permute-start.24 = (bf16[2,320,1024]{2,1,0:T(8,128)(2,1)}, bf16[2,320,1024]{2,1,0:T(8,128)(2,1)S(1)}, u32[]{:S(2)}, u32[]{:S(2)}) collective-permute-start(bf16[2,320,1024]{2,1,0:T(8,128)(2,1)} %dynamic-slice_bitcast_fusion.5), channel_id=1, source_target_pairs={{0,16},{16,0},{1,17},{17,1},{2,18},{18,2},{3,19},{19,3},{4,20},{20... | collective-permute-start | bytes 3932168 | tf_op jit(solution)/shard_map/ppermute | solution.py:820
  379.1 25.8 %collective-permute-start.10 = (bf16[320,1024]{1,0:T(8,128)(2,1)S(1)}, bf16[320,1024]{1,0:T(8,128)(2,1)}, u32[]{:S(2)}, u32[]{:S(2)}) collective-permute-start(bf16[320,1024]{1,0:T(8,128)(2,1)S(1)} %copy-done.4), channel_id=1, source_target_pairs={{16,2},{17,3},{18,0},{19,1},{20,6},{21,7},{22,4},{23,5},{24,10},{2... | collective-permute-start | bytes 1966088 | tf_op jit(solution)/shard_map/ppermute | solution.py:923
  383.1 21.8 %collective-permute-start.15 = (bf16[320,1024]{1,0:T(8,128)(2,1)}, bf16[320,1024]{1,0:T(8,128)(2,1)}, u32[]{:S(2)}, u32[]{:S(2)}) collective-permute-start(bf16[320,1024]{1,0:T(8,128)(2,1)} %get-tuple-element.74), channel_id=1, source_target_pairs={{0,16},{1,17},{2,18},{3,19},{4,20},{5,21},{6,22},{7,23},{8,24},{9,... | collective-permute-start | bytes 1966088 | tf_op jit(solution)/shard_map/ppermute | solution.py:920
  384.5 24.6 %collective-permute-start.16 = (bf16[320,1024]{1,0:T(8,128)(2,1)}, bf16[320,1024]{1,0:T(8,128)(2,1)}, u32[]{:S(2)}, u32[]{:S(2)}) collective-permute-start(bf16[320,1024]{1,0:T(8,128)(2,1)} %get-tuple-element.74), channel_id=1, source_target_pairs={{16,18},{17,19},{18,16},{19,17},{20,22},{21,23},{22,20},{23,21},{2... | collective-permute-start | bytes 1966088 | tf_op jit(solution)/shard_map/ppermute | solution.py:923
  391.7 27.7 %collective-permute-start.26 = (bf16[320,1024]{1,0:T(8,128)(2,1)}, bf16[320,1024]{1,0:T(8,128)(2,1)}, u32[]{:S(2)}, u32[]{:S(2)}) collective-permute-start(bf16[320,1024]{1,0:T(8,128)(2,1)} %get-tuple-element.87), channel_id=1, source_target_pairs={{0,16},{16,0},{1,17},{17,1},{2,18},{18,2},{3,19},{19,3},{4,20},{20... | collective-permute-start | bytes 1966088 | tf_op jit(solution)/shard_map/ppermute | solution.py:820
  402.8 22.0 %collective-permute-start.28 = (bf16[3,256,512]{2,1,0:T(8,128)(2,1)S(1)}, bf16[3,256,512]{2,1,0:T(8,128)(2,1)}, u32[]{:S(2)}, u32[]{:S(2)}) collective-permute-start(bf16[3,256,512]{2,1,0:T(8,128)(2,1)S(1)} %bitcast.308), channel_id=1, source_target_pairs={{0,16},{16,0},{1,17},{17,1},{2,18},{18,2},{3,19},{19,3},{4,20},{20... | collective-permute-start | bytes 2359304 | tf_op jit(solution)/shard_map/ppermute | solution.py:820
  404.9 184.0 %collective-permute-start.46 = (bf16[320,512]{1,0:T(8,128)(2,1)}, bf16[320,512]{1,0:T(8,128)(2,1)}, u32[]{:S(2)}, u32[]{:S(2)}) collective-permute-start(bf16[320,512]{1,0:T(8,128)(2,1)} %bitcast.158), channel_id=1, source_target_pairs={{0,16},{16,0},{1,17},{17,1},{2,18},{18,2},{3,19},{19,3},{4,20},{20... | collective-permute-start | bytes 983048 | tf_op jit(solution)/shard_map/ppermute | solution.py:820
  404.9 14.5 %collective-permute-start.27 = (bf16[320,512]{1,0:T(8,128)(2,1)S(1)}, bf16[320,512]{1,0:T(8,128)(2,1)}, u32[]{:S(2)}, u32[]{:S(2)}) collective-permute-start(bf16[320,512]{1,0:T(8,128)(2,1)S(1)} %bitcast.323), channel_id=1, source_target_pairs={{0,16},{16,0},{1,17},{17,1},{2,18},{18,2},{3,19},{19,3},{4,20},{20... | collective-permute-start | bytes 983048 | tf_op jit(solution)/shard_map/ppermute | solution.py:820
  409.1 18.7 %collective-permute-start.25 = (bf16[320,1024]{1,0:T(8,128)(2,1)S(1)}, bf16[320,1024]{1,0:T(8,128)(2,1)S(1)}, u32[]{:S(2)}, u32[]{:S(2)}) collective-permute-start(bf16[320,1024]{1,0:T(8,128)(2,1)S(1)} %get-tuple-element.202), channel_id=1, source_target_pairs={{0,1},{1,0},{2,3},{3,2},{4,5},{5,4},{6,7},{7,6},{8,9},{9,8},{10,11... | collective-permute-start | bytes 1966088 | tf_op jit(solution)/shard_map/ppermute | solution.py:820
  419.5 85.4 %collective-permute-start.32 = (bf16[320,2048]{1,0:T(8,128)(2,1)}, bf16[320,2048]{1,0:T(8,128)(2,1)}, u32[]{:S(2)}, u32[]{:S(2)}) collective-permute-start(bf16[320,2048]{1,0:T(8,128)(2,1)} %get-tuple-element.191), channel_id=1, source_target_pairs={{0,16},{16,0},{1,17},{17,1},{2,18},{18,2},{3,19},{19,3},{4,20},{20... | collective-permute-start | bytes 3932168 | tf_op jit(solution)/shard_map/ppermute | solution.py:820
  419.5 180.6 %collective-permute-start.44 = (bf16[320,1024]{1,0:T(8,128)(2,1)}, bf16[320,1024]{1,0:T(8,128)(2,1)}, u32[]{:S(2)}, u32[]{:S(2)}) collective-permute-start(bf16[320,1024]{1,0:T(8,128)(2,1)} %get-tuple-element.104), channel_id=1, source_target_pairs={{0,16},{16,0},{1,17},{17,1},{2,18},{18,2},{3,19},{19,3},{4,20},{20... | collective-permute-start | bytes 1966088 | tf_op jit(solution)/shard_map/ppermute | solution.py:820
  487.4 17.9 %collective-permute-start.31 = (bf16[320,1024]{1,0:T(8,128)(2,1)}, bf16[320,1024]{1,0:T(8,128)(2,1)}, u32[]{:S(2)}, u32[]{:S(2)}) collective-permute-start(bf16[320,1024]{1,0:T(8,128)(2,1)} %get-tuple-element.84.refs_0_), channel_id=1, source_target_pairs={{0,16},{16,0},{1,17},{17,1},{2,18},{18,2},{3,19},{19,3},{4,20},{20... | collective-permute-start | bytes 1966088 | tf_op jit(solution)/shard_map/ppermute | solution.py:820
  503.9 86.3 %collective-permute-start.45 = (bf16[320,1024]{1,0:T(8,128)(2,1)}, bf16[320,1024]{1,0:T(8,128)(2,1)}, u32[]{:S(2)}, u32[]{:S(2)}) collective-permute-start(bf16[320,1024]{1,0:T(8,128)(2,1)} %get-tuple-element.105), channel_id=1, source_target_pairs={{0,16},{16,0},{1,17},{17,1},{2,18},{18,2},{3,19},{19,3},{4,20},{20... | collective-permute-start | bytes 1966088 | tf_op jit(solution)/shard_map/ppermute | solution.py:820
  504.8 97.8 %collective-permute-start.43 = (bf16[320,2048]{1,0:T(8,128)(2,1)}, bf16[320,2048]{1,0:T(8,128)(2,1)}, u32[]{:S(2)}, u32[]{:S(2)}) collective-permute-start(bf16[320,2048]{1,0:T(8,128)(2,1)} %get-tuple-element.189), channel_id=1, source_target_pairs={{0,16},{16,0},{1,17},{17,1},{2,18},{18,2},{3,19},{19,3},{4,20},{20... | collective-permute-start | bytes 3932168 | tf_op jit(solution)/shard_map/ppermute | solution.py:820
  570.4 25.4 %collective-permute-start.33 = (bf16[2,320,1024]{2,1,0:T(8,128)(2,1)}, bf16[2,320,1024]{2,1,0:T(8,128)(2,1)}, u32[]{:S(2)}, u32[]{:S(2)}) collective-permute-start(bf16[2,320,1024]{2,1,0:T(8,128)(2,1)} %dynamic-slice_bitcast_fusion.2), channel_id=1, source_target_pairs={{0,16},{16,0},{1,17},{17,1},{2,18},{18,2},{3,19},{19,3},{4,20},{20... | collective-permute-start | bytes 3932168 | tf_op jit(solution)/shard_map/ppermute | solution.py:820
  588.9 132.2 %collective-permute-start.36 = (bf16[320,1024]{1,0:T(8,128)(2,1)}, bf16[320,1024]{1,0:T(8,128)(2,1)}, u32[]{:S(2)}, u32[]{:S(2)}) collective-permute-start(bf16[320,1024]{1,0:T(8,128)(2,1)} %get-tuple-element.84.refs_0_), channel_id=1, source_target_pairs={{0,16},{1,17},{2,18},{3,19},{4,20},{5,21},{6,22},{7,23},{8,24},{9,... | collective-permute-start | bytes 1966088 | tf_op jit(solution)/shard_map/ppermute | solution.py:920
  590.2 19.4 %collective-permute-start.47 = (bf16[3,256,512]{2,1,0:T(8,128)(2,1)S(1)}, bf16[3,256,512]{2,1,0:T(8,128)(2,1)S(1)}, u32[]{:S(2)}, u32[]{:S(2)}) collective-permute-start(bf16[3,256,512]{2,1,0:T(8,128)(2,1)S(1)} %bitcast.309), channel_id=1, source_target_pairs={{0,16},{16,0},{1,17},{17,1},{2,18},{18,2},{3,19},{19,3},{4,20},{20... | collective-permute-start | bytes 2359304 | tf_op jit(solution)/shard_map/ppermute | solution.py:820
  598.4 89.5 %collective-permute-start.34 = (bf16[320,1024]{1,0:T(8,128)(2,1)S(1)}, bf16[320,1024]{1,0:T(8,128)(2,1)S(1)}, u32[]{:S(2)}, u32[]{:S(2)}) collective-permute-start(bf16[320,1024]{1,0:T(8,128)(2,1)S(1)} %get-tuple-element.200), channel_id=1, source_target_pairs={{0,1},{1,0},{2,3},{3,2},{4,5},{5,4},{6,7},{7,6},{8,9},{9,8},{10,11... | collective-permute-start | bytes 1966088 | tf_op jit(solution)/shard_map/ppermute | solution.py:820
  600.0 121.1 %collective-permute-start.37 = (bf16[320,1024]{1,0:T(8,128)(2,1)}, bf16[320,1024]{1,0:T(8,128)(2,1)}, u32[]{:S(2)}, u32[]{:S(2)}) collective-permute-start(bf16[320,1024]{1,0:T(8,128)(2,1)} %get-tuple-element.84.refs_0_), channel_id=1, source_target_pairs={{16,18},{17,19},{18,16},{19,17},{20,22},{21,23},{22,20},{23,21},{2... | collective-permute-start | bytes 1966088 | tf_op jit(solution)/shard_map/ppermute | solution.py:923
  700.4 20.7 %collective-permute-start.35 = (bf16[320,1024]{1,0:T(8,128)(2,1)S(1)}, bf16[320,1024]{1,0:T(8,128)(2,1)S(1)}, u32[]{:S(2)}, u32[]{:S(2)}) collective-permute-start(bf16[320,1024]{1,0:T(8,128)(2,1)S(1)} %copy-done.30), channel_id=1, source_target_pairs={{16,2},{17,3},{18,0},{19,1},{20,6},{21,7},{22,4},{23,5},{24,10},{2... | collective-permute-start | bytes 1966088 | tf_op jit(solution)/shard_map/ppermute | solution.py:923
  (75 other events, 650.3 us)

commit v3 on v2

--- a/solution.py
+++ b/solution.py
@@ -50,97 +50,11 @@
     return centered * inverse, inverse
 
 
-def qkv_kernel(x_ref, w_ref, bias_ref, gain_ref, shift_ref, a_ref, q_ref, k_ref, v_ref):
-    width = q_ref.shape[1]
-    normal, _ = norm_stats(x_ref[...].astype(F32))
-    a = (normal * gain_ref[...] + shift_ref[...]).astype(BF16)
-    a_ref[...] = a
-    joined = mm(a, w_ref[...]) + bias_ref[...]
-    q_ref[...] = joined[:, :width].astype(BF16)
-    k_ref[...] = joined[:, width : 2 * width].astype(BF16)
-    v_ref[...] = joined[:, 2 * width :].astype(BF16)
-
-
-def qkv_call(x_all, weights, bias, gain, shift):
-    length = x_all.shape[0]
-    width = weights.shape[1] // 3
-    row = lambda i: (i, 0)
-    whole = lambda i: (0, 0)
-    return pl.pallas_call(
-        qkv_kernel,
-        grid=(length // BQ,),
-        in_specs=[
-            pl.BlockSpec((BQ, D), row),
-            pl.BlockSpec((D, 3 * width), whole),
-            pl.BlockSpec((1, 3 * width), whole),
-            pl.BlockSpec((1, D), whole),
-            pl.BlockSpec((1, D), whole),
-        ],
-        out_specs=[pl.BlockSpec((BQ, D), row)] + [pl.BlockSpec((BQ, width), row)] * 3,
-        out_shape=[jax.ShapeDtypeStruct((length, D), BF16)]
-        + [jax.ShapeDtypeStruct((length, width), BF16)] * 3,
-        compiler_params=params(),
-        cost_estimate=pl.CostEstimate(
-            flops=2 * length * D * 3 * width, bytes_accessed=8 * 2**20, transcendentals=0
-        ),
-    )(x_all, weights, bias, gain, shift)
-
-
 def head_lanes(shape, head):
     lane = lax.broadcasted_iota(jnp.int32, shape, 1)
     return (lane >= head * DH) & (lane < (head + 1) * DH)
 
 
-def attend_kernel(q_ref, k_ref, v_ref, mask_ref, o_ref, lse_ref):
-    width = q_ref.shape[1]
-    heads = width // DH
-    q = q_ref[...]
-    keys = k_ref[...]
-    values = v_ref[...]
-    mask = mask_ref[...]
-    mixed = jnp.zeros((BQ, width), F32)
-    totals = jnp.zeros((BQ, 128), F32)
-    lane = lax.broadcasted_iota(jnp.int32, (BQ, 128), 1)
-    for head in range(heads):
-        mine = head_lanes((BQ, width), head)
-        scores = mm_nt(jnp.where(mine, q, jnp.zeros_like(q)), keys) * SCALE2 + mask
-        top = jnp.max(scores, axis=-1, keepdims=True)
-        weights = jnp.exp2(scores - top)
-        total = jnp.sum(weights, axis=-1, keepdims=True)
-        part = mm(weights.astype(BF16), values) / total
-        mixed = jnp.where(mine, part, mixed)
-        totals = jnp.where(lane == head, top + jnp.log2(total), totals)
-    o_ref[...] = mixed.astype(BF16)
-    lse_ref[...] = totals
-
-
-def attend_call(q, k, v, mask):
-    length, width = q.shape
-    row = lambda i: (i, 0)
-    whole = lambda i: (0, 0)
-    return pl.pallas_call(
-        attend_kernel,
-        grid=(length // BQ,),
-        in_specs=[
-            pl.BlockSpec((BQ, width), row),
-            pl.BlockSpec((length, width), whole),
-            pl.BlockSpec((length, width), whole),
-            pl.BlockSpec((1, length), whole),
-        ],
-        out_specs=[pl.BlockSpec((BQ, width), row), pl.BlockSpec((BQ, 128), row)],
-        out_shape=[
-            jax.ShapeDtypeStruct((length, width), BF16),
-            jax.ShapeDtypeStruct((length, 128), F32),
-        ],
-        compiler_params=params(),
-        cost_estimate=pl.CostEstimate(
-            flops=16 * length * length * width,
-            bytes_accessed=4 * 2**20,
-            transcendentals=length * length * width // DH,
-        ),
-    )(q, k, v, mask)
-
-
 def shards_of():
     return lax.axis_size("dp") * lax.axis_size("seq")
 
@@ -152,132 +66,6 @@
 
 GELU_A = math.sqrt(2.0 / math.pi)
 GELU_B = 0.044715
-
-
-def mlp_kernel(
-    sel_ref,
-    o_ref,
-    x_ref,
-    wo_ref,
-    vec_ref,
-    bup_ref,
-    up0_ref,
-    up1_ref,
-    down0_ref,
-    down1_ref,
-    h_ref,
-    a_ref,
-    u_ref,
-    g_ref,
-    y_ref,
-    acc,
-):
-    step = pl.program_id(0)
-    groups, _, width = o_ref.shape
-    unit = FF // shards_of() // 2
-
-    @pl.when(step == 0)
-    def _():
-        hidden = x_ref[...].astype(F32) + vec_ref[0:1, :]
-        for group in range(groups):
-            hidden += mm(o_ref[group], wo_ref[group * width : (group + 1) * width, :])
-        h_ref[...] = hidden
-        normal, _ = norm_stats(hidden)
-        a_ref[...] = (normal * vec_ref[1:2, :] + vec_ref[2:3, :]).astype(BF16)
-        acc[...] = hidden + vec_ref[3:4, :]
-
-    def part(up_ref, down_ref):
-        upper = mm(a_ref[...], up_ref[...]) + bup_ref[...]
-        u_ref[...] = upper
-        inner = GELU_A * (upper + GELU_B * upper * upper * upper)
-        gated = (0.5 * upper * (1.0 + jnp.tanh(inner))).astype(BF16)
-        put_halves(g_ref, gated, unit)
-        acc[...] += mm(gated, down_ref[...])
-
-    pl.when(sel_ref[0] == 0)(lambda: part(up0_ref, down0_ref))
-    pl.when(sel_ref[0] == 1)(lambda: part(up1_ref, down1_ref))
-
-    @pl.when(step == pl.num_programs(0) - 1)
-    def _():
-        y_ref[...] = acc[...].astype(BF16)
-
-
-def mlp_call(sel, o_all, x_own, wo, vecs, bup, ups, downs):
-    rows = x_own.shape[0]
-    groups, _, width = o_all.shape
-    whole = lambda i, s: (0, 0)
-    col = lambda which: (lambda i, s: (0, jnp.where(s[0] == which, i, 0)))
-    line = lambda which: (lambda i, s: (jnp.where(s[0] == which, i, 0), 0))
-    chunk = lambda i, s: (0, i)
-    return pl.pallas_call(
-        mlp_kernel,
-        grid_spec=pltpu.PrefetchScalarGridSpec(
-            num_scalar_prefetch=1,
-            grid=(NCH,),
-            in_specs=[
-                pl.BlockSpec((groups, rows, width), lambda i, s: (0, 0, 0)),
-                pl.BlockSpec((rows, D), whole),
-                pl.BlockSpec((D, D), whole),
-                pl.BlockSpec((8, D), whole),
-                pl.BlockSpec((1, FC), chunk),
-                pl.BlockSpec((D, FC), col(0)),
-                pl.BlockSpec((D, FC), col(1)),
-                pl.BlockSpec((FC, D), line(0)),
-                pl.BlockSpec((FC, D), line(1)),
-            ],
-            out_specs=[
-                pl.BlockSpec((rows, D), whole),
-                pl.BlockSpec((rows, D), whole),
-                pl.BlockSpec((rows, FC), chunk),
-                pl.BlockSpec((2, rows, FC // 2), lambda i, s: (0, 0, i)),
-                pl.BlockSpec((rows, D), whole),
-            ],
-            scratch_shapes=[pltpu.VMEM((rows, D), F32)],
-        ),
-        out_shape=[
-            jax.ShapeDtypeStruct((rows, D), F32),
-            jax.ShapeDtypeStruct((rows, D), BF16),
-            jax.ShapeDtypeStruct((rows, FF), F32),
-            jax.ShapeDtypeStruct((2, rows, FF // 2), BF16),
-            jax.ShapeDtypeStruct((rows, D), BF16),
-        ],
-        compiler_params=params(),
-        cost_estimate=pl.CostEstimate(
-            flops=2 * rows * D * (D + 2 * FF), bytes_accessed=30 * 2**20, transcendentals=rows * FF
-        ),
-    )(sel, o_all, x_own, wo, vecs, bup, ups[0], ups[1], downs[0], downs[1])
-
-
-def norm_back_kernel(mine_ref, other_ref, x_ref, dh_ref, gain_ref, dx_ref, sums_ref):
-    d_normed = mine_ref[...].astype(F32) + other_ref[...].astype(F32)
-    normal, inverse = norm_stats(x_ref[...].astype(F32))
-    sums_ref[...] = jnp.zeros_like(sums_ref)
-    sums_ref[0:1, :] = jnp.sum(d_normed * normal, axis=0, keepdims=True)
-    sums_ref[1:2, :] = jnp.sum(d_normed, axis=0, keepdims=True)
-    d_normal = d_normed * gain_ref[...]
-    dx_ref[...] = (
-        dh_ref[...]
-        + inverse
-        * (
-            d_normal
-            - jnp.mean(d_normal, axis=-1, keepdims=True)
-            - normal * jnp.mean(d_normal * normal, axis=-1, keepdims=True)
-        )
-    ).astype(BF16)
-
-
-def norm_back_call(mine, other, x_own, d_hidden, gain):
-    return pl.pallas_call(
-        norm_back_kernel,
-        out_shape=[
-            jax.ShapeDtypeStruct(x_own.shape, BF16),
-            jax.ShapeDtypeStruct((8, D), F32),
-        ],
-        compiler_params=params(),
-        cost_estimate=pl.CostEstimate(
-            flops=20 * x_own.size, bytes_accessed=10 * x_own.size, transcendentals=0
-        ),
-    )(mine, other, x_own, d_hidden, gain)
 
 
 MESH_AXES = ("dp", "seq")
@@ -416,7 +204,9 @@
         self.copy(stage).wait_recv()
         got = self.buffers[stage + 1]
         rows = got.shape[-2]
-        chunk = 16
+        chunk = rows
+        while chunk * got.shape[-1] > 65536 and chunk % 32 == 0:
+            chunk //= 2
         per = rows // chunk
         last = stage == self.count - 1
         core = lax.axis_index("section")
@@ -474,6 +264,10 @@
     return tuple(unit * n for n in (first, first, rest - second, second))
 
 
+SPLIT = True
+DELAY = True
+
+
 class Hosted:
     def __init__(self, dp_count, count, shapes):
         self.dp_count, self.count, self.shapes = dp_count, count, shapes
@@ -490,7 +284,7 @@
             start = 0
             for order, size in zip(orders, widths):
                 pieces = [size] if size else []
-                if size >= 256 and not compact:
+                if size >= 256 and not compact and SPLIT:
                     first = 128 * -(-size // 256)
                     pieces = [first, size - first]
                 for k, piece in enumerate(pieces):
@@ -552,13 +346,17 @@
                 )
             )
     def begin(self):
-        greet(self.all_bits + [("section", 1)])
-        for part in self.parts:
-            part.begin()
+        for k, part in enumerate(self.parts):
+            if not (DELAY and self.plan[k][7]):
+                part.begin()
 
     def run(self, first, last):
         for _, k, stage in self.events[first:last]:
             self.parts[k].step(stage)
+            if DELAY and stage == 0 and self.plan[k][7] == 0:
+                for j, other in enumerate(self.plan):
+                    if other[:2] == self.plan[k][:2] and other[7] == 1:
+                        self.parts[j].begin()
 
     def slots(self, times, total):
         edges = []
@@ -587,6 +385,7 @@
 def reduce_kernel(host, *refs):
     n = host.arrays
     host.bind(refs[:n], refs[n : 2 * n], refs[2 * n :])
+    greet(host.all_bits + [("section", 1)])
     host.begin()
     host.run(0, len(host.events))
     host.finish()
@@ -605,27 +404,489 @@
     )(*host.views(arrays))
 
 
-MLP_SLOT = 2.4
+MLP_SLOT = 2.9
 ATT_SLOT = 1.4
+
+
+class Group:
+    def __init__(self):
+        self.half = lax.axis_size("seq") // 2
+        self.core = lax.axis_index("section")
+        self.place = lax.axis_index("seq")
+        self.low = lax.rem(self.place, self.half)
+        self.base = self.place - self.low
+        self.rank = self.core * self.half + self.low
+
+    def others(self):
+        pairs = [(dc, d) for d in range(1, self.half) for dc in (0, 1)]
+        return pairs + [(1, 0)]
+
+    def slot(self, dc, d):
+        return dc * self.half + d
+
+    def where(self, dc, d):
+        core = lax.rem(self.core + dc, 2)
+        low = lax.rem(self.low + d, self.half)
+        return core, low
+
+    def device(self, dc, d):
+        core, low = self.where(dc, d)
+        return {"section": core, "seq": self.base + low}
+
+    def rank_of(self, dc, d):
+        core, low = self.where(dc, d)
+        return core * self.half + low
+
+    def greet(self, dp_count):
+        barrier = pltpu.get_barrier_semaphore()
+        targets = [self.device(dc, d) for dc, d in self.others()]
+        mask = dp_count // 2
+        while mask:
+            targets.append({"dp": partner("dp", mask)})
+            mask //= 2
+        targets.append({"seq": partner("seq", self.half)})
+        for target in targets:
+            pl.semaphore_signal(
+                barrier, inc=1, device_id=target, device_id_type=pl.DeviceIdType.MESH
+            )
+        pl.semaphore_wait(barrier, len(targets))
+
+
+def send(src, dst, sems, slot, device):
+    return pltpu.make_async_remote_copy(
+        src_ref=src,
+        dst_ref=dst,
+        send_sem=sems[0].at[slot],
+        recv_sem=sems[1].at[slot],
+        device_id=device,
+        device_id_type=pl.DeviceIdType.MESH,
+    )
+
+
+def dma_pair(count):
+    return [pltpu.SemaphoreType.DMA((count,)), pltpu.SemaphoreType.DMA((count,))]
+
+
+VEC_ROWS = 16
+LN1_GAIN, LN1_BIAS, B_QUERY, B_VALUE, B_OUT, LN2_GAIN, LN2_BIAS, B_DOWN, B_UP = range(9)
+
+
+def attend_kernel(first, layer, dp_count, *refs):
+    if first:
+        x_ref, joint_ref, wout_ref, mask_ref = refs[:4]
+        vectors = refs[4:13]
+        o_out, lse_out, a_out, q_out, k_out, v_out = refs[13:19]
+        x_out, joint_out, wout_out, vec_out = refs[19:23]
+        rest = refs[23:]
+    else:
+        x_ref, joint_ref, mask_ref, vec_ref = refs[:4]
+        o_out, lse_out, a_out, q_out, k_out, v_out = refs[4:10]
+        rest = refs[10:]
+    x_all, a_all, q_all, k_all, v_all, lse, o_send, o_recv = rest[:8]
+    x_sems, o_sems = rest[8:10], rest[10:12]
+    out_sems = rest[12]
+    if first:
+        joint_pair, wide_own, wide_other, vec_send, vec_recv, vec_pair = rest[13:19]
+        wide_sems, vec_sems = rest[19:21], rest[21:23]
+        load_sems = rest[23]
+    else:
+        joint_one = rest[13]
+        load_sems = rest[14]
+    group = Group()
+    core, half, rank, low = group.core, group.half, group.rank, group.low
+    ranks, rows, _ = x_all.shape
+    width = q_all.shape[1]
+    heads = width // DH
+    span = half * width
+    partner_core = group.device(1, 0)
+    micro = lax.div(group.place, half)
+
+    group.greet(dp_count)
+
+    def x_copy(slot, from_rank, device):
+        return send(x_all.at[from_rank], x_all.at[from_rank], x_sems, slot, device)
+
+    far = {"seq": partner("seq", half)}
+
+    if first:
+        own_load = pltpu.make_async_copy(x_ref.at[micro, 0], x_all.at[rank], load_sems.at[0])
+        far_copy = send(x_ref.at[1 - micro, 0], x_all.at[rank], x_sems, 2 * half - 1, far)
+        pl.when(core == 1)(lambda: far_copy.start())
+        pl.when(core == 0)(lambda: own_load.start())
+        wide_copies = []
+        own_loads = []
+        for part in range(3):
+            theirs = pl.ds(pl.multiple_of(part * D + (1 - core) * span, 128), span)
+            ours = pl.ds(pl.multiple_of(part * D + core * span, 128), span)
+            wide_copies.append(
+                send(joint_ref.at[0, :, theirs], wide_other.at[part], wide_sems, part, partner_core)
+            )
+            own_loads.append(
+                pltpu.make_async_copy(
+                    joint_ref.at[0, :, ours], wide_own.at[part], load_sems.at[1 + part]
+                )
+            )
+            wide_copies[-1].start()
+            own_loads[-1].start()
+        vec_send[...] = jnp.zeros_like(vec_send)
+        for i, value in enumerate(vectors[:8]):
+            vec_send[i : i + 1, :] = value[...].astype(F32)
+        for i in range(FF // D):
+            vec_send[8 + i : 9 + i, :] = vectors[8][:, i * D : (i + 1) * D].astype(F32)
+        vec_copy = send(vec_send, vec_recv, vec_sems, 0, partner_core)
+        vec_copy.start()
+        wout_copy = send(wout_ref.at[0], wout_out, vec_sems, 1, partner_core)
+        pl.when(core == 1)(lambda: far_copy.wait_recv())
+        pl.when(core == 0)(lambda: own_load.wait())
+    else:
+        own_load = pltpu.make_async_copy(x_ref, x_all.at[rank], load_sems.at[0])
+        joint_load = pltpu.make_async_copy(joint_ref, joint_one, load_sems.at[1])
+        own_load.start()
+        joint_load.start()
+        own_load.wait()
+    for d in range(1, half):
+        x_copy(d - 1, rank, group.device(0, d)).start()
+    x_copy(half - 1, rank, partner_core).start()
+
+    source = lax.broadcasted_iota(jnp.int32, (span, width), 0)
+    target = lax.broadcasted_iota(jnp.int32, (span, width), 1)
+    if half == 2:
+        wanted = (2 * lax.div(target, DH) + low) * DH + lax.rem(target, DH)
+    else:
+        wanted = low * width + target
+    pick = (source == wanted).astype(F32).astype(BF16)
+    if first:
+        wout_copy.start()
+        vec_copy.wait_recv()
+        vec_pair[core] = vec_send[...]
+        vec_pair[1 - core] = vec_recv[...]
+        for load in own_loads:
+            load.wait()
+        for part in range(3):
+            joint_pair[core, :, part * width : (part + 1) * width] = mm(
+                wide_own[part], pick
+            ).astype(BF16)
+        for copy in wide_copies:
+            copy.wait_recv()
+        for part in range(3):
+            joint_pair[1 - core, :, part * width : (part + 1) * width] = mm(
+                wide_other[part], pick
+            ).astype(BF16)
+        vec = vec_pair[0]
+        weights = lambda: joint_pair[0]
+    else:
+        joint_load.wait()
+        vec = vec_ref[0]
+        weights = lambda: joint_one[...]
+
+    def of_heads(row):
+        parts = vec[row : row + 1, :]
+        mine = jnp.where(core == 0, parts[:, :span], parts[:, span:])
+        wide = jnp.broadcast_to(mine, (16, span)).astype(BF16)
+        return mm(wide, pick)[0:1, :]
+
+    bias_q = of_heads(B_QUERY)
+    bias_v = of_heads(B_VALUE)
+    gain = vec[LN1_GAIN : LN1_GAIN + 1, :]
+    shift = vec[LN1_BIAS : LN1_BIAS + 1, :]
+
+    def project(at):
+        normal, _ = norm_stats(x_all[at].astype(F32))
+        a = (normal * gain + shift).astype(BF16)
+        here = pl.ds(pl.multiple_of(at * rows, 16), rows)
+        a_all[here, :] = a
+        joined = mm(a, weights())
+        q_all[here, :] = (joined[:, :width] + bias_q).astype(BF16)
+        k_all[here, :] = joined[:, width : 2 * width].astype(BF16)
+        v_all[here, :] = (joined[:, 2 * width :] + bias_v).astype(BF16)
+
+    project(rank)
+    x_copy(half - 1, rank, partner_core).wait_recv()
+    project(group.rank_of(1, 0))
+    for d in range(1, half):
+        here = group.rank_of(0, half - d)
+        x_copy(d - 1, here, partner_core).wait_recv()
+        x_copy(half - 1 + d, here, partner_core).start()
+        project(here)
+    for d in range(1, half):
+        there = group.rank_of(1, half - d)
+        x_copy(half - 1 + d, there, partner_core).wait_recv()
+        project(there)
+
+    saves = [
+        pltpu.make_async_copy(a_all, a_out, out_sems.at[0]),
+        pltpu.make_async_copy(q_all, q_out, out_sems.at[1]),
+        pltpu.make_async_copy(k_all, k_out, out_sems.at[2]),
+        pltpu.make_async_copy(v_all, v_out, out_sems.at[3]),
+    ]
+    if first:
+        saves.append(pltpu.make_async_copy(joint_pair, joint_out, out_sems.at[4]))
+        saves.append(pltpu.make_async_copy(x_all.at[rank], x_out, out_sems.at[5]))
+        saves.append(pltpu.make_async_copy(vec_pair, vec_out, out_sems.at[6]))
+    for save in saves:
+        save.start()
+
+    lane = lax.broadcasted_iota(jnp.int32, (rows, 128), 1)
+    mask = mask_ref[...]
+
+    def attend(at):
+        here = pl.ds(pl.multiple_of(at * rows, 16), rows)
+        q = q_all[here, :]
+        mixed = jnp.zeros((rows, width), F32)
+        totals = jnp.zeros((rows, 128), F32)
+        for head in range(heads):
+            mine = head_lanes((rows, width), head)
+            scores = mm_nt(jnp.where(mine, q, jnp.zeros_like(q)), k_all[...]) * SCALE2 + mask
+            top = jnp.max(scores, axis=-1, keepdims=True)
+            expo = jnp.exp2(scores - top)
+            total = jnp.sum(expo, axis=-1, keepdims=True)
+            part = mm(expo.astype(BF16), v_all[...]) / total
+            mixed = jnp.where(mine, part, mixed)
+            totals = jnp.where(lane == head, top + jnp.log2(total), totals)
+        lse[here, :] = totals
+        return mixed.astype(BF16)
+
+    copies = []
+    for dc, d in group.others():
+        slot = group.slot(dc, d)
+        o_send[slot] = attend(group.rank_of(dc, d))
+        copies.append(send(o_send.at[slot], o_recv.at[rank], o_sems, slot, group.device(dc, d)))
+        copies[-1].start()
+    o_recv[rank] = attend(rank)
+    lse_out[...] = lse[...]
+    for copy in copies:
+        copy.wait()
+    o_out[...] = o_recv[...]
+    for save in saves:
+        save.wait()
+    for d in range(1, half):
+        x_copy(d - 1, rank, group.device(0, d)).wait_send()
+        x_copy(half - 1 + d, group.rank_of(0, half - d), partner_core).wait_send()
+    x_copy(half - 1, rank, partner_core).wait_send()
+    if first:
+        pl.when(core == 1)(lambda: far_copy.wait_send())
+        for copy in wide_copies:
+            copy.wait_send()
+        vec_copy.wait_send()
+        wout_copy.wait()
+
+
+def attend_call(first, layer, mask, ranks, dp_count, *args):
+    rows = args[0].shape[-2]
+    width = D // ranks
+    half = ranks // 2
+    span = half * width
+    anywhere = pl.BlockSpec(memory_space=pl.ANY)
+    vmem = pl.BlockSpec(memory_space=pltpu.VMEM)
+    out_shape = [
+        jax.ShapeDtypeStruct((ranks, rows, width), BF16),
+        jax.ShapeDtypeStruct((LEN, 128), F32),
+        jax.ShapeDtypeStruct((LEN, D), BF16),
+        jax.ShapeDtypeStruct((LEN, width), BF16),
+        jax.ShapeDtypeStruct((LEN, width), BF16),
+        jax.ShapeDtypeStruct((LEN, width), BF16),
+    ]
+    out_specs = [vmem, vmem] + [anywhere] * 4
+    scratch = [
+        pltpu.VMEM((ranks, rows, D), BF16),
+        pltpu.VMEM((LEN, D), BF16),
+        pltpu.VMEM((LEN, width), BF16),
+        pltpu.VMEM((LEN, width), BF16),
+        pltpu.VMEM((LEN, width), BF16),
+        pltpu.VMEM((LEN, 128), F32),
+        pltpu.VMEM((ranks, rows, width), BF16),
+        pltpu.VMEM((ranks, rows, width), BF16),
+    ]
+    scratch += dma_pair(2 * half) + dma_pair(ranks) + [pltpu.SemaphoreType.DMA((7,))]
+    if first:
+        operands = args[:3] + (mask,) + args[3:]
+        in_specs = [anywhere] * 3 + [vmem] * (1 + len(args[3:]))
+        out_shape += [
+            jax.ShapeDtypeStruct((rows, D), BF16),
+            jax.ShapeDtypeStruct((2, D, 3 * width), BF16),
+            jax.ShapeDtypeStruct((D, D), BF16),
+            jax.ShapeDtypeStruct((2, VEC_ROWS, D), F32),
+        ]
+        out_specs += [anywhere] * 4
+        scratch += [
+            pltpu.VMEM((2, D, 3 * width), BF16),
+            pltpu.VMEM((3, D, span), BF16),
+            pltpu.VMEM((3, D, span), BF16),
+            pltpu.VMEM((VEC_ROWS, D), F32),
+            pltpu.VMEM((VEC_ROWS, D), F32),
+            pltpu.VMEM((2, VEC_ROWS, D), F32),
+        ]
+        scratch += dma_pair(3) + dma_pair(2) + [pltpu.SemaphoreType.DMA((4,))]
+    else:
+        operands = args[:2] + (mask,) + args[2:]
+        in_specs = [anywhere] * 2 + [vmem] * 2
+        scratch += [pltpu.VMEM((D, 3 * width), BF16), pltpu.SemaphoreType.DMA((2,))]
+    return pl.pallas_call(
+        functools.partial(attend_kernel, first, layer, dp_count),
+        in_specs=in_specs,
+        out_specs=out_specs,
+        out_shape=out_shape,
+        scratch_shapes=scratch,
+        compiler_params=pltpu.CompilerParams(
+            vmem_limit_bytes=VMEM_LIMIT, collective_id=5 + layer, has_side_effects=True
+        ),
+        cost_estimate=pl.CostEstimate(
+            flops=40 * 10**9, bytes_accessed=20 * 2**20, transcendentals=LEN * LEN * width // DH
+        ),
+    )(*operands)
+
+
+def mlp_kernel(
+    layer,
+    o_ref,
+    x_ref,
+    wo0_ref,
+    wo1_ref,
+    vec_ref,
+    up0_ref,
+    up1_ref,
+    down0_ref,
+    down1_ref,
+    h_ref,
+    a_ref,
+    u_ref,
+    g_ref,
+    y_ref,
+    acc,
+    wo,
+    sem,
+):
+    step = pl.program_id(0)
+    groups, _, width = o_ref.shape
+    unit = FF // shards_of() // 2
+    own = lax.axis_index("section") == layer
+
+    @pl.when(step == 0)
+    def _():
+        first = pltpu.make_async_copy(wo0_ref, wo, sem)
+        second = pltpu.make_async_copy(wo1_ref, wo, sem)
+
+        @pl.when(own)
+        def _():
+            first.start()
+            first.wait()
+
+        @pl.when(jnp.logical_not(own))
+        def _():
+            second.start()
+            second.wait()
+
+        hidden = x_ref[...].astype(F32) + vec_ref[0, B_OUT : B_OUT + 1, :]
+        for group in range(groups):
+            hidden += mm(o_ref[group], wo[group * width : (group + 1) * width, :])
+        h_ref[...] = hidden
+        normal, _ = norm_stats(hidden)
+        a_ref[...] = (
+            normal * vec_ref[0, LN2_GAIN : LN2_GAIN + 1, :] + vec_ref[0, LN2_BIAS : LN2_BIAS + 1, :]
+        ).astype(BF16)
+        acc[...] = hidden + vec_ref[0, B_DOWN : B_DOWN + 1, :]
+
+    def part(up_ref, down_ref):
+        at = pl.multiple_of(lax.rem(step, D // FC) * FC, FC)
+        bias = vec_ref[0, pl.ds(B_UP + lax.div(step, D // FC), 1), pl.ds(at, FC)]
+        upper = mm(a_ref[...], up_ref[...]) + bias
+        u_ref[...] = upper
+        inner = GELU_A * (upper + GELU_B * upper * upper * upper)
+        gated = (0.5 * upper * (1.0 + jnp.tanh(inner))).astype(BF16)
+        put_halves(g_ref, gated, unit)
+        acc[...] += mm(gated, down_ref[...])
+
+    pl.when(own)(lambda: part(up0_ref, down0_ref))
+    pl.when(jnp.logical_not(own))(lambda: part(up1_ref, down1_ref))
+
+    @pl.when(step == pl.num_programs(0) - 1)
+    def _():
+        y_ref[...] = acc[...].astype(BF16)
+
+
+def mlp_call(layer, o_all, x_own, outs, vec, ups, downs):
+    rows = x_own.shape[0]
+    groups, _, width = o_all.shape
+    whole = lambda i: (0, 0)
+    mine = lambda i, first: jnp.where((lax.axis_index("section") == layer) == first, i, 0)
+    col = lambda first: (lambda i: (0, mine(i, first)))
+    line = lambda first: (lambda i: (mine(i, first), 0))
+    chunk = lambda i: (0, i)
+    return pl.pallas_call(
+        functools.partial(mlp_kernel, layer),
+        grid=(NCH,),
+        in_specs=[
+            pl.BlockSpec((groups, rows, width), lambda i: (0, 0, 0)),
+            pl.BlockSpec((rows, D), whole),
+            pl.BlockSpec(memory_space=pl.ANY),
+            pl.BlockSpec(memory_space=pl.ANY),
+            pl.BlockSpec((1, VEC_ROWS, D), lambda i: (layer, 0, 0)),
+            pl.BlockSpec((D, FC), col(True)),
+            pl.BlockSpec((D, FC), col(False)),
+            pl.BlockSpec((FC, D), line(True)),
+            pl.BlockSpec((FC, D), line(False)),
+        ],
+        out_specs=[
+            pl.BlockSpec((rows, D), whole),
+            pl.BlockSpec((rows, D), whole),
+            pl.BlockSpec((rows, FC), chunk),
+            pl.BlockSpec((2, rows, FC // 2), lambda i: (0, 0, i)),
+            pl.BlockSpec((rows, D), whole),
+        ],
+        scratch_shapes=[
+            pltpu.VMEM((rows, D), F32),
+            pltpu.VMEM((D, D), BF16),
+            pltpu.SemaphoreType.DMA,
+        ],
+        out_shape=[
+            jax.ShapeDtypeStruct((rows, D), F32),
+            jax.ShapeDtypeStruct((rows, D), BF16),
+            jax.ShapeDtypeStruct((rows, FF), F32),
+            jax.ShapeDtypeStruct((2, rows, FF // 2), BF16),
+            jax.ShapeDtypeStruct((rows, D), BF16),
+        ],
+        compiler_params=params(),
+        cost_estimate=pl.CostEstimate(
+            flops=2 * rows * D * (D + 2 * FF), bytes_accessed=30 * 2**20, transcendentals=rows * FF
+        ),
+    )(o_all, x_own, outs[0], outs[1], vec, ups[0], ups[1], downs[0], downs[1])
 
 
 def mlp_back_kernel(layer, host, ranges, *refs):
     n = host.arrays
-    dy_ref, h_ref, wo_ref, vec_ref, u_ref, up0_ref, up1_ref, down0_ref, down1_ref = refs[:9]
-    srcs = refs[9 : 9 + n]
-    du_ref, gbup_ref, dh_ref, dr_ref, do_ref, sums_ref = refs[9 + n : 15 + n]
-    outs = refs[15 + n : 15 + 2 * n]
-    acc = refs[15 + 2 * n]
-    host.bind(srcs, outs, refs[16 + 2 * n :])
+    dy_ref, h_ref, wo0_ref, wo1_ref, vec_ref, u_ref, a2_ref = refs[:7]
+    up0_ref, up1_ref, down0_ref, down1_ref = refs[7:11]
+    srcs = refs[11 : 11 + n]
+    refs = refs[1:]
+    gup_ref, gbup_ref, dh_ref, dr_ref, do_ref, sums_ref = refs[10 + n : 16 + n]
+    outs = refs[16 + n : 16 + 2 * n]
+    (acc, du_mine, du_send, du_recv, dr_send, dr_recv, do_send, do_recv) = refs[
+        16 + 2 * n : 24 + 2 * n
+    ]
+    du_sems = refs[24 + 2 * n : 26 + 2 * n]
+    do_sems = refs[26 + 2 * n : 28 + 2 * n]
+    wo_ref, wo_sem = refs[28 + 2 * n : 30 + 2 * n]
+    host.bind(srcs, outs, refs[30 + 2 * n :])
+    group = Group()
+    core = group.core
     step = pl.program_id(0)
-    groups, _, width = do_ref.shape
+    ranks, rows, width = do_ref.shape
     unit = FF // shards_of() // 2
-    own = lax.axis_index("section") == layer
+    own = core == layer
+    partner_core = group.device(1, 0)
 
     @pl.when(step == 0)
     def _():
+        group.greet(host.dp_count)
         host.begin()
+        pl.when(own)(lambda: pltpu.make_async_copy(wo0_ref, wo_ref, wo_sem).start())
+        pl.when(jnp.logical_not(own))(
+            lambda: pltpu.make_async_copy(wo1_ref, wo_ref, wo_sem).start()
+        )
         acc[...] = jnp.zeros_like(acc)
+
+    def du_copy(at):
+        return send(du_send.at[at], du_recv.at[at], du_sems, at, partner_core)
 
     def part(up_ref, down_ref):
         d_gated = mm_nt(dy_ref[...], down_ref[...])
@@ -636,18 +897,33 @@
             1.0 + (3.0 * GELU_B) * square
         )
         d_upper = (d_gated * slope).astype(BF16)
-        put_halves(du_ref, d_upper, unit)
+        for at in range(0, FC // unit, 2):
+            even = d_upper[:, at * unit : (at + 1) * unit]
+            odd = d_upper[:, (at + 1) * unit : (at + 2) * unit]
+            cols = slice(at // 2 * unit, (at // 2 + 1) * unit)
+            du_mine[step, :, cols] = jnp.where(core == 0, even, odd)
+            du_send[step, :, cols] = jnp.where(core == 0, odd, even)
         gbup_ref[...] = jnp.sum(d_upper.astype(F32), axis=0, keepdims=True)
         acc[...] += mm_nt(d_upper, up_ref[...])
 
-    pl.when(own)(lambda: part(up0_ref, down0_ref))
-    pl.when(jnp.logical_not(own))(lambda: part(up1_ref, down1_ref))
+    @pl.when(step < NCH)
+    def _():
+        pl.when(own)(lambda: part(up0_ref, down0_ref))
+        pl.when(jnp.logical_not(own))(lambda: part(up1_ref, down1_ref))
+        du_copy(step).start()
+
+    @pl.when(step > 0)
+    def _():
+        at = step - 1
+        du_copy(at).wait()
+        value = mm_tn(du_mine[at], a2_ref[:rows, :]) + mm_tn(du_recv[at], a2_ref[rows:, :])
+        gup_ref[...] = value.astype(BF16).reshape(gup_ref.shape)
 
     for slot, (first, last) in enumerate(ranges[:-1]):
         if last > first:
             pl.when(step == slot)(functools.partial(host.run, first, last))
 
-    @pl.when(step == pl.num_programs(0) - 1)
+    @pl.when(step == NCH)
     def _():
         normal, inverse = norm_stats(h_ref[...])
         d_out = dy_ref[...].astype(F32)
@@ -655,7 +931,7 @@
         sums_ref[...] = jnp.zeros_like(sums_ref)
         sums_ref[0:1, :] = jnp.sum(d_normed * normal, axis=0, keepdims=True)
         sums_ref[1:2, :] = jnp.sum(d_normed, axis=0, keepdims=True)
-        d_normal = d_normed * vec_ref[1:2, :]
+        d_normal = d_normed * vec_ref[0, LN2_GAIN : LN2_GAIN + 1, :]
         d_hidden = d_out + inverse * (
             d_normal
             - jnp.mean(d_normal, axis=-1, keepdims=True)
@@ -663,35 +939,60 @@
         )
         dh_ref[...] = d_hidden
         d_branch = d_hidden.astype(BF16)
-        dr_ref[...] = d_branch
+        dr_ref[0] = d_branch
+        dr_send[...] = d_branch
+        branch_copy = send(dr_send, dr_recv, do_sems, ranks, partner_core)
+        branch_copy.start()
+        pltpu.make_async_copy(wo0_ref, wo_ref, wo_sem).wait()
+
+        def heads_of(rank):
+            at = pl.multiple_of(rank * width, width)
+            return mm_nt(d_branch, wo_ref[pl.ds(at, width), :]).astype(BF16)
+
+        copies = []
+        for dc, d in group.others():
+            slot = group.slot(dc, d)
+            do_send[slot] = heads_of(group.rank_of(dc, d))
+            copies.append(
+                send(do_send.at[slot], do_recv.at[group.rank], do_sems, slot, group.device(dc, d))
+            )
+            copies[-1].start()
+        do_recv[group.rank] = heads_of(group.rank)
         sums_ref[2:3, :] = jnp.sum(d_branch.astype(F32), axis=0, keepdims=True)
         sums_ref[3:4, :] = jnp.sum(d_out, axis=0, keepdims=True)
-        for group in range(groups):
-            do_ref[group] = mm_nt(
-                d_branch, wo_ref[group * width : (group + 1) * width, :]
-            ).astype(BF16)
         host.run(*ranges[-1])
+        branch_copy.wait()
+        dr_ref[1] = dr_recv[...]
+        for copy in copies:
+            copy.wait()
+        do_ref[...] = do_recv[...]
         host.finish()
 
 
-def mlp_back_call(layer, dy, hidden, wo, vecs, upper, ups, downs, groups, host, arrays, total):
+def mlp_back_call(layer, dy, hidden, wos, vec, upper, a2_all, ups, downs, ranks, host, arrays, total):
     rows = dy.shape[0]
-    width = D // groups
+    width = D // ranks
+    shards = host.dp_count * host.count
+    per = shards // NCH if shards >= NCH else 1
+    unit = FF // shards // 2
     whole = lambda i: (0, 0)
-    mine = lambda i, first: jnp.where((lax.axis_index("section") == layer) == first, i, 0)
+    now = lambda i: jnp.minimum(i, NCH - 1)
+    mine = lambda i, first: jnp.where((lax.axis_index("section") == layer) == first, now(i), 0)
     col = lambda first: (lambda i: (0, mine(i, first)))
     line = lambda first: (lambda i: (mine(i, first), 0))
-    chunk = lambda i: (0, i)
-    ranges = host.slots([MLP_SLOT * (i + 1) for i in range(NCH)], total)
+    chunk = lambda i: (0, now(i))
+    ranges = host.slots([MLP_SLOT * (i + 1) for i in range(NCH + 1)], total)
     return pl.pallas_call(
         functools.partial(mlp_back_kernel, layer, host, ranges),
-        grid=(NCH,),
+        grid=(NCH + 1,),
         in_specs=[
             pl.BlockSpec((rows, D), whole),
             pl.BlockSpec((rows, D), whole),
-            pl.BlockSpec((D, D), whole),
-            pl.BlockSpec((8, D), whole),
+            pl.BlockSpec(memory_space=pl.ANY),
+            pl.BlockSpec(memory_space=pl.ANY),
+            pl.BlockSpec((1, VEC_ROWS, D), lambda i: (layer, 0, 0)),
             pl.BlockSpec((rows, FC), chunk),
+            pl.BlockSpec((2 * rows, D), whole),
             pl.BlockSpec((D, FC), col(True)),
             pl.BlockSpec((D, FC), col(False)),
             pl.BlockSpec((FC, D), line(True)),
@@ -699,120 +1000,228 @@
         ]
         + host.in_specs(),
         out_specs=[
-            pl.BlockSpec((2, rows, FC // 2), lambda i: (0, 0, i)),
+            pl.BlockSpec((per, unit, D), lambda i: (jnp.maximum(i - 1, 0), 0, 0)),
             pl.BlockSpec((1, FC), chunk),
             pl.BlockSpec((rows, D), whole),
-            pl.BlockSpec((rows, D), whole),
-            pl.BlockSpec((groups, rows, width), lambda i: (0, 0, 0)),
+            pl.BlockSpec((2, rows, D), lambda i: (0, 0, 0)),
+            pl.BlockSpec((ranks, rows, width), lambda i: (0, 0, 0)),
             pl.BlockSpec((8, D), whole),
         ]
         + host.out_specs(),
-        scratch_shapes=[pltpu.VMEM((rows, D), F32)] + host.scratch(),
+        scratch_shapes=[
+            pltpu.VMEM((rows, D), F32),
+            pltpu.VMEM((NCH, rows, FC // 2), BF16),
+            pltpu.VMEM((NCH, rows, FC // 2), BF16),
+            pltpu.VMEM((NCH, rows, FC // 2), BF16),
+            pltpu.VMEM((rows, D), BF16),
+            pltpu.VMEM((rows, D), BF16),
+            pltpu.VMEM((ranks, rows, width), BF16),
+            pltpu.VMEM((ranks, rows, width), BF16),
+        ]
+        + dma_pair(NCH)
+        + dma_pair(ranks + 1)
+        + [pltpu.VMEM((D, D), BF16), pltpu.SemaphoreType.DMA]
+        + host.scratch(),
         out_shape=[
-            jax.ShapeDtypeStruct((2, rows, FF // 2), BF16),
+            jax.ShapeDtypeStruct((shards, unit, D), BF16),
             jax.ShapeDtypeStruct((1, FF), F32),
             jax.ShapeDtypeStruct((rows, D), F32),
-            jax.ShapeDtypeStruct((rows, D), BF16),
-            jax.ShapeDtypeStruct((groups, rows, width), BF16),
+            jax.ShapeDtypeStruct((2, rows, D), BF16),
+            jax.ShapeDtypeStruct((ranks, rows, width), BF16),
             jax.ShapeDtypeStruct((8, D), F32),
         ]
         + host.out_shapes(),
         compiler_params=pltpu.CompilerParams(
             vmem_limit_bytes=VMEM_LIMIT, collective_id=layer, has_side_effects=True
         ),
-    )(dy, hidden, wo, vecs, upper, ups[0], ups[1], downs[0], downs[1], *host.views(arrays))
+    )(dy, hidden, wos[0], wos[1], vec, upper, a2_all, ups[0], ups[1], downs[0], downs[1], *host.views(arrays))
 
 
 def attend_back_kernel(host, ranges, *refs):
     n = host.arrays
-    q_ref, do_ref, k_ref, v_ref, lse_ref, mask_ref = refs[:6]
-    srcs = refs[6 : 6 + n]
-    dj_ref, sums_ref = refs[6 + n : 8 + n]
-    outs = refs[8 + n : 8 + 2 * n]
-    dk_acc, dv_acc = refs[8 + 2 * n : 10 + 2 * n]
-    host.bind(srcs, outs, refs[10 + 2 * n :])
-    step = pl.program_id(0)
+    (q_ref, do_ref, k_ref, v_ref, lse_ref, mask_ref, gain_ref) = refs[:7]
+    late = refs[7:13]
+    srcs = refs[13 : 13 + n]
+    dx_ref, sums_ref, sums_qv_ref, gjoint_ref, gout_ref = refs[13 + n : 18 + n]
+    outs = refs[18 + n : 18 + 2 * n]
+    rest = refs[18 + 2 * n :]
+    dk_acc, dv_acc, dj, da_acc, core_send, core_recv, far_send, far_recv = rest[:8]
+    g_send, g_recv, dx_send, dx_recv = rest[8:12]
+    a1, w_joint, x_own, dh, branch, mixed = rest[12:18]
+    load_sems = rest[18]
+    core_sems, far_sems, pair_sems = rest[19:21], rest[21:23], rest[23:25]
+    host.bind(srcs, outs, rest[25:])
+    group = Group()
+    core, half = group.core, group.half
+    partner_core = group.device(1, 0)
     width = q_ref.shape[1]
+    length = q_ref.shape[0]
+    rows = x_own.shape[0]
     heads = width // DH
     scale = DH ** (-0.5)
 
-    @pl.when(step == 0)
-    def _():
-        host.begin()
-        dk_acc[...] = jnp.zeros_like(dk_acc)
-        dv_acc[...] = jnp.zeros_like(dv_acc)
-        sums_ref[...] = jnp.zeros_like(sums_ref)
-
-    q = q_ref[...]
-    grad = do_ref[...]
-    keys = k_ref[...]
-    values = v_ref[...]
-    mask = mask_ref[...]
-    totals = lse_ref[...]
-    d_q = jnp.zeros((BQ, width), F32)
-    for head in range(heads):
-        mine = head_lanes((BQ, width), head)
-        q_head = jnp.where(mine, q, jnp.zeros_like(q))
-        grad_head = jnp.where(mine, grad, jnp.zeros_like(grad))
-        scores = mm_nt(q_head, keys) * SCALE2 + mask
-        probs = jnp.exp2(scores - totals[:, head : head + 1])
-        d_probs = mm_nt(grad_head, values)
-        term = jnp.sum(probs * d_probs, axis=-1, keepdims=True)
-        d_scores = (probs * (d_probs - term)).astype(BF16)
-        dv_acc[...] += mm_tn(probs.astype(BF16), grad_head)
-        dk_acc[...] += mm_tn(d_scores, q_head)
-        d_q = jnp.where(mine, mm(d_scores, keys), d_q)
-        for slot, (first, last) in enumerate(ranges[:-1]):
-            if last > first and slot % heads == head:
-                pl.when(step == slot // heads)(functools.partial(host.run, first, last))
-    low = (d_q * scale).astype(BF16)
-    dj_ref[pl.ds(pl.multiple_of(step * BQ, BQ), BQ), :width] = low
-    sums_ref[0:1, :] += jnp.sum(low.astype(F32), axis=0, keepdims=True)
-
-    @pl.when(step == pl.num_programs(0) - 1)
-    def _():
-        dj_ref[:, width : 2 * width] = (dk_acc[...] * scale).astype(BF16)
-        low_v = dv_acc[...].astype(BF16)
-        dj_ref[:, 2 * width :] = low_v
-        sums_ref[1:2, :] = jnp.sum(low_v.astype(F32), axis=0, keepdims=True)
-        host.run(*ranges[-1])
-        host.finish()
-
-
-def attend_back_call(q, d_o, k, v, lse, mask, host, arrays, total, collective_id):
+    group.greet(host.dp_count)
+    host.begin()
+    loads = []
+    for i, (source, target) in enumerate(zip(late, (a1, w_joint, x_own, dh, branch, mixed))):
+        loads.append(pltpu.make_async_copy(source, target, load_sems.at[i]))
+        loads[-1].start()
+    dk_acc[...] = jnp.zeros_like(dk_acc)
+    dv_acc[...] = jnp.zeros_like(dv_acc)
+    sums_qv_ref[...] = jnp.zeros_like(sums_qv_ref)
+    sums_ref[...] = jnp.zeros_like(sums_ref)
+
+    def block(step, carry):
+        here = pl.ds(pl.multiple_of(step * BQ, BQ), BQ)
+        q = q_ref[here, :]
+        grad = do_ref[here, :]
+        totals = lse_ref[here, :]
+        d_q = jnp.zeros((BQ, width), F32)
+        for head in range(heads):
+            mine = head_lanes((BQ, width), head)
+            q_head = jnp.where(mine, q, jnp.zeros_like(q))
+            grad_head = jnp.where(mine, grad, jnp.zeros_like(grad))
+            scores = mm_nt(q_head, k_ref[...]) * SCALE2 + mask_ref[...]
+            probs = jnp.exp2(scores - totals[:, head : head + 1])
+            d_probs = mm_nt(grad_head, v_ref[...])
+            term = jnp.sum(probs * d_probs, axis=-1, keepdims=True)
+            d_scores = (probs * (d_probs - term)).astype(BF16)
+            dv_acc[...] += mm_tn(probs.astype(BF16), grad_head)
+            dk_acc[...] += mm_tn(d_scores, q_head)
+            d_q = jnp.where(mine, mm(d_scores, k_ref[...]), d_q)
+            for slot, (first, last) in enumerate(ranges[: length // BQ * heads]):
+                if last > first and slot % heads == head:
+                    pl.when(step == slot // heads)(functools.partial(host.run, first, last))
+        low = (d_q * scale).astype(BF16)
+        dj[here, :width] = low
+        sums_qv_ref[0:1, :] += jnp.sum(low.astype(F32), axis=0, keepdims=True)
+        return carry
+
+    lax.fori_loop(0, length // BQ, block, 0)
+    dj[:, width : 2 * width] = (dk_acc[...] * scale).astype(BF16)
+    low_v = dv_acc[...].astype(BF16)
+    dj[:, 2 * width :] = low_v
+    sums_qv_ref[1:2, :] = jnp.sum(low_v.astype(F32), axis=0, keepdims=True)
+
+    for load in loads:
+        load.wait()
+
+    def partial_rows(rank):
+        here = pl.ds(pl.multiple_of(rank * rows, 16), rows)
+        return mm_nt(dj[here, :], w_joint[...])
+
+    def core_copy(d):
+        return send(core_send.at[d], core_recv.at[d], core_sems, d, partner_core)
+
+    def far_copy(d):
+        return send(far_send.at[d - 1], far_recv.at[d - 1], far_sems, d - 1, group.device(0, d))
+
+    for d in [d for d in range(1, half)] + [0]:
+        core_send[d] = partial_rows(group.rank_of(1, d)).astype(BF16)
+        core_copy(d).start()
+    for d in range(1, half):
+        value = partial_rows(group.rank_of(0, d))
+        core_copy(d).wait_recv()
+        far_send[d - 1] = (value + core_recv[d].astype(F32)).astype(BF16)
+        far_copy(d).start()
+    value = partial_rows(group.rank)
+    core_copy(0).wait_recv()
+    da_acc[...] = value + core_recv[0].astype(F32)
+    tail = ranges[length // BQ * heads :]
+    host.run(*tail[0])
+
+    half_cols = D // 2
+    mine_cols = pl.ds(pl.multiple_of(core * half_cols, half_cols), half_cols)
+    other_cols = pl.ds(pl.multiple_of((1 - core) * half_cols, half_cols), half_cols)
+    g_send[...] = mm_tn(dj[...], a1[:, other_cols]).astype(BF16)
+    g_copy = send(g_send, g_recv, pair_sems, 0, partner_core)
+    g_copy.start()
+    gjoint_ref[:, core] = mm_tn(dj[...], a1[:, mine_cols]).astype(BF16).reshape(3, width, half_cols)
+    host.run(*tail[1])
+    gout_ref[...] = mm_tn(branch[...], mixed[...]).astype(BF16)
+    host.run(*tail[2])
+
+    for d in range(1, half):
+        far_copy(d).wait_recv()
+        da_acc[...] += far_recv[d - 1].astype(F32)
+    d_normed = da_acc[...]
+    normal, inverse = norm_stats(x_own[...].astype(F32))
+    sums_ref[0:1, :] = jnp.sum(d_normed * normal, axis=0, keepdims=True)
+    sums_ref[1:2, :] = jnp.sum(d_normed, axis=0, keepdims=True)
+    d_normal = d_normed * gain_ref[LN1_GAIN : LN1_GAIN + 1, :]
+    d_in = (
+        dh[...]
+        + inverse
+        * (
+            d_normal
+            - jnp.mean(d_normal, axis=-1, keepdims=True)
+            - normal * jnp.mean(d_normal * normal, axis=-1, keepdims=True)
+        )
+    ).astype(BF16)
+    dx_send[...] = d_in
+    dx_copy = send(dx_send, dx_recv, pair_sems, 1, partner_core)
+    dx_copy.start()
+    dx_ref[0] = d_in
+    host.run(*tail[3])
+    g_copy.wait()
+    gjoint_ref[:, 1 - core] = g_recv[...].reshape(3, width, half_cols)
+    dx_copy.wait()
+    dx_ref[1] = dx_recv[...]
+    for d in range(half):
+        core_copy(d).wait_send()
+    for d in range(1, half):
+        far_copy(d).wait_send()
+    host.finish()
+
+
+def attend_back_call(
+    q, d_o, k, v, lse, mask, gain, a1, w_joint, x_own, d_hidden, branch, mixed, host, arrays, total, collective_id
+):
     length, width = q.shape
-    row = lambda i: (i, 0)
-    whole = lambda i: (0, 0)
-    slots = length // BQ * (width // DH)
-    ranges = host.slots([ATT_SLOT * (i + 1) for i in range(slots)], total)
+    rows = x_own.shape[0]
+    half = host.count // 2
+    blocks = length // BQ * (width // DH)
+    times = [ATT_SLOT * (i + 1) for i in range(blocks)]
+    times += [times[-1] + extra for extra in (5.0, 10.0, 13.0, 18.0)]
+    ranges = host.slots(times, total)
+    vmem = pl.BlockSpec(memory_space=pltpu.VMEM)
+    late = (a1, w_joint, x_own, d_hidden, branch, mixed)
     return pl.pallas_call(
         functools.partial(attend_back_kernel, host, ranges),
-        grid=(length // BQ,),
-        in_specs=[
-            pl.BlockSpec((BQ, width), row),
-            pl.BlockSpec((BQ, width), row),
-            pl.BlockSpec((length, width), whole),
-            pl.BlockSpec((length, width), whole),
-            pl.BlockSpec((BQ, 128), row),
-            pl.BlockSpec((1, length), whole),
-        ]
-        + host.in_specs(),
-        out_specs=[
-            pl.BlockSpec((length, 3 * width), whole),
-            pl.BlockSpec((8, width), whole),
-        ]
-        + host.out_specs(),
+        in_specs=[vmem] * 7 + [pl.BlockSpec(memory_space=pl.ANY)] * 6 + host.in_specs(),
+        out_specs=[vmem] * 5 + host.out_specs(),
         out_shape=[
-            jax.ShapeDtypeStruct((length, 3 * width), BF16),
+            jax.ShapeDtypeStruct((2, rows, D), BF16),
+            jax.ShapeDtypeStruct((8, D), F32),
             jax.ShapeDtypeStruct((8, width), F32),
+            jax.ShapeDtypeStruct((3, 2, width, D // 2), BF16),
+            jax.ShapeDtypeStruct((D, D // 2), BF16),
         ]
         + host.out_shapes(),
-        scratch_shapes=[pltpu.VMEM((length, width), F32), pltpu.VMEM((length, width), F32)]
+        scratch_shapes=[
+            pltpu.VMEM((length, width), F32),
+            pltpu.VMEM((length, width), F32),
+            pltpu.VMEM((length, 3 * width), BF16),
+            pltpu.VMEM((rows, D), F32),
+            pltpu.VMEM((half, rows, D), BF16),
+            pltpu.VMEM((half, rows, D), BF16),
+            pltpu.VMEM((half - 1, rows, D), BF16),
+            pltpu.VMEM((half - 1, rows, D), BF16),
+            pltpu.VMEM((3 * width, D // 2), BF16),
+            pltpu.VMEM((3 * width, D // 2), BF16),
+            pltpu.VMEM((rows, D), BF16),
+            pltpu.VMEM((rows, D), BF16),
+        ]
+        + [pltpu.VMEM(t.shape, t.dtype) for t in late]
+        + [pltpu.SemaphoreType.DMA((len(late),))]
+        + dma_pair(half)
+        + dma_pair(half - 1)
+        + dma_pair(2)
         + host.scratch(),
         compiler_params=pltpu.CompilerParams(
             vmem_limit_bytes=VMEM_LIMIT, collective_id=collective_id, has_side_effects=True
         ),
-    )(q, d_o, k, v, lse, mask, *host.views(arrays))
+    )(q, d_o, k, v, lse, mask, gain, *late, *host.views(arrays))
 
 
 def swap(value, axis, mask):
@@ -927,41 +1336,8 @@
         )
         return ordered(micro, first, second, 0)
 
-    def both_vectors(value):
-        return jnp.stack([value, value])
-
-    vectors = jnp.concatenate(
-        [v[0].astype(F32) for v in (ln1_gain, ln1_bias, b_query, b_value, b_out, ln2_gain, ln2_bias, b_down, b_up)]
-    )
-    vector_pair = ordered(core, vectors, swap_core(vectors), 0)
-
-    def vector(layer, index):
-        size = FF if index == 8 else D
-        return vector_pair[layer, index * D : index * D + size]
-
-    compact = half == 2 and D // groups == DH
+    compact = half == 2
     span = half * width
-
-    def joint_of(which):
-        wide = lax.dynamic_slice_in_dim(
-            w_qkv[0].reshape(D, 3, 2, span), which, 1, 2
-        ).reshape(D, 3, span)
-        source = jnp.arange(span)[:, None]
-        target = jnp.arange(width)[None, :]
-        if compact:
-            wanted = (2 * (target // DH) + low) * DH + target % DH
-        else:
-            wanted = low * width + target
-        pick = (source == wanted).astype(BF16)
-        return lax.dot_general(
-            wide, pick, (((2,), (0,)), ((), ())), preferred_element_type=F32
-        ).astype(BF16).reshape(D, 3 * width)
-
-    def vector_of(value):
-        wide = lax.dynamic_slice_in_dim(value, core * span, span)
-        if compact:
-            return take(wide.reshape(-1, 2, DH), low, 1).reshape(width)
-        return lax.dynamic_slice_in_dim(wide, low * width, width)
 
     def vector_to(value):
         if compact:
@@ -979,45 +1355,44 @@
             return jnp.swapaxes(value, 1, 2).reshape(D, D)
         return value
 
-    joint_mine = joint_of(core)
-    joint_other = swap_core(joint_of(1 - core))
     out_mine = rank_rows(w_out[0])
-    out_other = swap_core(out_mine)
-    up_other = swap_core(w_up[0])
-    down_other = swap_core(w_down[0])
-    ups = (w_up[0], up_other)
-    downs = (w_down[0], down_other)
-
+    ups = (w_up[0], swap_core(w_up[0]))
+    downs = (w_down[0], swap_core(w_down[0]))
     bias_mask = key_bias(take(view_tokens[:, 0], micro, 0), micro == 1)
 
     saved = []
-    layer_in = own_rows(inputs)
     acts = []
     for layer in range(2):
-        sel = jnp.where(core == layer, 0, 1).astype(jnp.int32)[None]
-        w_joint = jnp.where(core == layer, joint_mine, joint_other)
-        w_proj = jnp.where(core == layer, out_mine, out_other)
-        zero = jnp.zeros((width,), F32)
-        bias = jnp.concatenate([vector_of(vector(layer, 2)), zero, vector_of(vector(layer, 3))])
-        vecs = jnp.concatenate(
-            [
-                jnp.stack([vector(layer, 4), vector(layer, 5), vector(layer, 6), vector(layer, 7)]),
-                jnp.zeros((4, D), F32),
-            ]
-        )
-        x_all = gather_rows(layer_in)
-        a1, q, k, v = qkv_call(
-            x_all, w_joint, bias[None], vector(layer, 0)[None], vector(layer, 1)[None]
-        )
-        mixed, lse = attend_call(q, k, v, bias_mask)
-        o_own = exchange(mixed.reshape(count, rows, width))
+        if layer == 0:
+            o_own, lse, a1, q, k, v, layer_in, joint_pair, out_other, vec = attend_call(
+                True,
+                0,
+                bias_mask,
+                count,
+                dp_count,
+                inputs,
+                w_qkv,
+                out_mine[None],
+                ln1_gain,
+                ln1_bias,
+                b_query,
+                b_value,
+                b_out,
+                ln2_gain,
+                ln2_bias,
+                b_down,
+                b_up,
+            )
+            outs_pair = (out_mine, out_other)
+        else:
+            o_own, lse, a1, q, k, v = attend_call(
+                False, 1, bias_mask, count, dp_count, layer_in, joint_pair[1], vec[1:2]
+            )
         hidden, a2, upper, gated, output = mlp_call(
-            sel, o_own, layer_in, w_proj, vecs, vector(layer, 8)[None], ups, downs
+            layer, o_own, layer_in, outs_pair, vec, ups, downs
         )
         acts.append(output)
-        saved.append(
-            (sel, w_joint, w_proj, vecs, layer_in, a1, q, k, v, lse, o_own, hidden, a2, upper, gated)
-        )
+        saved.append((layer_in, a1, q, k, v, lse, o_own, hidden, a2, upper, gated))
         layer_in = output
 
     dp_bits = dp_count.bit_length() - 1
@@ -1064,44 +1439,48 @@
     grads_in = []
     pending = None
     d_out = own_rows(cotangent)
+    d_out_all = joined(d_out, swap_core(d_out))
     for layer in (1, 0):
-        _, w_joint, w_proj, vecs, x_own, a1, q, k, v, lse, o_own, hidden, a2, upper, gated = saved[layer]
+        x_own, a1, q, k, v, lse, o_own, hidden, a2, upper, gated = saved[layer]
         gated_all = both_halves(gated)
         a2_all = joined(a2, swap_core(a2))
-        d_out_all = joined(d_out, swap_core(d_out))
+        o_split = o_own.reshape(2, half, rows, width)
+        flat = lambda t: jnp.swapaxes(t, 0, 1).reshape(rows, half * width)
+        o_all = joined(flat(take(o_split, core, 0)), swap_core(flat(take(o_split, 1 - core, 0))))
         g_down = mm_tn(d_out_all, gated_all).astype(BF16).reshape(groups, D // groups, FF // 2)
         host, arrays = hosted(g_down) if pending is None else hosted(*pending)
-        d_upper, g_bup, d_hidden, d_branch, d_heads, sums_two, *reduced = mlp_back_call(
-            layer, d_out, hidden, w_proj, vecs, upper, ups, downs, count, host, arrays, 32.0
+        g_up, g_bup, d_hidden, branch, d_heads, sums_two, *reduced = mlp_back_call(
+            layer, d_out, hidden, outs_pair, vec, upper, a2_all, ups, downs, count, host, arrays, 40.0
         )
         if pending is None:
             results[layer]["down"] = reduced[0]
         else:
             results[1]["out"], results[1]["joint"] = reduced
-        upper_all = both_halves(d_upper)
-        g_up = mm_tn(upper_all, a2_all).astype(BF16).reshape(groups, FF // groups // 2, D)
-        d_mixed = exchange(d_heads).reshape(LEN, width)
-        host, arrays = hosted(g_up) if pending is None else hosted(g_down)
-        d_joint, sums_qv, reduced = attend_back_call(
-            q, d_mixed, k, v, lse, bias_mask, host, arrays, 32.0, 2 + layer
+        host, arrays = hosted(g_up) if pending is None else hosted(g_down, g_up)
+        d_in, sums_one, sums_qv, g_joint, g_out, *reduced = attend_back_call(
+            q,
+            d_heads.reshape(LEN, width),
+            k,
+            v,
+            lse,
+            bias_mask,
+            vec[layer],
+            a1,
+            joint_pair[layer],
+            x_own,
+            d_hidden,
+            branch.reshape(2 * rows, D),
+            o_all,
+            host,
+            arrays,
+            42.0 if pending is None else 80.0,
+            2 + layer,
         )
-        results[layer]["up" if pending is None else "down"] = reduced
-        d_normed = mm_nt(d_joint, w_joint).astype(BF16).reshape((2,) * (low_bits + 1) + (rows, D))
-        other = swap_core(take(d_normed, 1 - core, 0))
-        mine = take(d_normed, core, 0)
-        for bit in range(low_bits):
-            total = (mine.astype(F32) + other.astype(F32)).astype(BF16)
-            dim = low_bits - 1 - bit
-            other = swap_seq(take(total, 1 - low_bit(bit), dim), bit)
-            mine = take(total, low_bit(bit), dim)
-        d_in, sums_one = norm_back_call(mine, other, x_own, d_hidden, vector(layer, 0)[None])
-        o_split = o_own.reshape(2, half, rows, width)
-        flat = lambda t: jnp.swapaxes(t, 0, 1).reshape(rows, half * width)
-        o_all = joined(flat(take(o_split, core, 0)), swap_core(flat(take(o_split, 1 - core, 0))))
-        branch_all = joined(d_branch, swap_core(d_branch))
-        g_out = mm_tn(branch_all, o_all).astype(BF16).reshape(groups, D // groups, D // 2)
-        g_joint = mm_tn(d_joint, a1).astype(BF16).reshape(3, width, 2, D // 2)
-        g_joint = ordered(core, take(g_joint, core, 2), swap_core(take(g_joint, 1 - core, 2)), 1)
+        if pending is None:
+            results[layer]["up"] = reduced[0]
+        else:
+            results[layer]["down"], results[layer]["up"] = reduced
+        g_out = g_out.reshape(groups, D // groups, D // 2)
         if compact:
             g_joint = g_joint.reshape(groups // 2, 3 * D // groups, D // 2)
         else:
@@ -1112,10 +1491,10 @@
         if pending is None:
             pending = (g_out, g_joint)
         else:
-            host, arrays = hosted(g_up, g_out, g_joint)
-            results[layer]["up"], results[layer]["out"], results[layer]["joint"] = reduce_call(
-                host, arrays, 4
-            )
+            host, arrays = hosted(g_out, g_joint)
+            results[layer]["out"], results[layer]["joint"] = reduce_call(host, arrays, 4)
+        d_out = d_in[0]
+        d_out_all = d_in.reshape(2 * rows, D)
         smalls.append(
             jnp.concatenate(
                 [
@@ -1135,8 +1514,7 @@
                 axis=1,
             )
         )
-        grads_in.append(d_in)
-        d_out = d_in
+        grads_in.append(d_out)
 
     grads_in = grads_in[::-1]
     small_pair = jnp.stack(smalls[::-1])

time: 735 us -> 582 us (0.79)
  the two profiles are of different devices: /device:TPU:9 before, /device:TPU:1 now
where the time goes in v3:
time: 582 us; the launch traced here: 572 us
  Pallas kernels  451 us (77%)
  local copies, waits for them, and re-layouts  35.1 us (6%)
  starting transfers between devices  31.6 us (5%)
  waiting for transfers between devices  24.6 us (4%)
  other arithmetic  17.9 us (3%)
  matrix products  10.2 us (2%)
    pallas_call x2, Pallas kernels, attend_back_call(): pl.pallas_call(functools.partial(attend_back_kernel, host, ranges), in_sp...  166 us
    pallas_call x2, Pallas kernels, mlp_back_call(): pl.pallas_call(functools.partial(mlp_back_kernel, layer, host, ranges), g...  121 us
    pallas_call x2, Pallas kernels, attend_call(): pl.pallas_call(functools.partial(attend_kernel, first, layer, dp_count),...  87.6 us
    pallas_call x1, Pallas kernels, reduce_call(): pl.pallas_call(functools.partial(reduce_kernel, host), in_specs=host.in_s...  39.1 us
    pallas_call x2, Pallas kernels, mlp_call(): pl.pallas_call(functools.partial(mlp_kernel, layer), grid=(NCH,), in_spec...  38 us
    ppermute x4, waiting for transfers between devices, to_section(): lax.ppermute(own, ('section', 'seq'), [(count + z, layer * count + (z ^ h...  17.7 us
    ppermute x4, starting transfers between devices, to_section(): lax.ppermute(own, ('section', 'seq'), [(count + z, layer * count + (z ^ h...  15.5 us
  transfers between devices with their start and end apart: 21, of which 2 were waited for; matrix products, arithmetic and copies ran while one was open for 10% of the time, Pallas kernels for 79%

profile of v3, /device:TPU:1, one launch (start us, length us, event | category | flops | bytes accessed | tf_op | source)
XLA Modules:
  0.0 572.1 jit_solution(15093156499603285680)
XLA Ops:
  1.2 2.0 dynamic-slice_bitcast_fusion.4
  3.2 5.3 collective-permute-start.5
  8.5 3.2 copy.57
  12.5 49.1 %shard_map.271 = (bf16[4,320,256]{2,1,0:T(8,128)(2,1)}, f32[1280,128]{1,0:T(8,128)}, bf16[1280,1024]{1,0:T(8,128)(2,1)}, bf16[1280,256]{1,0:T(8,128)(2,1)}, bf16...) custom-call(bf16[2,1,320,1024]{3,2,1,0:T(8,128)(2,1)} %refs_0_.1, ...), custom_call_target="tpu_custom_call" | custom-call | flops 40000000000 | bytes 20971520 | tf_op jit(solution)/shard_map/pallas_call | solution.py:724
  61.6 2.0 constant_dynamic-slice_fusion.4
  67.5 1.9 slice_bitcast_fusion
  69.5 19.2 %shard_map.272 = (f32[320,1024]{1,0:T(8,128)}, bf16[320,1024]{1,0:T(8,128)(2,1)}, f32[320,4096]{1,0:T(8,128)}, bf16[2,320,2048]{2,1,0:T(8,128)(2,1)}, bf16[320,1024]{1,0:T(8,128)(2,1)}) custom-call(bf16[4,320,256]{2,1,0:T(8,128)(2,1)} %get-tuple-element.71.o_ref, bf16[320,1024]{1,0:T(8,128)(2,1)} %get-tuple-element.72.x_ref.refs_9_, ...), custom_call_target="tpu_custom_call" | custom-call | flops 6039797760 | bytes 31457280 | tf_op jit(solution)/shard_map/pallas_call | solution.py:815
  88.7 38.4 %shard_map.273 = (bf16[4,320,256]{2,1,0:T(8,128)(2,1)}, f32[1280,128]{1,0:T(8,128)}, bf16[1280,1024]{1,0:T(8,128)(2,1)}, bf16[1280,256]{1,0:T(8,128)(2,1)}, bf16...) custom-call(bf16[320,1024]{1,0:T(8,128)(2,1)} %get-tuple-element.75.refs_0_.x_ref.refs_9_, ...), custom_call_target="tpu_custom_call" | custom-call | flops 40000000000 | bytes 20971520 | tf_op jit(solution)/shard_map/pallas_call | solution.py:724
  129.2 18.8 %shard_map.274 = (f32[320,1024]{1,0:T(8,128)}, bf16[320,1024]{1,0:T(8,128)(2,1)}, f32[320,4096]{1,0:T(8,128)}, bf16[2,320,2048]{2,1,0:T(8,128)(2,1)}, bf16[320,1024]{1,0:T(8,128)(2,1)}) custom-call(bf16[4,320,256]{2,1,0:T(8,128)(2,1)} %get-tuple-element.77.o_ref, bf16[320,1024]{1,0:T(8,128)(2,1)} %get-tuple-element.75.refs_0_.x_ref.refs_9_, ...), custom_call_target="tpu_custom_call" | custom-call | flops 6039797760 | bytes 31457280 | tf_op jit(solution)/shard_map/pallas_call | solution.py:815
  148.1 2.0 dynamic-slice_bitcast_fusion.3
  152.1 1.9 pad_maximum_fusion.5.refs_12_
  155.7 3.2 collective-permute-start.4
  158.9 1.3 collective-permute-start.2
  164.3 17.7 %collective-permute-done.4 = bf16[320,1024]{1,0:T(8,128)(2,1)S(1)} collective-permute-done((bf16[320,1024]{1,0:T(8,128)(2,1)S(1)}, bf16[320,1024]{1,0:T(8,128)(2,1)S(1)}, u32[]{:S(2)}, u32[]{:S(2)}) %collective-permute-start.4) | collective-permute-done | bytes 655392 | tf_op jit(solution)/shard_map/ppermute | solution.py:1332
  182.0 1.5 fusion.6
  183.5 5.1 convolution_convert_fusion.1
  188.6 68.3 %shard_map.275 = (bf16[16,128,1024]{2,1,0:T(8,128)(2,1)}, f32[1,4096]{1,0:T(1,128)}, f32[320,1024]{1,0:T(8,128)}, bf16[2,320,1024]{2,1,0:T(8,128)(2,1)}, bf16[4,...) custom-call(bf16[320,1024]{1,0:T(8,128)(2,1)} %copy-done.9, ...), custom_call_target="tpu_custom_call" | custom-call | tf_op jit(solution)/shard_map/pallas_call | solution.py:985
  256.9 71.7 %shard_map.276 = (bf16[2,320,1024]{2,1,0:T(8,128)(2,1)}, f32[8,1024]{1,0:T(8,128)}, f32[8,256]{1,0:T(8,128)}, bf16[3,2,256,512]{3,2,1,0:T(8,128)(2,1)}, bf16[102...) custom-call(bf16[1280,256]{1,0:T(8,128)(2,1)} %get-tuple-element.80.refs_0_, bf16[1280,256]{1,0:T(8,128)(2,1)} %bitcast.199, ...), custom_call_target="tpu_custom_call" | custom-call | tf_op jit(solution)/shard_map/pallas_call | solution.py:1189
  328.6 2.1 slice_bitcast_fusion.2.refs_0_
  332.0 2.4 collective-permute-start.15
  334.3 5.1 convolution_convert_fusion
  339.4 52.5 %shard_map.277 = (bf16[16,128,1024]{2,1,0:T(8,128)(2,1)}, f32[1,4096]{1,0:T(1,128)}, f32[320,1024]{1,0:T(8,128)}, bf16[2,320,1024]{2,1,0:T(8,128)(2,1)}, bf16[4,...) custom-call(bf16[320,1024]{1,0:T(8,128)(2,1)} %slice_bitcast_fusion.2.refs_0_, ...), custom_call_target="tpu_custom_call" | custom-call | tf_op jit(solution)/shard_map/pallas_call | solution.py:985
  391.9 93.8 %shard_map.278 = (bf16[2,320,1024]{2,1,0:T(8,128)(2,1)}, f32[8,1024]{1,0:T(8,128)}, f32[8,256]{1,0:T(8,128)}, bf16[3,2,256,512]{3,2,1,0:T(8,128)(2,1)}, bf16[102...) custom-call(bf16[1280,256]{1,0:T(8,128)(2,1)} %get-tuple-element.79.refs_0_, ...), custom_call_target="tpu_custom_call" | custom-call | tf_op jit(solution)/shard_map/pallas_call | solution.py:1189
  493.4 1.4 collective-permute-start.16
  495.1 39.1 %shard_map.279 = (f32[2,64,512]{2,1,0:T(8,128)}, f32[2,256,512]{2,1,0:T(8,128)}) custom-call(bf16[2,2,2,2,64,512]{5,4,3,2,1,0:T(8,128)(2,1)} %bitcast.197, bf16[2,2,2,192,512]{4,3,2,1,0:T(8,128)(2,1)} %bitcast.187), custom_call_target="tpu_custom_call" | custom-call | tf_op jit(solution)/shard_map/pallas_call | solution.py:395
  536.2 2.3 slice_bitcast_fusion.4
  539.7 8.6 %collective-permute-start.13 = (bf16[320,1024]{1,0:T(8,128)(2,1)}, bf16[320,1024]{1,0:T(8,128)(2,1)}, u32[]{:S(2)}, u32[]{:S(2)}) collective-permute-start(bf16[320,1024]{1,0:T(8,128)(2,1)} %get-tuple-element.201), channel_id=1, source_target_pairs={{16,2},{17,3},{18,0},{19,1},{20,6},{21,7},{22,4},{23,5},{24,10},{2... | collective-permute-start | bytes 1966088 | tf_op jit(solution)/shard_map/ppermute | solution.py:1332
  548.5 6.9 %collective-permute-done.19 = f32[2,768]{1,0:T(2,128)S(1)} collective-permute-done((f32[2,768]{1,0:T(2,128)S(1)}, f32[2,768]{1,0:T(2,128)S(1)}, u32[]{:S(2)}, u32[]{:S(2)}) %collective-permute-start.19) | collective-permute-done | bytes 6176 | tf_op jit(solution)/shard_map/ppermute | solution.py:1229
  555.4 2.8 collective-permute-start.20
  559.9 1.8 broadcast_in_dim_reshape.19
  565.4 1.6 broadcast_in_dim_reshape.16
  568.3 3.4 fusion.10
  (168 shorter events, 34.0 us)
Async XLA Ops:
  0.6 11.1 %copy-start = (s32[2,1,6]{2,1,0:T(1,128)S(1)}, s32[2,1,6]{2,1,0:T(1,128)}, u32[]{:S(2)}) copy-start(s32[2,1,6]{2,1,0:T(1,128)} %param.18) | copy-start | bytes 148
  0.7 68.8 %collective-permute-start = (bf16[1024,4096]{1,0:T(8,128)(2,1)}, bf16[1024,4096]{1,0:T(8,128)(2,1)}, u32[]{:S(2)}, u32[]{:S(2)}) collective-permute-start(bf16[1024,4096]{1,0:T(8,128)(2,1)} %bitcast.156), channel_id=1, source_target_pairs={{0,16},{16,0},{1,17},{17,1},{2,18},{18,2},{3,19},{19,3},{4,20},{20... | collective-permute-start | bytes 25165832 | tf_op jit(solution)/shard_map/ppermute | solution.py:1229
  0.8 68.7 %collective-permute-start.1 = (bf16[4096,1024]{1,0:T(8,128)(2,1)}, bf16[4096,1024]{1,0:T(8,128)(2,1)}, u32[]{:S(2)}, u32[]{:S(2)}) collective-permute-start(bf16[4096,1024]{1,0:T(8,128)(2,1)} %bitcast.161), channel_id=1, source_target_pairs={{0,16},{16,0},{1,17},{17,1},{2,18},{18,2},{3,19},{19,3},{4,20},{20... | collective-permute-start | bytes 25165832 | tf_op jit(solution)/shard_map/ppermute | solution.py:1229
  3.2 147.6 %collective-permute-start.5 = (bf16[320,1024]{1,0:T(8,128)(2,1)}, bf16[320,1024]{1,0:T(8,128)(2,1)}, u32[]{:S(2)}, u32[]{:S(2)}) collective-permute-start(bf16[320,1024]{1,0:T(8,128)(2,1)} %dynamic-slice_bitcast_fusion.4), channel_id=1, source_target_pairs={{16,18},{17,19},{18,16},{19,17},{20,22},{21,23},{22,20},{23,21},{2... | collective-permute-start | bytes 1966088 | tf_op jit(solution)/shard_map/ppermute | solution.py:1299
  61.6 5.9 %copy-start.5 = (bf16[2,1024,768]{2,1,0:T(8,128)(2,1)S(1)}, bf16[2,1024,768]{2,1,0:T(8,128)(2,1)}, u32[]{:S(2)}) copy-start(bf16[2,1024,768]{2,1,0:T(8,128)(2,1)} %get-tuple-element.76) | copy-start | bytes 9437188
  64.7 86.0 %collective-permute-start.11 = (bf16[320,512]{1,0:T(8,128)(2,1)}, bf16[320,512]{1,0:T(8,128)(2,1)}, u32[]{:S(2)}, u32[]{:S(2)}) collective-permute-start(bf16[320,512]{1,0:T(8,128)(2,1)} %bitcast.106), channel_id=1, source_target_pairs={{0,16},{16,0},{1,17},{17,1},{2,18},{18,2},{3,19},{19,3},{4,20},{20... | collective-permute-start | bytes 983048 | tf_op jit(solution)/shard_map/ppermute | solution.py:1229
  128.6 27.1 %collective-permute-start.9 = (bf16[320,512]{1,0:T(8,128)(2,1)S(1)}, bf16[320,512]{1,0:T(8,128)(2,1)S(1)}, u32[]{:S(2)}, u32[]{:S(2)}) collective-permute-start(bf16[320,512]{1,0:T(8,128)(2,1)S(1)} %bitcast.208), channel_id=1, source_target_pairs={{0,16},{16,0},{1,17},{17,1},{2,18},{18,2},{3,19},{19,3},{4,20},{20... | collective-permute-start | bytes 983048 | tf_op jit(solution)/shard_map/ppermute | solution.py:1229
  148.0 10.9 %collective-permute-start.6 = (bf16[320,1024]{1,0:T(8,128)(2,1)}, bf16[320,1024]{1,0:T(8,128)(2,1)S(1)}, u32[]{:S(2)}, u32[]{:S(2)}) collective-permute-start(bf16[320,1024]{1,0:T(8,128)(2,1)} %get-tuple-element.83), channel_id=1, source_target_pairs={{0,16},{16,0},{1,17},{17,1},{2,18},{18,2},{3,19},{19,3},{4,20},{20... | collective-permute-start | bytes 1966088 | tf_op jit(solution)/shard_map/ppermute | solution.py:1229
  150.2 33.3 %collective-permute-start.8 = (bf16[320,2048]{1,0:T(8,128)(2,1)S(1)}, bf16[320,2048]{1,0:T(8,128)(2,1)S(1)}, u32[]{:S(2)}, u32[]{:S(2)}) collective-permute-start(bf16[320,2048]{1,0:T(8,128)(2,1)S(1)} %get-tuple-element.199), channel_id=1, source_target_pairs={{0,16},{16,0},{1,17},{17,1},{2,18},{18,2},{3,19},{19,3},{4,20},{20... | collective-permute-start | bytes 3932168 | tf_op jit(solution)/shard_map/ppermute | solution.py:1229
  150.7 9.8 %collective-permute-start.10 = (bf16[320,1024]{1,0:T(8,128)(2,1)S(1)}, bf16[320,1024]{1,0:T(8,128)(2,1)S(1)}, u32[]{:S(2)}, u32[]{:S(2)}) collective-permute-start(bf16[320,1024]{1,0:T(8,128)(2,1)S(1)} %copy-done.15), channel_id=1, source_target_pairs={{0,16},{16,0},{1,17},{17,1},{2,18},{18,2},{3,19},{19,3},{4,20},{20... | collective-permute-start | bytes 1966088 | tf_op jit(solution)/shard_map/ppermute | solution.py:1229
  150.8 9.7 %collective-permute-start.3 = (bf16[320,1024]{1,0:T(8,128)(2,1)S(1)}, bf16[320,1024]{1,0:T(8,128)(2,1)S(1)}, u32[]{:S(2)}, u32[]{:S(2)}) collective-permute-start(bf16[320,1024]{1,0:T(8,128)(2,1)S(1)} %copy-done.24), channel_id=1, source_target_pairs={{0,16},{1,17},{2,18},{3,19},{4,20},{5,21},{6,22},{7,23},{8,24},{9,... | collective-permute-start | bytes 1966088 | tf_op jit(solution)/shard_map/ppermute | solution.py:1329
  154.0 6.3 %copy-start.7 = (bf16[2,320,2048]{2,1,0:T(8,128)(2,1)S(1)}, bf16[2,320,2048]{2,1,0:T(8,128)(2,1)}, u32[]{:S(2)}) copy-start(bf16[2,320,2048]{2,1,0:T(8,128)(2,1)} %get-tuple-element.106) | copy-start | bytes 7864324
  155.3 28.2 %copy-start.9 = (bf16[320,1024]{1,0:T(8,128)(2,1)}, bf16[320,1024]{1,0:T(8,128)(2,1)S(1)}, u32[]{:S(2)}) copy-start(bf16[320,1024]{1,0:T(8,128)(2,1)S(1)} %bitcast_select_fusion.refs_0_) | copy-start | bytes 1966084
  155.7 26.3 %collective-permute-start.4 = (bf16[320,1024]{1,0:T(8,128)(2,1)S(1)}, bf16[320,1024]{1,0:T(8,128)(2,1)S(1)}, u32[]{:S(2)}, u32[]{:S(2)}) collective-permute-start(bf16[320,1024]{1,0:T(8,128)(2,1)S(1)} %copy-done.24), channel_id=1, source_target_pairs={{16,18},{17,19},{18,16},{19,17},{20,22},{21,23},{22,20},{23,21},{2... | collective-permute-start | bytes 1966088 | tf_op jit(solution)/shard_map/ppermute | solution.py:1332
  158.9 23.1 %collective-permute-start.2 = (bf16[320,1024]{1,0:T(8,128)(2,1)S(1)}, bf16[320,1024]{1,0:T(8,128)(2,1)S(1)}, u32[]{:S(2)}, u32[]{:S(2)}) collective-permute-start(bf16[320,1024]{1,0:T(8,128)(2,1)S(1)} %copy-done.2), channel_id=1, source_target_pairs={{16,2},{17,3},{18,0},{19,1},{20,6},{21,7},{22,4},{23,5},{24,10},{2... | collective-permute-start | bytes 1966088 | tf_op jit(solution)/shard_map/ppermute | solution.py:1332
  160.5 23.0 %collective-permute-start.7 = (bf16[320,1024]{1,0:T(8,128)(2,1)S(1)}, bf16[320,1024]{1,0:T(8,128)(2,1)S(1)}, u32[]{:S(2)}, u32[]{:S(2)}) collective-permute-start(bf16[320,1024]{1,0:T(8,128)(2,1)S(1)} %bitcast_select_fusion.refs_0_), channel_id=1, source_target_pairs={{0,16},{16,0},{1,17},{17,1},{2,18},{18,2},{3,19},{19,3},{4,20},{20... | collective-permute-start | bytes 1966088 | tf_op jit(solution)/shard_map/ppermute | solution.py:1229
  160.5 173.8 %collective-permute-start.12 = (bf16[320,2048]{1,0:T(8,128)(2,1)S(1)}, bf16[320,2048]{1,0:T(8,128)(2,1)S(1)}, u32[]{:S(2)}, u32[]{:S(2)}) collective-permute-start(bf16[320,2048]{1,0:T(8,128)(2,1)S(1)} %get-tuple-element.197), channel_id=1, source_target_pairs={{0,16},{16,0},{1,17},{17,1},{2,18},{18,2},{3,19},{19,3},{4,20},{20... | collective-permute-start | bytes 3932168 | tf_op jit(solution)/shard_map/ppermute | solution.py:1229
  328.6 5.8 %copy-start.17 = (bf16[2,320,1024]{2,1,0:T(8,128)(2,1)S(1)}, bf16[2,320,1024]{2,1,0:T(8,128)(2,1)}, u32[]{:S(2)}) copy-start(bf16[2,320,1024]{2,1,0:T(8,128)(2,1)} %get-tuple-element.93) | copy-start | bytes 3932164
  330.7 237.6 %collective-permute-start.14 = (bf16[320,1024]{1,0:T(8,128)(2,1)}, bf16[320,1024]{1,0:T(8,128)(2,1)}, u32[]{:S(2)}, u32[]{:S(2)}) collective-permute-start(bf16[320,1024]{1,0:T(8,128)(2,1)} %slice_bitcast_fusion.2.refs_0_), channel_id=1, source_target_pairs={{0,16},{1,17},{2,18},{3,19},{4,20},{5,21},{6,22},{7,23},{8,24},{9,... | collective-permute-start | bytes 1966088 | tf_op jit(solution)/shard_map/ppermute | solution.py:1329
  332.0 236.3 %collective-permute-start.15 = (bf16[320,1024]{1,0:T(8,128)(2,1)}, bf16[320,1024]{1,0:T(8,128)(2,1)}, u32[]{:S(2)}, u32[]{:S(2)}) collective-permute-start(bf16[320,1024]{1,0:T(8,128)(2,1)} %slice_bitcast_fusion.2.refs_0_), channel_id=1, source_target_pairs={{16,18},{17,19},{18,16},{19,17},{20,22},{21,23},{22,20},{23,21},{2... | collective-permute-start | bytes 1966088 | tf_op jit(solution)/shard_map/ppermute | solution.py:1332
  391.9 93.9 %copy-start.14 = (f32[2,64,2048]{2,1,0:T(8,128)S(1)}, f32[2,64,2048]{2,1,0:T(8,128)}, u32[]{:S(2)}) copy-start(f32[2,64,2048]{2,1,0:T(8,128)} %get-tuple-element.126) | copy-start | bytes 3145732
  486.0 6.4 %copy-start.21 = (f32[1,4096]{1,0:T(1,128)S(1)}, f32[1,4096]{1,0:T(1,128)}, u32[]{:S(2)}) copy-start(f32[1,4096]{1,0:T(1,128)} %get-tuple-element.112) | copy-start | bytes 49156
  486.0 8.9 %copy-start.12 = (f32[2,128,1024]{2,1,0:T(8,128)S(1)}, f32[2,128,1024]{2,1,0:T(8,128)}, u32[]{:S(2)}) copy-start(f32[2,128,1024]{2,1,0:T(8,128)} %get-tuple-element.124) | copy-start | bytes 3145732
  493.4 42.1 %collective-permute-start.16 = (f32[16,768]{1,0:T(8,128)S(1)}, f32[16,768]{1,0:T(8,128)S(1)}, u32[]{:S(2)}, u32[]{:S(2)}) collective-permute-start(f32[16,768]{1,0:T(8,128)S(1)} %fusion.15), channel_id=1, source_target_pairs={{0,16},{16,0},{1,17},{17,1},{2,18},{18,2},{3,19},{19,3},{4,20},{20... | collective-permute-start | bytes 147464 | tf_op jit(solution)/shard_map/ppermute | solution.py:1229
  495.1 39.1 %copy-start.13 = (f32[2,256,512]{2,1,0:T(8,128)S(1)}, f32[2,256,512]{2,1,0:T(8,128)}, u32[]{:S(2)}) copy-start(f32[2,256,512]{2,1,0:T(8,128)} %get-tuple-element.120) | copy-start | bytes 3145732
  535.6 2.9 collective-permute-start.17
  538.5 9.8 %copy-start.18 = (f32[2,64,512]{2,1,0:T(8,128)S(1)}, f32[2,64,512]{2,1,0:T(8,128)}, u32[]{:S(2)}) copy-start(f32[2,64,512]{2,1,0:T(8,128)} %get-tuple-element.122) | copy-start | bytes 786436
  538.5 9.9 %copy-start.19 = (f32[2,64,512]{2,1,0:T(8,128)S(1)}, f32[2,64,512]{2,1,0:T(8,128)}, u32[]{:S(2)}) copy-start(f32[2,64,512]{2,1,0:T(8,128)} %get-tuple-element.121) | copy-start | bytes 786436
  538.6 9.7 %collective-permute-start.18 = (f32[2,2,768]{2,1,0:T(2,128)S(1)}, f32[2,2,768]{2,1,0:T(2,128)S(1)}, u32[]{:S(2)}, u32[]{:S(2)}) collective-permute-start(f32[2,2,768]{2,1,0:T(2,128)S(1)} %dynamic-slice_bitcast_fusion.6), channel_id=1, source_target_pairs={{0,8},{4,12},{8,0},{12,4},{1,9},{5,13},{9,1},{13,5},{2,10},{6,14},... | collective-permute-start | bytes 36872 | tf_op jit(solution)/shard_map/ppermute | solution.py:1229
  539.7 28.6 %collective-permute-start.13 = (bf16[320,1024]{1,0:T(8,128)(2,1)}, bf16[320,1024]{1,0:T(8,128)(2,1)}, u32[]{:S(2)}, u32[]{:S(2)}) collective-permute-start(bf16[320,1024]{1,0:T(8,128)(2,1)} %get-tuple-element.201), channel_id=1, source_target_pairs={{16,2},{17,3},{18,0},{19,1},{20,6},{21,7},{22,4},{23,5},{24,10},{2... | collective-permute-start | bytes 1966088 | tf_op jit(solution)/shard_map/ppermute | solution.py:1332
  548.3 7.0 %collective-permute-start.19 = (f32[2,768]{1,0:T(2,128)S(1)}, f32[2,768]{1,0:T(2,128)S(1)}, u32[]{:S(2)}, u32[]{:S(2)}) collective-permute-start(f32[2,768]{1,0:T(2,128)S(1)} %bitcast.225), channel_id=1, source_target_pairs={{0,1},{1,0},{2,3},{3,2},{4,5},{5,4},{6,7},{7,6},{8,9},{9,8},{10,11... | collective-permute-start | bytes 18440 | tf_op jit(solution)/shard_map/ppermute | solution.py:1229
  555.4 11.6 %collective-permute-start.20 = (f32[768]{0:T(1024)S(1)}, f32[768]{0:T(1024)S(1)}, u32[]{:S(2)}, u32[]{:S(2)}) collective-permute-start(f32[768]{0:T(1024)S(1)} %get-tuple-element.192), channel_id=1, source_target_pairs={{0,2},{1,3},{2,0},{3,1},{4,6},{5,7},{6,4},{7,5},{8,10},{9,11},{10,... | collective-permute-start | bytes 9224 | tf_op jit(solution)/shard_map/ppermute | solution.py:1229
  (14 other events, 41.4 us)

commit v4 on v3

v4 whole, which is shorter than its diff:
```python
import functools
import math

import jax
import jax.numpy as jnp
from jax import lax
from jax.experimental import pallas as pl
from jax.experimental.pallas import tpu as pltpu
from jax.sharding import PartitionSpec as P

D = 1024
H = 16
DH = 64
FF = 4096
VIEWS = 6
TRI = 512
VSLOT = 128
MICRO = 2
LEN = 1280
BQ = 256
NCH = 8
FC = FF // NCH
SCALE2 = DH ** (-0.5) * math.log2(math.e)
F32 = jnp.float32
BF16 = jnp.bfloat16
VMEM_LIMIT = 56 * 2**20


def params():
    return pltpu.CompilerParams(vmem_limit_bytes=VMEM_LIMIT)


def mm(a, b):
    return lax.dot_general(a, b, (((1,), (0,)), ((), ())), preferred_element_type=F32)


def mm_nt(a, b):
    return lax.dot_general(a, b, (((1,), (1,)), ((), ())), preferred_element_type=F32)


def mm_tn(a, b):
    return lax.dot_general(a, b, (((0,), (0,)), ((), ())), preferred_element_type=F32)


def norm_stats(values):
    average = jnp.mean(values, axis=-1, keepdims=True)
    centered = values - average
    variance = jnp.mean(centered * centered, axis=-1, keepdims=True)
    inverse = lax.rsqrt(variance + 1e-05)
    return centered * inverse, inverse


def head_lanes(shape, head):
    lane = lax.broadcasted_iota(jnp.int32, shape, 1)
    return (lane >= head * DH) & (lane < (head + 1) * DH)


def shards_of():
    return lax.axis_size("dp") * lax.axis_size("seq")


def split_halves(value, unit, core, mine, other, step):
    for at in range(0, value.shape[1] // unit, 2):
        even = value[:, at * unit : (at + 1) * unit]
        odd = value[:, (at + 1) * unit : (at + 2) * unit]
        cols = slice(at // 2 * unit, (at // 2 + 1) * unit)
        mine[step, :, cols] = jnp.where(core == 0, even, odd)
        other[step, :, cols] = jnp.where(core == 0, odd, even)


GELU_A = math.sqrt(2.0 / math.pi)
GELU_B = 0.044715


MESH_AXES = ("dp", "seq")


def axis_bits(dp_count, count):
    bits = []
    for axis, size in (("dp", dp_count), ("seq", count)):
        mask = size // 2
        while mask:
            bits.append((axis, mask))
            mask //= 2
    return bits


def stream_orders(dp_count, count):
    dp_bits = dp_count.bit_length() - 1
    seq_bits = count.bit_length() - 1
    dp_dims = list(range(dp_bits))
    seq_dims = list(range(dp_bits, dp_bits + seq_bits))[::-1]
    return (
        dp_dims[::-1] + seq_dims,
        dp_dims + seq_dims,
        seq_dims[:1] + dp_dims + seq_dims[1:],
        seq_dims[:1] + dp_dims[::-1] + seq_dims[1:],
    )


def my_bit(axis, mask):
    return lax.rem(lax.div(lax.axis_index(axis), mask), 2)


def partner(axis, mask):
    return lax.axis_index(axis) + mask * (1 - 2 * my_bit(axis, mask))


def greet(bits):
    barrier = pltpu.get_barrier_semaphore()
    for axis, mask in bits:
        pl.semaphore_signal(
            barrier,
            inc=1,
            device_id={axis: partner(axis, mask)},
            device_id_type=pl.DeviceIdType.MESH,
        )
    pl.semaphore_wait(barrier, len(bits))


class Reducer:
    def __init__(self, bits, order, src, cols, out, rows, compact, buffers, sems):
        self.bits, self.order, self.src, self.cols = bits, order, src, cols
        self.out, self.out_cols, self.buffers, self.sems = out, cols, buffers, sems
        self.count, self.rows, self.compact = len(bits), rows, compact

    @staticmethod
    def scratch(count, rows, width, dtype):
        shapes = [pltpu.VMEM((2,) * (count - 1) + (rows, width), dtype)]
        for stage in range(count):
            shapes.append(pltpu.VMEM((2,) * (count - 1 - stage) + (rows, width), dtype))
        shapes += [
            pltpu.SemaphoreType.DMA((count + 2,)),
            pltpu.SemaphoreType.DMA((count + 2,)),
            pltpu.SemaphoreType.DMA,
        ]
        return shapes

    def place(self, stage):
        left = [d for d in range(self.count) if d not in self.order[:stage]]
        dim = self.order[stage]
        return left, left.index(dim), self.bits[dim]

    def cut(self, stage, index):
        left, at, _ = self.place(stage)
        where = [slice(None)] * len(left)
        where[at] = index
        return tuple(where)

    def source(self, stage):
        if stage == 0:
            return self.src
        return self.buffers[0] if stage == 1 else self.buffers[stage]

    def copy(self, stage):
        axis, mask = self.place(stage)[2]
        where = self.cut(stage, 1 - my_bit(axis, mask))
        if stage == 0:
            where = where + (slice(None), pl.ds(*self.cols))
        return pltpu.make_async_remote_copy(
            src_ref=self.source(stage).at[where],
            dst_ref=self.buffers[stage + 1],
            send_sem=self.sems[0].at[stage],
            recv_sem=self.sems[1].at[stage],
            device_id={axis: partner(axis, mask)},
            device_id_type=pl.DeviceIdType.MESH,
        )

    def load(self):
        axis, mask = self.place(0)[2]
        where = self.cut(0, my_bit(axis, mask)) + (slice(None), pl.ds(*self.cols))
        return pltpu.make_async_copy(self.src.at[where], self.buffers[0], self.sems[2])

    def share(self):
        core = lax.axis_index("section")
        return pltpu.make_async_remote_copy(
            src_ref=self.out.at[core, :, pl.ds(*self.out_cols)],
            dst_ref=self.out.at[core, :, pl.ds(*self.out_cols)],
            send_sem=self.sems[0].at[self.count],
            recv_sem=self.sems[1].at[self.count],
            device_id={"section": 1 - core},
            device_id_type=pl.DeviceIdType.MESH,
        )

    def trade(self):
        third = self.rows // 3
        core = lax.axis_index("section")
        bit = lax.rem(lax.axis_index("seq"), 2)
        row = pl.multiple_of((1 - bit) * 2 * third, third)
        return pltpu.make_async_remote_copy(
            src_ref=self.out.at[core, pl.ds(row, third), pl.ds(*self.out_cols)],
            dst_ref=self.out.at[core, pl.ds(self.rows, third), pl.ds(*self.out_cols)],
            send_sem=self.sems[0].at[self.count + 1],
            recv_sem=self.sems[1].at[self.count + 1],
            device_id={"seq": partner("seq", 1)},
            device_id_type=pl.DeviceIdType.MESH,
        )

    def begin(self):
        self.copy(0).start()
        self.load().start()

    def step(self, stage):
        left, at, (axis, mask) = self.place(stage)
        bit = my_bit(axis, mask)
        if stage == 0:
            self.load().wait()
        self.copy(stage).wait_recv()
        got = self.buffers[stage + 1]
        rows = got.shape[-2]
        chunk = rows
        while chunk * got.shape[-1] > 65536 and chunk % 32 == 0:
            chunk //= 2
        per = rows // chunk
        last = stage == self.count - 1
        core = lax.axis_index("section")
        total = 2 ** (len(left) - 1)

        def body(i, carry):
            flat = lax.div(i, per)
            row = pl.multiple_of(lax.rem(i, per) * chunk, chunk)
            index = []
            for j in range(len(left) - 1):
                index.append(lax.rem(lax.div(flat, 2 ** (len(left) - 2 - j)), 2))
            there = tuple(index) + (pl.ds(row, chunk), slice(None))
            if stage == 0:
                mine = self.buffers[0][there]
            else:
                own = index[:at] + [bit] + index[at:]
                mine = self.source(stage)[tuple(own) + (pl.ds(row, chunk), slice(None))]
            value = mine.astype(F32) + got[there].astype(F32)
            if last:
                self.out[core, pl.ds(row, chunk), pl.ds(*self.out_cols)] = value
            elif stage == 0:
                self.buffers[0][there] = value.astype(got.dtype)
            else:
                got[there] = value.astype(got.dtype)
            return carry

        lax.fori_loop(0, total * per, body, 0)
        if not last:
            self.copy(stage + 1).start()
        elif self.compact:
            self.trade().start()
        else:
            self.share().start()

    def tail(self):
        if self.compact:
            self.trade().wait()
            self.share().start()

    def finish(self):
        for stage in range(self.count):
            self.copy(stage).wait_send()
        self.share().wait()


def part_widths(width):
    unit = 128 if width % 128 == 0 else width
    tiles = width // unit
    rest = tiles // 8
    first = -(-(tiles - rest) // 2)
    second = rest // 2
    return tuple(unit * n for n in (first, tiles - rest - first, rest - second, second))


STAGE_SHARES = (0.35, 0.6, 0.85, 1.0)


class Hosted:
    def __init__(self, dp_count, count, shapes, spans=None):
        self.dp_count, self.count, self.shapes = dp_count, count, shapes
        self.spans = spans or ((0, 0.0, 1.0),) * len(shapes)
        self.all_bits = axis_bits(dp_count, count)
        self.plan = []
        for index, (rows, width, compact, _) in enumerate(shapes):
            bits = self.all_bits[:-1] if compact else self.all_bits
            orders = stream_orders(dp_count, count)
            widths = part_widths(width)
            if compact:
                last = len(bits)
                orders = [tuple(d for d in order if d != last) for order in orders[:2]]
                widths = (width // 2, width // 2)
            start = 0
            for order, size in zip(orders, widths):
                pieces = [size] if size else []
                if size >= 256 and not compact:
                    first = 128 * -(-size // 256)
                    pieces = [first, size - first]
                for k, piece in enumerate(pieces):
                    self.plan.append((index, tuple(order), bits, start, piece, rows, compact, k))
                    start += piece
        self.plan.sort(key=lambda p: (p[0], p[7]))
        self.arrays = len(shapes)
        self.events = []
        for k, part in enumerate(self.plan):
            _, first, last = self.spans[part[0]]
            for stage in range(len(part[2])):
                share = STAGE_SHARES[min(stage, 3)]
                self.events.append((first + (last - first) * share + 0.01 * stage, k, stage))
        self.events.sort()

    def views(self, arrays):
        return [self.view(i, array) for i, array in enumerate(arrays)]

    def view_shape(self, index):
        rows, width, compact, _ = self.shapes[index]
        depth = len(self.all_bits) - (1 if compact else 0)
        return (2,) * depth + (rows, width)

    def view(self, index, array):
        return array.reshape(self.view_shape(index))

    def in_specs(self):
        return [pl.BlockSpec(memory_space=pl.ANY)] * self.arrays

    def out_shapes(self):
        return [
            jax.ShapeDtypeStruct((2, rows + (rows // 3 if compact else 0), width), F32)
            for rows, width, compact, _ in self.shapes
        ]

    def out_specs(self):
        return [pl.BlockSpec(memory_space=pl.ANY)] * self.arrays

    def scratch(self):
        shapes = [pltpu.VMEM(o.shape, F32) for o in self.out_shapes()]
        shapes.append(pltpu.SemaphoreType.DMA((max(1, self.arrays),)))
        for index, _, bits, _, size, rows, _, _ in self.plan:
            shapes += Reducer.scratch(len(bits), rows, size, self.shapes[index][3])
        return shapes

    def bind(self, srcs, outs, scratch):
        self.parts = []
        self.outs, self.sums = outs, scratch[: self.arrays]
        self.out_sems = scratch[self.arrays]
        at = self.arrays + 1
        for index, order, bits, start, size, rows, compact, _ in self.plan:
            depth = len(bits) + 1
            mine = scratch[at : at + depth + 3]
            at += depth + 3
            self.parts.append(
                Reducer(
                    bits,
                    order,
                    srcs[index],
                    (start, size),
                    self.sums[index],
                    rows,
                    compact,
                    mine[:depth],
                    mine[depth:],
                )
            )

    def begin(self, phase=0):
        for part, plan in zip(self.parts, self.plan):
            if self.spans[plan[0]][0] == phase:
                part.begin()

    def run(self, first, last):
        for _, k, stage in self.events[first:last]:
            self.parts[k].step(stage)

    def slots(self, times):
        edges = []
        done = 0
        for time in times:
            while done < len(self.events) and self.events[done][0] <= time:
                done += 1
            edges.append(done)
        edges[-1] = len(self.events)
        return list(zip([0] + edges[:-1], edges))

    def settle(self):
        for part in self.parts:
            part.tail()
        for part in self.parts:
            part.finish()

    def finish(self):
        self.settle()
        copies = []
        for i, (out, value) in enumerate(zip(self.outs, self.sums)):
            copies.append(pltpu.make_async_copy(value, out, self.out_sems.at[i]))
            copies[-1].start()
        for copy in copies:
            copy.wait()


BACK_LIMIT = 64 * 2**20 - 2**18


class Group:
    def __init__(self):
        self.half = lax.axis_size("seq") // 2
        self.core = lax.axis_index("section")
        self.place = lax.axis_index("seq")
        self.low = lax.rem(self.place, self.half)
        self.base = self.place - self.low
        self.rank = self.core * self.half + self.low

    def others(self):
        pairs = [(dc, d) for d in range(1, self.half) for dc in (0, 1)]
        return pairs + [(1, 0)]

    def slot(self, dc, d):
        return dc * self.half + d

    def where(self, dc, d):
        core = lax.rem(self.core + dc, 2)
        low = lax.rem(self.low + d, self.half)
        return core, low

    def device(self, dc, d):
        core, low = self.where(dc, d)
        return {"section": core, "seq": self.base + low}

    def rank_of(self, dc, d):
        core, low = self.where(dc, d)
        return core * self.half + low

    def greet(self, dp_count):
        barrier = pltpu.get_barrier_semaphore()
        targets = [self.device(dc, d) for dc, d in self.others()]
        mask = dp_count // 2
        while mask:
            targets.append({"dp": partner("dp", mask)})
            mask //= 2
        targets.append({"seq": partner("seq", self.half)})
        targets.append({"section": 1 - self.core, "seq": partner("seq", self.half)})
        for target in targets:
            pl.semaphore_signal(
                barrier, inc=1, device_id=target, device_id_type=pl.DeviceIdType.MESH
            )
        pl.semaphore_wait(barrier, len(targets))


def send(src, dst, sems, slot, device):
    return pltpu.make_async_remote_copy(
        src_ref=src,
        dst_ref=dst,
        send_sem=sems[0].at[slot],
        recv_sem=sems[1].at[slot],
        device_id=device,
        device_id_type=pl.DeviceIdType.MESH,
    )


class Deliver:
    def __init__(self, group, layer, src, out, sems):
        micro = lax.div(group.place, group.half)
        here, there = sems[0], sems[1]
        self.core, self.layer = group.core, layer
        self.local = pltpu.make_async_copy(src, out.at[micro], sems[2])
        self.chip = send(src, out.at[micro], (here, there), 0, {"section": 1 - group.core})
        self.far = send(
            src,
            out.at[micro],
            (here, there),
            1,
            {"section": layer, "seq": partner("seq", group.half)},
        )

    def start(self):
        first = self.local if self.layer == 0 else self.chip
        pl.when(self.core == 0)(lambda: first.start())
        pl.when(self.core == 1)(lambda: self.far.start())

    def wait(self):
        @pl.when(self.core == 0)
        def _():
            if self.layer == 0:
                self.local.wait()
                self.far.wait_recv()
            else:
                self.chip.wait_send()

        @pl.when(self.core == 1)
        def _():
            self.far.wait_send()
            if self.layer == 1:
                self.far.wait_recv()
                self.chip.wait_recv()


def deliver_sems():
    return dma_pair(2) + [pltpu.SemaphoreType.DMA]


def dma_pair(count):
    return [pltpu.SemaphoreType.DMA((count,)), pltpu.SemaphoreType.DMA((count,))]


VEC_ROWS = 16
LN1_GAIN, LN1_BIAS, B_QUERY, B_VALUE, B_OUT, LN2_GAIN, LN2_BIAS, B_DOWN, B_UP = range(9)


def attend_kernel(first, layer, dp_count, *refs):
    if first:
        x_ref, joint_ref, wout_ref, mask_ref = refs[:4]
        vectors = refs[4:13]
        o_out, lse_out, a_out, q_out, k_out, v_out = refs[13:19]
        x_out, joint_out, wout_out, vec_out = refs[19:23]
        rest = refs[23:]
    else:
        x_ref, joint_ref, mask_ref, vec_ref, cot_ref = refs[:5]
        o_out, lse_out, a_out, q_out, k_out, v_out, cot_out, rows_out = refs[5:13]
        rest = refs[13:]
    x_all, a_all, q_all, k_all, v_all, lse, o_send, o_recv = rest[:8]
    x_sems, o_sems = rest[8:10], rest[10:12]
    out_sems = rest[12]
    if first:
        joint_pair, wide_own, wide_other, vec_send, vec_recv, vec_pair = rest[13:19]
        wide_sems, vec_sems = rest[19:21], rest[21:23]
        load_sems = rest[23]
    else:
        joint_one, cot_own, cot_other = rest[13:16]
        cot_sems = rest[16:18]
        load_sems = rest[18]
        rows_sems = rest[19:22]
    group = Group()
    core, half, rank, low = group.core, group.half, group.rank, group.low
    ranks, rows, _ = x_all.shape
    width = q_all.shape[1]
    heads = width // DH
    span = half * width
    partner_core = group.device(1, 0)
    micro = lax.div(group.place, half)

    group.greet(dp_count)

    def x_copy(slot, from_rank, device):
        return send(x_all.at[from_rank], x_all.at[from_rank], x_sems, slot, device)

    far = {"seq": partner("seq", half)}

    if first:
        own_load = pltpu.make_async_copy(x_ref.at[micro, 0], x_all.at[rank], load_sems.at[0])
        far_copy = send(x_ref.at[1 - micro, 0], x_all.at[rank], x_sems, 2 * half - 1, far)
        pl.when(core == 1)(lambda: far_copy.start())
        pl.when(core == 0)(lambda: own_load.start())
        wide_copies = []
        own_loads = []
        for part in range(3):
            theirs = pl.ds(pl.multiple_of(part * D + (1 - core) * span, 128), span)
            ours = pl.ds(pl.multiple_of(part * D + core * span, 128), span)
            wide_copies.append(
                send(joint_ref.at[0, :, theirs], wide_other.at[part], wide_sems, part, partner_core)
            )
            own_loads.append(
                pltpu.make_async_copy(
                    joint_ref.at[0, :, ours], wide_own.at[part], load_sems.at[1 + part]
                )
            )
            wide_copies[-1].start()
            own_loads[-1].start()
        vec_send[...] = jnp.zeros_like(vec_send)
        for i, value in enumerate(vectors[:8]):
            vec_send[i : i + 1, :] = value[...].astype(F32)
        for i in range(FF // D):
            vec_send[8 + i : 9 + i, :] = vectors[8][:, i * D : (i + 1) * D].astype(F32)
        vec_copy = send(vec_send, vec_recv, vec_sems, 0, partner_core)
        vec_copy.start()
        wout_copy = send(wout_ref.at[0], wout_out, vec_sems, 1, partner_core)
        pl.when(core == 1)(lambda: far_copy.wait_recv())
        pl.when(core == 0)(lambda: own_load.wait())
    else:
        own_load = pltpu.make_async_copy(x_ref, x_all.at[rank], load_sems.at[0])
        joint_load = pltpu.make_async_copy(joint_ref, joint_one, load_sems.at[1])
        own_load.start()
        joint_load.start()
        cot_far = send(cot_ref.at[1 - micro, 0], cot_own, cot_sems, 0, far)
        cot_load = pltpu.make_async_copy(cot_ref.at[micro, 0], cot_own, load_sems.at[2])
        pl.when(core == 1)(lambda: cot_far.start())
        pl.when(core == 0)(lambda: cot_load.start())
        own_load.wait()
    for d in range(1, half):
        x_copy(d - 1, rank, group.device(0, d)).start()
    x_copy(half - 1, rank, partner_core).start()

    source = lax.broadcasted_iota(jnp.int32, (span, width), 0)
    target = lax.broadcasted_iota(jnp.int32, (span, width), 1)
    if half == 2:
        wanted = (2 * lax.div(target, DH) + low) * DH + lax.rem(target, DH)
    else:
        wanted = low * width + target
    pick = (source == wanted).astype(F32).astype(BF16)
    if first:
        wout_copy.start()
        vec_copy.wait_recv()
        vec_pair[core] = vec_send[...]
        vec_pair[1 - core] = vec_recv[...]
        for load in own_loads:
            load.wait()
        for part in range(3):
            joint_pair[core, :, part * width : (part + 1) * width] = mm(
                wide_own[part], pick
            ).astype(BF16)
        for copy in wide_copies:
            copy.wait_recv()
        for part in range(3):
            joint_pair[1 - core, :, part * width : (part + 1) * width] = mm(
                wide_other[part], pick
            ).astype(BF16)
        vec = vec_pair[0]
        weights = lambda: joint_pair[0]
    else:
        joint_load.wait()
        vec = vec_ref[0]
        weights = lambda: joint_one[...]

    def of_heads(row):
        parts = vec[row : row + 1, :]
        mine = jnp.where(core == 0, parts[:, :span], parts[:, span:])
        wide = jnp.broadcast_to(mine, (16, span)).astype(BF16)
        return mm(wide, pick)[0:1, :]

    bias_q = of_heads(B_QUERY)
    bias_v = of_heads(B_VALUE)
    gain = vec[LN1_GAIN : LN1_GAIN + 1, :]
    shift = vec[LN1_BIAS : LN1_BIAS + 1, :]

    def project(at):
        normal, _ = norm_stats(x_all[at].astype(F32))
        a = (normal * gain + shift).astype(BF16)
        here = pl.ds(pl.multiple_of(at * rows, 16), rows)
        a_all[here, :] = a
        joined = mm(a, weights())
        q_all[here, :] = (joined[:, :width] + bias_q).astype(BF16)
        k_all[here, :] = joined[:, width : 2 * width].astype(BF16)
        v_all[here, :] = (joined[:, 2 * width :] + bias_v).astype(BF16)

    project(rank)
    x_copy(half - 1, rank, partner_core).wait_recv()
    project(group.rank_of(1, 0))
    for d in range(1, half):
        here = group.rank_of(0, half - d)
        x_copy(d - 1, here, partner_core).wait_recv()
        x_copy(half - 1 + d, here, partner_core).start()
        project(here)
    for d in range(1, half):
        there = group.rank_of(1, half - d)
        x_copy(half - 1 + d, there, partner_core).wait_recv()
        project(there)

    saves = [
        pltpu.make_async_copy(a_all, a_out, out_sems.at[0]),
        pltpu.make_async_copy(q_all, q_out, out_sems.at[1]),
        pltpu.make_async_copy(k_all, k_out, out_sems.at[2]),
        pltpu.make_async_copy(v_all, v_out, out_sems.at[3]),
    ]
    if first:
        saves.append(pltpu.make_async_copy(joint_pair, joint_out, out_sems.at[4]))
        saves.append(pltpu.make_async_copy(x_all.at[rank], x_out, out_sems.at[5]))
        saves.append(pltpu.make_async_copy(vec_pair, vec_out, out_sems.at[6]))
    for save in saves:
        save.start()
    if not first:
        rows_copy = Deliver(group, 0, x_ref, rows_out, rows_sems)
        rows_copy.start()

    lane = lax.broadcasted_iota(jnp.int32, (rows, 128), 1)
    mask = mask_ref[...]

    def attend(at):
        here = pl.ds(pl.multiple_of(at * rows, 16), rows)
        q = q_all[here, :]
        mixed = jnp.zeros((rows, width), F32)
        totals = jnp.zeros((rows, 128), F32)
        for head in range(heads):
            mine = head_lanes((rows, width), head)
            scores = mm_nt(jnp.where(mine, q, jnp.zeros_like(q)), k_all[...]) * SCALE2 + mask
            top = jnp.max(scores, axis=-1, keepdims=True)
            expo = jnp.exp2(scores - top)
            total = jnp.sum(expo, axis=-1, keepdims=True)
            part = mm(expo.astype(BF16), v_all[...]) / total
            mixed = jnp.where(mine, part, mixed)
            totals = jnp.where(lane == head, top + jnp.log2(total), totals)
        lse[here, :] = totals
        return mixed.astype(BF16)

    copies = []
    for dc, d in group.others():
        slot = group.slot(dc, d)
        o_send[slot] = attend(group.rank_of(dc, d))
        copies.append(send(o_send.at[slot], o_recv.at[rank], o_sems, slot, group.device(dc, d)))
        copies[-1].start()
    if not first:
        pl.when(core == 1)(lambda: cot_far.wait())
        pl.when(core == 0)(lambda: cot_load.wait())
        cot_share = send(cot_own, cot_other, cot_sems, 1, partner_core)
        cot_share.start()
    o_recv[rank] = attend(rank)
    if not first:
        cot_share.wait()
        cot_out[0] = cot_own[...]
        cot_out[1] = cot_other[...]
    lse_out[...] = lse[...]
    for copy in copies:
        copy.wait()
    o_out[...] = o_recv[...]
    for save in saves:
        save.wait()
    if not first:
        rows_copy.wait()
    for d in range(1, half):
        x_copy(d - 1, rank, group.device(0, d)).wait_send()
        x_copy(half - 1 + d, group.rank_of(0, half - d), partner_core).wait_send()
    x_copy(half - 1, rank, partner_core).wait_send()
    if first:
        pl.when(core == 1)(lambda: far_copy.wait_send())
        for copy in wide_copies:
            copy.wait_send()
        vec_copy.wait_send()
        wout_copy.wait()


def attend_call(first, layer, mask, ranks, dp_count, *args):
    rows = args[0].shape[-2]
    width = D // ranks
    half = ranks // 2
    span = half * width
    anywhere = pl.BlockSpec(memory_space=pl.ANY)
    vmem = pl.BlockSpec(memory_space=pltpu.VMEM)
    out_shape = [
        jax.ShapeDtypeStruct((ranks, rows, width), BF16),
        jax.ShapeDtypeStruct((LEN, 128), F32),
        jax.ShapeDtypeStruct((LEN, D), BF16),
        jax.ShapeDtypeStruct((LEN, width), BF16),
        jax.ShapeDtypeStruct((LEN, width), BF16),
        jax.ShapeDtypeStruct((LEN, width), BF16),
    ]
    out_specs = [vmem, vmem] + [anywhere] * 4
    scratch = [
        pltpu.VMEM((ranks, rows, D), BF16),
        pltpu.VMEM((LEN, D), BF16),
        pltpu.VMEM((LEN, width), BF16),
        pltpu.VMEM((LEN, width), BF16),
        pltpu.VMEM((LEN, width), BF16),
        pltpu.VMEM((LEN, 128), F32),
        pltpu.VMEM((ranks, rows, width), BF16),
        pltpu.VMEM((ranks, rows, width), BF16),
    ]
    scratch += dma_pair(2 * half) + dma_pair(ranks) + [pltpu.SemaphoreType.DMA((7,))]
    if first:
        operands = args[:3] + (mask,) + args[3:]
        in_specs = [anywhere] * 3 + [vmem] * (1 + len(args[3:]))
        out_shape += [
            jax.ShapeDtypeStruct((rows, D), BF16),
            jax.ShapeDtypeStruct((2, D, 3 * width), BF16),
            jax.ShapeDtypeStruct((D, D), BF16),
            jax.ShapeDtypeStruct((2, VEC_ROWS, D), F32),
        ]
        out_specs += [anywhere] * 4
        scratch += [
            pltpu.VMEM((2, D, 3 * width), BF16),
            pltpu.VMEM((3, D, span), BF16),
            pltpu.VMEM((3, D, span), BF16),
            pltpu.VMEM((VEC_ROWS, D), F32),
            pltpu.VMEM((VEC_ROWS, D), F32),
            pltpu.VMEM((2, VEC_ROWS, D), F32),
        ]
        scratch += dma_pair(3) + dma_pair(2) + [pltpu.SemaphoreType.DMA((4,))]
    else:
        operands = args[:2] + (mask,) + args[2:]
        in_specs = [anywhere] * 2 + [vmem] * 2 + [anywhere]
        out_shape += [jax.ShapeDtypeStruct((2, rows, D), BF16)] * 2
        out_specs += [vmem, anywhere]
        scratch += [
            pltpu.VMEM((D, 3 * width), BF16),
            pltpu.VMEM((rows, D), BF16),
            pltpu.VMEM((rows, D), BF16),
        ]
        scratch += dma_pair(2) + [pltpu.SemaphoreType.DMA((3,))] + deliver_sems()
    return pl.pallas_call(
        functools.partial(attend_kernel, first, layer, dp_count),
        in_specs=in_specs,
        out_specs=out_specs,
        out_shape=out_shape,
        scratch_shapes=scratch,
        compiler_params=pltpu.CompilerParams(
            vmem_limit_bytes=VMEM_LIMIT, collective_id=5 + layer, has_side_effects=True
        ),
        cost_estimate=pl.CostEstimate(
            flops=40 * 10**9, bytes_accessed=20 * 2**20, transcendentals=LEN * LEN * width // DH
        ),
    )(*operands)


def mlp_kernel(
    layer,
    o_ref,
    x_ref,
    wo0_ref,
    wo1_ref,
    vec_ref,
    up0_ref,
    up1_ref,
    down0_ref,
    down1_ref,
    h_ref,
    u_ref,
    y_ref,
    a_all,
    o_all,
    g_all,
    acc,
    wo,
    a_mine,
    a_other,
    o_send,
    o_other,
    g_mine,
    g_send,
    g_other,
    send_sems,
    recv_sems,
    save_sems,
    wo_sem,
):
    step = pl.program_id(0)
    groups, rows, width = o_ref.shape
    half = groups // 2
    unit = FF // shards_of() // 2
    core = lax.axis_index("section")
    own = core == layer
    device = {"section": 1 - core}
    sems = (send_sems, recv_sems)
    a_copy = send(a_mine, a_other, sems, NCH, device)
    o_copy = send(o_send, o_other, sems, NCH + 1, device)

    def g_copy(at):
        return send(g_send.at[at], g_other.at[at], sems, at, device)

    def g_save(which, at):
        cols = pl.ds(pl.multiple_of(at * (FC // 2), FC // 2), FC // 2)
        source = g_other if which else g_mine
        return pltpu.make_async_copy(
            source.at[at], g_all.at[which, :, cols], save_sems.at[which, at]
        )

    @pl.when(step == 0)
    def _():
        barrier = pltpu.get_barrier_semaphore()
        pl.semaphore_signal(
            barrier, inc=1, device_id=device, device_id_type=pl.DeviceIdType.MESH
        )
        pl.semaphore_wait(barrier, 1)
        first = pltpu.make_async_copy(wo0_ref, wo, wo_sem)
        second = pltpu.make_async_copy(wo1_ref, wo, wo_sem)
        pl.when(own)(lambda: first.start())
        pl.when(jnp.logical_not(own))(lambda: second.start())
        for i in range(half):
            o_send[i] = o_ref[(1 - core) * half + i]
            o_all[0, :, i * width : (i + 1) * width] = o_ref[core * half + i]
        o_copy.start()
        first.wait()
        hidden = x_ref[...].astype(F32) + vec_ref[0, B_OUT : B_OUT + 1, :]
        for group in range(groups):
            hidden += mm(o_ref[group], wo[group * width : (group + 1) * width, :])
        h_ref[...] = hidden
        normal, _ = norm_stats(hidden)
        a_mine[...] = (
            normal * vec_ref[0, LN2_GAIN : LN2_GAIN + 1, :] + vec_ref[0, LN2_BIAS : LN2_BIAS + 1, :]
        ).astype(BF16)
        a_copy.start()
        acc[...] = hidden + vec_ref[0, B_DOWN : B_DOWN + 1, :]

    def part(up_ref, down_ref):
        at = pl.multiple_of(lax.rem(step, D // FC) * FC, FC)
        bias = vec_ref[0, pl.ds(B_UP + lax.div(step, D // FC), 1), pl.ds(at, FC)]
        upper = mm(a_mine[...], up_ref[...]) + bias
        u_ref[...] = upper
        inner = GELU_A * (upper + GELU_B * upper * upper * upper)
        gated = (0.5 * upper * (1.0 + jnp.tanh(inner))).astype(BF16)
        split_halves(gated, unit, core, g_mine, g_send, step)
        acc[...] += mm(gated, down_ref[...])

    @pl.when(step < NCH)
    def _():
        pl.when(own)(lambda: part(up0_ref, down0_ref))
        pl.when(jnp.logical_not(own))(lambda: part(up1_ref, down1_ref))
        g_copy(step).start()
        g_save(0, step).start()

    @pl.when(step > 0)
    def _():
        g_copy(step - 1).wait()
        g_save(1, step - 1).start()

    @pl.when(step == NCH)
    def _():
        y_ref[...] = acc[...].astype(BF16)
        a_copy.wait()
        a_all[0] = a_mine[...]
        a_all[1] = a_other[...]
        o_copy.wait()
        for i in range(half):
            o_all[1, :, i * width : (i + 1) * width] = o_other[i]

        def drain(at, carry):
            g_save(0, at).wait()
            g_save(1, at).wait()
            return carry

        lax.fori_loop(0, NCH, drain, 0)


def mlp_call(layer, o_all, x_own, outs, vec, ups, downs):
    rows = x_own.shape[0]
    groups, _, width = o_all.shape
    whole = lambda i: (0, 0)
    now = lambda i: jnp.minimum(i, NCH - 1)
    mine = lambda i, first: jnp.where((lax.axis_index("section") == layer) == first, now(i), 0)
    col = lambda first: (lambda i: (0, mine(i, first)))
    line = lambda first: (lambda i: (mine(i, first), 0))
    chunk = lambda i: (0, now(i))
    piece = pltpu.VMEM((NCH, rows, FC // 2), BF16)
    return pl.pallas_call(
        functools.partial(mlp_kernel, layer),
        grid=(NCH + 1,),
        in_specs=[
            pl.BlockSpec((groups, rows, width), lambda i: (0, 0, 0)),
            pl.BlockSpec((rows, D), whole),
            pl.BlockSpec(memory_space=pl.ANY),
            pl.BlockSpec(memory_space=pl.ANY),
            pl.BlockSpec((1, VEC_ROWS, D), lambda i: (layer, 0, 0)),
            pl.BlockSpec((D, FC), col(True)),
            pl.BlockSpec((D, FC), col(False)),
            pl.BlockSpec((FC, D), line(True)),
            pl.BlockSpec((FC, D), line(False)),
        ],
        out_specs=[
            pl.BlockSpec((rows, D), whole),
            pl.BlockSpec((rows, FC), chunk),
            pl.BlockSpec((rows, D), whole),
            pl.BlockSpec((2, rows, D), lambda i: (0, 0, 0)),
            pl.BlockSpec((2, rows, D // 2), lambda i: (0, 0, 0)),
            pl.BlockSpec(memory_space=pl.ANY),
        ],
        scratch_shapes=[
            pltpu.VMEM((rows, D), F32),
            pltpu.VMEM((D, D), BF16),
            pltpu.VMEM((rows, D), BF16),
            pltpu.VMEM((rows, D), BF16),
            pltpu.VMEM((groups // 2, rows, width), BF16),
            pltpu.VMEM((groups // 2, rows, width), BF16),
            piece,
            piece,
            piece,
        ]
        + dma_pair(NCH + 2)
        + [pltpu.SemaphoreType.DMA((2, NCH)), pltpu.SemaphoreType.DMA],
        out_shape=[
            jax.ShapeDtypeStruct((rows, D), F32),
            jax.ShapeDtypeStruct((rows, FF), F32),
            jax.ShapeDtypeStruct((rows, D), BF16),
            jax.ShapeDtypeStruct((2, rows, D), BF16),
            jax.ShapeDtypeStruct((2, rows, D // 2), BF16),
            jax.ShapeDtypeStruct((2, rows, FF // 2), BF16),
        ],
        compiler_params=pltpu.CompilerParams(
            vmem_limit_bytes=VMEM_LIMIT, collective_id=7 + layer, has_side_effects=True
        ),
        cost_estimate=pl.CostEstimate(
            flops=2 * rows * D * (D + 2 * FF), bytes_accessed=30 * 2**20, transcendentals=rows * FF
        ),
    )(o_all, x_own, outs[0], outs[1], vec, ups[0], ups[1], downs[0], downs[1])


def back_kernel(layer, host, ranges, *refs):
    n = host.arrays - 1
    refs = list(refs)

    def pop(count):
        taken = refs[:count]
        del refs[:count]
        return taken

    u_ref, mask_ref, vec_ref = pop(3)
    dy_src, h_src, a2_src, wo0_src, wo1_src, up0_src, up1_src, down0_src, down1_src = pop(9)
    rows_src = pop(1)[0]
    late = pop(8)
    srcs = pop(n)
    gbup_ref, sums_two_ref, sums_one_ref, sums_qv_ref = pop(4)
    gup_out, dx_out, gjoint_out, gout_out, rows_out = pop(5)
    outs = pop(n + 1)
    dy, h, a2, wo, ups, downs = pop(6)
    load_sems, weight_sems = pop(2)
    acc, du_mine, du_send, du_recv, gup, branch, dh, do_send, do_recv = pop(9)
    du_sems, do_sems = pop(2), pop(2)
    gup_sems, save_sems = pop(2)
    q_all, k_all, v_all, lse, a1, w_joint, x_own, mixed = pop(8)
    late_sems = pop(1)[0]
    dk_acc, dv_acc, dj, core_recv, far_send, far_recv = pop(6)
    core_send = a2 if lax.axis_size("seq") == 4 else pop(1)[0]
    g_own, g_send, g_recv, gout, dx_recv = pop(5)
    dx_own = dy
    core_sems, far_sems, pair_sems = pop(2), pop(2), pop(2)
    rows_sems = pop(3)
    host.bind(list(srcs) + [gup_out], outs, refs)
    group = Group()
    core, half, rank = group.core, group.half, group.rank
    step = pl.program_id(0)
    ranks, rows, width = do_send.shape
    length = q_all.shape[0]
    heads = width // DH
    scale = DH ** (-0.5)
    unit = FF // shards_of() // 2
    own = core == layer
    partner_core = group.device(1, 0)
    ranges = list(ranges)
    lead, middle = ranges[: 2 * NCH], ranges[2 * NCH : 2 * NCH + 3]
    blocks = length // BQ * heads
    inner = ranges[2 * NCH + 3 : 2 * NCH + 3 + blocks]
    tail = ranges[2 * NCH + 3 + blocks :]

    def weight_copies(at, second):
        slot = lax.rem(at, 2)
        cols = pl.ds(pl.multiple_of(at * FC, FC), FC)
        up, down = (up1_src, down1_src) if second else (up0_src, down0_src)
        return (
            pltpu.make_async_copy(up.at[:, cols], ups.at[slot], weight_sems.at[0, slot]),
            pltpu.make_async_copy(down.at[cols, :], downs.at[slot], weight_sems.at[1, slot]),
        )

    def fetch(at):
        @pl.when(own)
        def _():
            for copy in weight_copies(at, False):
                copy.start()

        @pl.when(jnp.logical_not(own))
        def _():
            for copy in weight_copies(at, True):
                copy.start()

    rows_copy = Deliver(group, 1, rows_src, rows_out, rows_sems)
    dy_load = pltpu.make_async_copy(dy_src, dy, load_sems.at[0])
    h_load = pltpu.make_async_copy(h_src, h, load_sems.at[1])
    a2_load = pltpu.make_async_copy(a2_src, a2, load_sems.at[2])
    wo_load = pltpu.make_async_copy(wo0_src, wo, load_sems.at[3])
    wo_load_other = pltpu.make_async_copy(wo1_src, wo, load_sems.at[3])
    late_loads = [
        pltpu.make_async_copy(source, target, late_sems.at[i])
        for i, (source, target) in enumerate(
            zip(late, (q_all, k_all, v_all, lse, a1, w_joint, x_own, mixed))
        )
    ]

    def du_copy(at):
        return send(du_send.at[at], du_recv.at[at], du_sems, at, partner_core)

    def gup_save(at):
        per = gup.shape[1]
        lead_bits = NCH.bit_length() - 1
        index = tuple(
            lax.rem(lax.div(at, 2 ** (lead_bits - 1 - j)), 2) for j in range(lead_bits)
        )
        return pltpu.make_async_copy(
            gup.at[lax.rem(at, 2)].reshape(gup_out.shape[lead_bits:]),
            gup_out.at[index],
            gup_sems.at[lax.rem(at, 2)],
        )

    @pl.when(step == 0)
    def _():
        group.greet(host.dp_count)
        rows_copy.start()
        dy_load.start()
        fetch(0)
        host.begin()
        a2_load.start()
        h_load.start()
        pl.when(own)(lambda: wo_load.start())
        pl.when(jnp.logical_not(own))(lambda: wo_load_other.start())
        for load in late_loads:
            load.start()
        acc[...] = jnp.zeros_like(acc)
        dy_load.wait()
        a2_load.wait()

    @pl.when(step < NCH - 1)
    def _():
        fetch(step + 1)

    @pl.when(step < NCH)
    def _():
        slot = lax.rem(step, 2)
        for copy in weight_copies(step, False):
            copy.wait()
        d_gated = mm_nt(dy[...], downs[slot])
        upper = u_ref[...]
        square = upper * upper
        turn = jnp.tanh(GELU_A * upper * (1.0 + GELU_B * square))
        slope = 0.5 * (1.0 + turn) + (0.5 * GELU_A) * upper * (1.0 - turn * turn) * (
            1.0 + (3.0 * GELU_B) * square
        )
        d_upper = (d_gated * slope).astype(BF16)
        split_halves(d_upper, unit, core, du_mine, du_send, step)
        du_copy(step).start()
        gbup_ref[...] = jnp.sum(d_upper.astype(F32), axis=0, keepdims=True)
        acc[...] += mm_nt(d_upper, ups[slot])

    for at, (first, last) in enumerate(lead):
        if last > first and at % 2 == 0:
            pl.when(step == at // 2)(functools.partial(host.run, first, last))

    @pl.when(step > 0)
    def _():
        at = step - 1
        du_copy(at).wait()
        pl.when(at >= 2)(lambda: gup_save(at - 2).wait())
        value = mm_tn(du_mine[at], a2[0]) + mm_tn(du_recv[at], a2[1])
        gup[lax.rem(at, 2)] = value.astype(BF16).reshape(gup.shape[1:])
        gup_save(at).start()

    for at, (first, last) in enumerate(lead):
        if last > first and at % 2 == 1:
            pl.when(step == at // 2)(functools.partial(host.run, first, last))

    @pl.when(step == NCH)
    def _():
        h_load.wait()
        gup_save(NCH - 2).wait()
        gup_save(NCH - 1).wait()
        host.begin(1)
        normal, inverse = norm_stats(h[...])
        d_out = dy[...].astype(F32)
        d_normed = acc[...]
        sums_two_ref[...] = jnp.zeros_like(sums_two_ref)
        sums_two_ref[0:1, :] = jnp.sum(d_normed * normal, axis=0, keepdims=True)
        sums_two_ref[1:2, :] = jnp.sum(d_normed, axis=0, keepdims=True)
        d_normal = d_normed * vec_ref[0, LN2_GAIN : LN2_GAIN + 1, :]
        d_hidden = d_out + inverse * (
            d_normal
            - jnp.mean(d_normal, axis=-1, keepdims=True)
            - normal * jnp.mean(d_normal * normal, axis=-1, keepdims=True)
        )
        dh[...] = d_hidden
        d_branch = d_hidden.astype(BF16)
        branch[0] = d_branch
        branch_copy = send(branch.at[0], branch.at[1], do_sems, ranks, partner_core)
        branch_copy.start()
        wo_load.wait()

        def heads_of(to_rank):
            at = pl.multiple_of(to_rank * width, width)
            return mm_nt(d_branch, wo[pl.ds(at, width), :]).astype(BF16)

        copies = []
        for dc, d in group.others():
            slot = group.slot(dc, d)
            do_send[slot] = heads_of(group.rank_of(dc, d))
            copies.append(
                send(do_send.at[slot], do_recv.at[pl.ds(pl.multiple_of(rank * rows, 16), rows)], do_sems, slot, group.device(dc, d))
            )
            copies[-1].start()
        do_recv[pl.ds(pl.multiple_of(rank * rows, 16), rows), :] = heads_of(rank)
        host.run(*middle[0])
        sums_two_ref[2:3, :] = jnp.sum(d_branch.astype(F32), axis=0, keepdims=True)
        sums_two_ref[3:4, :] = jnp.sum(d_out, axis=0, keepdims=True)
        dk_acc[...] = jnp.zeros_like(dk_acc)
        dv_acc[...] = jnp.zeros_like(dv_acc)
        sums_qv_ref[...] = jnp.zeros_like(sums_qv_ref)
        sums_one_ref[...] = jnp.zeros_like(sums_one_ref)
        for load in late_loads:
            load.wait()
        branch_copy.wait()
        gout[...] = (mm_tn(branch[0], mixed[0]) + mm_tn(branch[1], mixed[1])).astype(BF16)
        gout_save = pltpu.make_async_copy(gout, gout_out, save_sems.at[0])
        gout_save.start()
        host.run(*middle[1])
        for copy in copies:
            copy.wait()
        host.run(*middle[2])

        def block(at, carry):
            here = pl.ds(pl.multiple_of(at * BQ, BQ), BQ)
            q = q_all[here, :]
            grad = do_recv[here, :]
            totals = lse[here, :]
            d_q = jnp.zeros((BQ, width), F32)
            for head in range(heads):
                mine = head_lanes((BQ, width), head)
                q_head = jnp.where(mine, q, jnp.zeros_like(q))
                grad_head = jnp.where(mine, grad, jnp.zeros_like(grad))
                scores = mm_nt(q_head, k_all[...]) * SCALE2 + mask_ref[...]
                probs = jnp.exp2(scores - totals[:, head : head + 1])
                d_probs = mm_nt(grad_head, v_all[...])
                term = jnp.sum(probs * d_probs, axis=-1, keepdims=True)
                d_scores = (probs * (d_probs - term)).astype(BF16)
                dv_acc[...] += mm_tn(probs.astype(BF16), grad_head)
                dk_acc[...] += mm_tn(d_scores, q_head)
                d_q = jnp.where(mine, mm(d_scores, k_all[...]), d_q)
                for slot, (first, last) in enumerate(inner):
                    if last > first and slot % heads == head:
                        pl.when(at == slot // heads)(functools.partial(host.run, first, last))
            low = (d_q * scale).astype(BF16)
            dj[here, :width] = low
            sums_qv_ref[0:1, :] += jnp.sum(low.astype(F32), axis=0, keepdims=True)
            return carry

        lax.fori_loop(0, length // BQ, block, 0)
        dj[:, width : 2 * width] = (dk_acc[...] * scale).astype(BF16)
        low_v = dv_acc[...].astype(BF16)
        dj[:, 2 * width :] = low_v
        sums_qv_ref[1:2, :] = jnp.sum(low_v.astype(F32), axis=0, keepdims=True)

        def partial_rows(to_rank):
            here = pl.ds(pl.multiple_of(to_rank * rows, 16), rows)
            return mm_nt(dj[here, :], w_joint[...])

        def core_copy(d):
            return send(core_send.at[d], core_recv.at[d], core_sems, d, partner_core)

        def far_copy(d):
            return send(far_send.at[d - 1], far_recv.at[d - 1], far_sems, d - 1, group.device(0, d))

        for d in [d for d in range(1, half)] + [0]:
            core_send[d] = partial_rows(group.rank_of(1, d)).astype(BF16)
            core_copy(d).start()
        for d in range(1, half):
            value = partial_rows(group.rank_of(0, d))
            core_copy(d).wait_recv()
            far_send[d - 1] = (value + core_recv[d].astype(F32)).astype(BF16)
            far_copy(d).start()
        host.run(*tail[0])
        value = partial_rows(rank)
        core_copy(0).wait_recv()
        acc[...] = value + core_recv[0].astype(F32)

        half_cols = D // 2
        mine_cols = pl.ds(pl.multiple_of(core * half_cols, half_cols), half_cols)
        other_cols = pl.ds(pl.multiple_of((1 - core) * half_cols, half_cols), half_cols)
        g_send[...] = mm_tn(dj[...], a1[:, other_cols]).astype(BF16).reshape(g_send.shape)
        g_copy = send(g_send, g_recv, pair_sems, 0, partner_core)
        g_copy.start()
        host.run(*tail[1])
        g_own[...] = mm_tn(dj[...], a1[:, mine_cols]).astype(BF16).reshape(g_own.shape)
        g_save = pltpu.make_async_copy(g_own, gjoint_out.at[:, core], save_sems.at[1])
        g_save.start()
        host.run(*tail[2])

        for d in range(1, half):
            far_copy(d).wait_recv()
            acc[...] += far_recv[d - 1].astype(F32)
        d_normed = acc[...]
        normal, inverse = norm_stats(x_own[...].astype(F32))
        sums_one_ref[0:1, :] = jnp.sum(d_normed * normal, axis=0, keepdims=True)
        sums_one_ref[1:2, :] = jnp.sum(d_normed, axis=0, keepdims=True)
        d_normal = d_normed * vec_ref[0, LN1_GAIN : LN1_GAIN + 1, :]
        d_in = (
            dh[...]
            + inverse
            * (
                d_normal
                - jnp.mean(d_normal, axis=-1, keepdims=True)
                - normal * jnp.mean(d_normal * normal, axis=-1, keepdims=True)
            )
        ).astype(BF16)
        dx_own[...] = d_in
        dx_copy = send(dx_own, dx_recv, pair_sems, 1, partner_core)
        dx_copy.start()
        dx_save = pltpu.make_async_copy(dx_own, dx_out.at[0], save_sems.at[2])
        dx_save.start()
        host.run(*tail[3])
        g_copy.wait()
        g_save_other = pltpu.make_async_copy(g_recv, gjoint_out.at[:, 1 - core], save_sems.at[3])
        g_save_other.start()
        dx_copy.wait()
        dx_save_other = pltpu.make_async_copy(dx_recv, dx_out.at[1], save_sems.at[4])
        dx_save_other.start()
        for d in range(half):
            core_copy(d).wait_send()
        for d in range(1, half):
            far_copy(d).wait_send()
        for save in (gout_save, g_save, dx_save, g_save_other, dx_save_other):
            save.wait()
        rows_copy.wait()
        host.finish()


def back_call(layer, dy, hidden, wos, vec, upper, a2, ups, downs, given, late, mask, host, arrays):
    rows = dy.shape[0]
    ranks = host.count
    width = D // ranks
    half = ranks // 2
    shards = host.dp_count * ranks
    per = shards // NCH
    unit = FF // shards // 2
    heads = width // DH
    now = lambda i: (0, jnp.minimum(i, NCH - 1))
    whole = lambda i: (0, 0)
    anywhere = pl.BlockSpec(memory_space=pl.ANY)
    times = []
    for i in range(NCH):
        times += [2.9 * i + 1.6, 2.9 * i + 2.9]
    times += [29.0, 33.0, 36.0]
    for i in range(LEN // BQ * heads):
        times.append(36.0 + 28.0 / (LEN // BQ * heads) * (i + 1))
    times += [69.0, 73.0, 76.0, 84.0]
    ranges = host.slots(times)
    piece = pltpu.VMEM((NCH, rows, FC // 2), BF16)
    tokens = pltpu.VMEM((LEN, width), BF16)
    own = pltpu.VMEM((rows, D), BF16)
    view = host.view_shape(host.arrays - 1)
    return pl.pallas_call(
        functools.partial(back_kernel, layer, host, ranges),
        grid=(NCH + 1,),
        in_specs=[
            pl.BlockSpec((rows, FC), now),
            pl.BlockSpec((1, LEN), whole),
            pl.BlockSpec((1, VEC_ROWS, D), lambda i: (layer, 0, 0)),
        ]
        + [anywhere] * (10 + len(late) + len(arrays)),
        out_specs=[
            pl.BlockSpec((1, FC), now),
            pl.BlockSpec((8, D), whole),
            pl.BlockSpec((8, D), whole),
            pl.BlockSpec((8, width), whole),
        ]
        + [anywhere] * 5
        + host.out_specs(),
        out_shape=[
            jax.ShapeDtypeStruct((1, FF), F32),
            jax.ShapeDtypeStruct((8, D), F32),
            jax.ShapeDtypeStruct((8, D), F32),
            jax.ShapeDtypeStruct((8, width), F32),
            jax.ShapeDtypeStruct(view, BF16),
            jax.ShapeDtypeStruct((2, rows, D), BF16),
            jax.ShapeDtypeStruct((3, 2, width, D // 2), BF16),
            jax.ShapeDtypeStruct((D, D // 2), BF16),
            jax.ShapeDtypeStruct((2, rows, D), BF16),
        ]
        + host.out_shapes(),
        scratch_shapes=[
            own,
            pltpu.VMEM((rows, D), F32),
            pltpu.VMEM((2, rows, D), BF16),
            pltpu.VMEM((D, D), BF16),
            pltpu.VMEM((2, D, FC), BF16),
            pltpu.VMEM((2, FC, D), BF16),
            pltpu.SemaphoreType.DMA((4,)),
            pltpu.SemaphoreType.DMA((2, 2)),
            pltpu.VMEM((rows, D), F32),
            piece,
            piece,
            piece,
            pltpu.VMEM((2, per, unit, D), BF16),
            pltpu.VMEM((2, rows, D), BF16),
            pltpu.VMEM((rows, D), F32),
            pltpu.VMEM((ranks, rows, width), BF16),
            tokens,
        ]
        + dma_pair(NCH)
        + dma_pair(ranks + 1)
        + [pltpu.SemaphoreType.DMA((2,)), pltpu.SemaphoreType.DMA((5,))]
        + [pltpu.VMEM(t.shape, t.dtype) for t in late]
        + [pltpu.SemaphoreType.DMA((len(late),))]
        + [
            pltpu.VMEM((LEN, width), F32),
            pltpu.VMEM((LEN, width), F32),
            pltpu.VMEM((LEN, 3 * width), BF16),
            pltpu.VMEM((half, rows, D), BF16),
            pltpu.VMEM((half - 1, rows, D), BF16),
            pltpu.VMEM((half - 1, rows, D), BF16),
        ]
        + ([] if ranks == 4 else [pltpu.VMEM((half, rows, D), BF16)])
        + [
            pltpu.VMEM((3, width, D // 2), BF16),
            pltpu.VMEM((3, width, D // 2), BF16),
            pltpu.VMEM((3, width, D // 2), BF16),
            pltpu.VMEM((D, D // 2), BF16),
            own,
        ]
        + dma_pair(half)
        + dma_pair(half - 1)
        + dma_pair(2)
        + deliver_sems()
        + host.scratch(),
        compiler_params=pltpu.CompilerParams(
            vmem_limit_bytes=BACK_LIMIT, collective_id=layer, has_side_effects=True
        ),
        cost_estimate=pl.CostEstimate(
            flops=100 * 10**9, bytes_accessed=60 * 2**20, transcendentals=rows * FF
        ),
    )(
        upper,
        mask,
        vec,
        dy,
        hidden,
        a2,
        wos[0],
        wos[1],
        ups[0],
        ups[1],
        downs[0],
        downs[1],
        given,
        *late,
        *[host.view(i, array) for i, array in enumerate(arrays)],
    )


def final_kernel(host, *refs):
    refs = list(refs)

    def pop(count):
        taken = refs[:count]
        del refs[:count]
        return taken

    n = host.arrays
    srcs = pop(n)
    downs, ups = pop(2), pop(2)
    others = pop(3)
    rows_src = pop(1)[0]
    up_out, down_out, out_out, joint_out = pop(4)
    vec_outs = pop(9)
    rows_out = pop(1)[0]
    down, up = pop(2)
    held = pop(3)
    load_sems = pop(1)[0]
    rows_sems = pop(3)
    host.bind(srcs, [], refs)
    group = Group()
    core = group.core
    compact = group.half == 2
    group.greet(host.dp_count)
    host.begin()
    rows_copy = Deliver(group, 0, rows_src, rows_out, rows_sems)
    rows_copy.start()
    loads = []
    for i, (pair, target) in enumerate(((downs, down), (ups, up))):
        first = pltpu.make_async_copy(pair[0], target, load_sems.at[i])
        second = pltpu.make_async_copy(pair[1], target, load_sems.at[i])
        pl.when(core == 0)(functools.partial(first.start))
        pl.when(core == 1)(functools.partial(second.start))
        loads.append(first)
    for i, (source, target) in enumerate(zip(others, held)):
        loads.append(pltpu.make_async_copy(source, target, load_sems.at[2 + i]))
        loads[-1].start()
    for load in loads:
        load.wait()
    unit = up.shape[1]
    half_cols = D // 2
    for half in range(2):
        up_out[:, half * unit : (half + 1) * unit] = up[half].T
    for half in range(2):
        turned = down[half].T
        for g in range(FF // 2 // unit):
            at = (2 * g + half) * unit
            down_out[at : at + unit, :] = turned[g * unit : (g + 1) * unit, :]
    host.run(0, len(host.events))
    host.settle()

    def chosen(index, half):
        return jnp.where(core == 0, host.sums[index][half], held[index][half])

    for half in range(2):
        turned = chosen(0, half).T
        if compact:
            heads = half_cols // DH // 2
            for low in range(2):
                for i in range(heads):
                    to = (half * 2 * heads + 2 * i + low) * DH
                    at = (low * heads + i) * DH
                    out_out[to : to + DH, :] = turned[at : at + DH, :]
        else:
            out_out[half * half_cols : (half + 1) * half_cols, :] = turned
        value = chosen(1, half)
        if compact:
            low = group.low
            pieces = [value[i * DH : (i + 1) * DH, :] for i in range(4)]
            ordered_pieces = (
                jnp.where(low == 0, pieces[0], pieces[1]),
                pieces[3],
                jnp.where(low == 0, pieces[1], pieces[2]),
            )
            for i, piece in enumerate(ordered_pieces):
                joint_out[half * half_cols : (half + 1) * half_cols, i * DH : (i + 1) * DH] = piece.T
        else:
            joint_out[half * half_cols : (half + 1) * half_cols, :] = value.T
    small = chosen(2, 0) + chosen(2, 1)
    at = 0
    for out in vec_outs:
        size = out.shape[1]
        for start in range(0, size, 128):
            take_lanes = min(128, size - start)
            row, lane = (at + start) // 128, (at + start) % 128
            out[:, start : start + take_lanes] = small[row : row + 1, lane : lane + take_lanes]
        at += size
    rows_copy.wait()


def final_call(host, arrays, downs, ups, others, rows_src, collective_id):
    rows = rows_src.shape[0]
    groups = host.dp_count * host.count
    unit = D // groups
    anywhere = pl.BlockSpec(memory_space=pl.ANY)
    vmem = pl.BlockSpec(memory_space=pltpu.VMEM)
    sizes = [unit] * 8 + [FF // groups]
    return pl.pallas_call(
        functools.partial(final_kernel, host),
        in_specs=[anywhere] * (host.arrays + 8),
        out_specs=[vmem] * 13 + [anywhere],
        out_shape=[
            jax.ShapeDtypeStruct((D, FF // groups), F32),
            jax.ShapeDtypeStruct((FF, unit), F32),
            jax.ShapeDtypeStruct((D, unit), F32),
            jax.ShapeDtypeStruct((D, 3 * unit), F32),
        ]
        + [jax.ShapeDtypeStruct((1, size), F32) for size in sizes]
        + [jax.ShapeDtypeStruct((2, rows, D), BF16)],
        scratch_shapes=[
            pltpu.VMEM(downs[0].shape, F32),
            pltpu.VMEM(ups[0].shape, F32),
        ]
        + [pltpu.VMEM(o.shape, F32) for o in others]
        + [pltpu.SemaphoreType.DMA((5,))]
        + deliver_sems()
        + host.scratch(),
        compiler_params=pltpu.CompilerParams(
            vmem_limit_bytes=VMEM_LIMIT, collective_id=collective_id, has_side_effects=True
        ),
        cost_estimate=pl.CostEstimate(
            flops=10**9, bytes_accessed=60 * 2**20, transcendentals=0
        ),
    )(*host.views(arrays), *downs, *ups, *others, rows_src)


def swap(value, axis, mask):
    count = lax.axis_size(axis)
    return lax.ppermute(value, axis, [(i, i ^ mask) for i in range(count)])


def take(value, index, dim):
    return lax.dynamic_index_in_dim(value, index, dim, keepdims=False)


def ordered(bit, mine, other, dim):
    return jnp.where(
        bit == 0,
        jnp.stack([mine, other], axis=dim),
        jnp.stack([other, mine], axis=dim),
    )


def key_bias(counts, rotate):
    places = jnp.arange(LEN, dtype=jnp.int32)
    places = jnp.where(rotate, (places + LEN // 2) % LEN, places)
    offset = jnp.maximum(places - TRI, 0)
    view_index = offset // VSLOT
    inside = offset - view_index * VSLOT
    match = view_index[:, None] == jnp.arange(VIEWS, dtype=jnp.int32)[None, :]
    limits = jnp.sum(jnp.where(match, counts[None, :], 0), axis=1)
    valid = (places < TRI) | (inside < limits)
    return jnp.where(valid, 0.0, -1e30).astype(F32)[None, :]


def shards(
    inputs,
    cotangent,
    view_tokens,
    ln1_gain,
    ln1_bias,
    w_qkv,
    b_query,
    b_value,
    w_out,
    b_out,
    ln2_gain,
    ln2_bias,
    w_up,
    b_up,
    w_down,
    b_down,
):
    core = lax.axis_index("section")
    place = lax.axis_index("seq")
    dp_index = lax.axis_index("dp")
    count = lax.axis_size("seq")
    dp_count = lax.axis_size("dp")
    groups = dp_count * count
    half = count // 2
    micro = place // half
    low = place % half
    low_bits = half.bit_length() - 1
    rows = inputs.shape[2]
    width = D // count
    rank = core * half + low

    def swap_core(value):
        return swap(value, "section", 1)

    def swap_seq(value, bit):
        return swap(value, "seq", 1 << bit)

    def low_bit(bit):
        return (place >> bit) & 1

    def own_rows(local):
        chunks = local[:, 0]
        far = lax.ppermute(
            take(chunks, 1 - micro, 0),
            ("section", "seq"),
            [(count + z, count + (z ^ half)) for z in range(count)],
        )
        return jnp.where(core == 0, take(chunks, micro, 0), far)

    def gather_rows(own):
        value = own[None]
        for bit in range(low_bits):
            other = swap_seq(value, bit)
            value = ordered(low_bit(bit), value, other, 0).reshape((-1,) + own.shape)
        value = ordered(core, value, swap_core(value), 0)
        return value.reshape((-1,) + own.shape[1:])

    def exchange(value):
        tail = value.shape[1:]
        value = value.reshape((2,) * (low_bits + 1) + tail)
        for bit in range(low_bits):
            dim = low_bits - bit
            mine = take(value, low_bit(bit), dim)
            other = swap_seq(take(value, 1 - low_bit(bit), dim), bit)
            value = ordered(low_bit(bit), mine, other, dim)
        mine = take(value, core, 0)
        other = swap_core(take(value, 1 - core, 0))
        return ordered(core, mine, other, 0).reshape((count,) + tail)

    compact = half == 2
    span = half * width

    def vector_to(value):
        if compact:
            wide = jnp.stack(
                [jnp.where(low == i, value.reshape(2, -1, DH), 0.0) for i in range(2)], axis=2
            )
        else:
            wide = jnp.stack([jnp.where(low == i, value, 0.0) for i in range(half)], axis=1)
        wide = wide.reshape(2, span)
        return jnp.concatenate([jnp.where(core == i, wide, 0.0) for i in range(2)], axis=1)

    def rank_rows(value):
        if compact:
            value = value.reshape(2, width // DH, 2, DH, D)
            return jnp.swapaxes(value, 1, 2).reshape(D, D)
        return value

    out_mine = rank_rows(w_out[0])
    ups = (w_up[0], swap_core(w_up[0]))
    downs = (w_down[0], swap_core(w_down[0]))
    bias_mask = key_bias(take(view_tokens[:, 0], micro, 0), micro == 1)

    saved = []
    acts = []
    for layer in range(2):
        if layer == 0:
            o_own, lse, a1, q, k, v, layer_in, joint_pair, out_other, vec = attend_call(
                True,
                0,
                bias_mask,
                count,
                dp_count,
                inputs,
                w_qkv,
                out_mine[None],
                ln1_gain,
                ln1_bias,
                b_query,
                b_value,
                b_out,
                ln2_gain,
                ln2_bias,
                b_down,
                b_up,
            )
            outs_pair = (out_mine, out_other)
        else:
            o_own, lse, a1, q, k, v, d_out_all, first_rows = attend_call(
                False, 1, bias_mask, count, dp_count, layer_in, joint_pair[1], vec[1:2], cotangent
            )
        hidden, upper, output, a2_all, o_all, gated_all = mlp_call(
            layer, o_own, layer_in, outs_pair, vec, ups, downs
        )
        acts.append(output)
        saved.append((layer_in, a1, q, k, v, lse, hidden, upper, a2_all, o_all, gated_all))
        layer_in = output

    def hosted(arrays, spans=None):
        shapes = []
        for array in arrays:
            shapes.append((array.shape[1], array.shape[2], array.shape[0] != groups, array.dtype))
        return Hosted(dp_count, count, tuple(shapes), spans)

    results = [{}, {}]
    pending = None
    d_out = d_out_all[0]
    for layer in (1, 0):
        x_own, a1, q, k, v, lse, hidden, upper, a2_all, o_all, gated_all = saved[layer]
        g_down = mm_tn(d_out_all.reshape(2 * rows, D), gated_all.reshape(2 * rows, FF // 2))
        g_down = g_down.astype(BF16).reshape(groups, D // groups, FF // 2)
        up_like = jax.ShapeDtypeStruct((groups, FF // groups // 2, D), BF16)
        if pending is None:
            arrays = [g_down]
            host = hosted(arrays + [up_like], ((0, 0.0, 52.0), (1, 28.0, 84.0)))
        else:
            arrays = list(pending) + [g_down]
            host = hosted(
                arrays + [up_like],
                ((0, 0.0, 30.0), (0, 0.0, 30.0), (0, 0.0, 30.0), (0, 5.0, 68.0), (1, 40.0, 105.0)),
            )
        (g_bup, sums_two, sums_one, sums_qv, g_up, d_in, g_joint, g_out, given, *reduced) = back_call(
            layer,
            d_out,
            hidden,
            outs_pair,
            vec,
            upper,
            a2_all,
            ups,
            downs,
            acts[1] if pending is None else d_out,
            (q, k, v, lse, a1, joint_pair[layer], x_own, o_all),
            bias_mask,
            host,
            arrays,
        )
        if pending is None:
            second_rows = given
        else:
            second_grads = given
            for name in ("out", "joint", "small"):
                results[1][name] = reduced.pop(0)
        results[layer]["down"], results[layer]["up"] = reduced
        g_out = g_out.reshape(groups, D // groups, D // 2)
        if compact:
            g_joint = g_joint.reshape(groups // 2, 3 * D // groups, D // 2)
        else:
            spread = jnp.stack(
                [jnp.where(low == i, g_joint, jnp.zeros_like(g_joint)) for i in range(half)], axis=2
            )
            g_joint = spread.reshape(groups, 3 * D // groups, D // 2)
        wide = vector_to(sums_qv[0:2])
        rows_of = jnp.concatenate([sums_one[0:2], wide, sums_two[2:3], sums_two[0:2], sums_two[3:4]])
        small = jnp.concatenate(
            [
                jnp.swapaxes(rows_of.reshape(8, groups, D // groups), 0, 1).reshape(groups, -1),
                g_bup.reshape(groups, FF // groups),
            ],
            axis=1,
        )
        lines = -(-small.shape[1] // 128)
        lines += -lines % 8
        small = jnp.pad(small, ((0, 0), (0, lines * 128 - small.shape[1])))
        small = small.reshape(groups, lines, 128)
        if pending is None:
            pending = (g_out, g_joint, small)
        else:
            arrays = (g_out, g_joint, small)
            results[0]["last"] = final_call(
                hosted(arrays),
                arrays,
                (results[0]["down"], results[1]["down"]),
                (results[0]["up"], results[1]["up"]),
                [results[1][name] for name in ("out", "joint", "small")],
                d_in[0],
                4,
            )
        d_out = d_in[0]
        d_out_all = d_in

    g_w_up, g_w_down, g_w_out, g_w_qkv, *pieces, first_grads = results[0]["last"]
    acts_rows = jnp.where(core == 0, first_rows, second_rows)
    grad_rows = jnp.where(core == 0, first_grads, second_grads)
    g_ln1g, g_ln1b, g_bq, g_bv, g_bo, g_ln2g, g_ln2b, g_bd, g_bup = pieces
    return (
        acts_rows[None, :, None],
        grad_rows[None, :, None],
        g_ln1g,
        g_ln1b,
        g_w_qkv[None],
        g_bq,
        g_bv,
        g_w_out[None],
        g_bo,
        g_ln2g,
        g_ln2b,
        g_w_up[None],
        g_bup,
        g_w_down[None],
        g_bd,
    )


def solution(mesh):
    rows = P(None, "dp", "seq", None)
    vector = P("section", None)
    matrix = P("section", None, None)
    placed = (
        rows,
        rows,
        P(None, "dp", None),
        vector,
        vector,
        matrix,
        vector,
        vector,
        matrix,
        vector,
        vector,
        vector,
        matrix,
        vector,
        matrix,
        vector,
    )
    both = P("section", None, "dp", "seq", None)
    line = P("section", ("dp", "seq"))
    table = P("section", None, ("dp", "seq"))
    return jax.shard_map(
        shards,
        mesh=mesh,
        in_specs=placed,
        out_specs=(
            both,
            both,
            line,
            line,
            table,
            line,
            line,
            table,
            line,
            line,
            line,
            table,
            line,
            table,
            line,
        ),
        check_vma=False,
    )
```

time: 582 us -> 533 us (0.916)
  the two profiles are of different devices: /device:TPU:1 before, /device:TPU:9 now
where the time goes in v4:
time: 533 us; the launch traced here: 523 us
  Pallas kernels  465 us (87%)
  local copies, waits for them, and re-layouts  34.3 us (6%)
  matrix products  14.4 us (3%)
  other arithmetic  6.94 us (1%)
    pallas_call x2, Pallas kernels, back_call(): pl.pallas_call(functools.partial(back_kernel, layer, host, ranges), grid=...  277 us
    pallas_call x2, Pallas kernels, attend_call(): pl.pallas_call(functools.partial(attend_kernel, first, layer, dp_count),...  90.9 us
    pallas_call x2, Pallas kernels, mlp_call(): pl.pallas_call(functools.partial(mlp_kernel, layer), grid=(NCH + 1,), in_...  49.2 us
    pallas_call x1, Pallas kernels, final_call(): pl.pallas_call(functools.partial(final_kernel, host), in_specs=[anywhere]...  47.6 us
    dot_general x2, matrix products, mm_tn(): lax.dot_general(a, b, (((0,), (0,)), ((), ())), preferred_element_type=F32)  14.4 us
    unnamed x53, local copies, waits for them, and re-layouts  13.7 us
  transfers between devices with their start and end apart: 2, of which 0 were waited for; matrix products, arithmetic and copies ran while one was open for 2% of the time, Pallas kernels for 9%

profile of v4, /device:TPU:9, one launch (start us, length us, event | category | flops | bytes accessed | tf_op | source)
XLA Modules:
  0.0 522.6 jit_solution(524395984830808057)
XLA Ops:
  0.7 0.7 collective-permute-start
  1.5 3.1 copy.43
  4.7 0.6 or_select_fusion.refs_3_.refs_2_.refs_1_
  5.4 45.1 %shard_map.271 = (bf16[4,320,256]{2,1,0:T(8,128)(2,1)}, f32[1280,128]{1,0:T(8,128)}, bf16[1280,1024]{1,0:T(8,128)(2,1)}, bf16[1280,256]{1,0:T(8,128)(2,1)}, bf16...) custom-call(bf16[2,1,320,1024]{3,2,1,0:T(8,128)(2,1)} %refs_0_.1, ...), custom_call_target="tpu_custom_call" | custom-call | flops 40000000000 | bytes 20971520 | tf_op jit(solution)/shard_map/pallas_call | solution.py:777
  50.4 1.5 slice.50.refs_3_
  51.9 3.7 slice_bitcast_fusion
  55.6 21.8 %shard_map.272 = (f32[320,1024]{1,0:T(8,128)}, f32[320,4096]{1,0:T(8,128)}, bf16[320,1024]{1,0:T(8,128)(2,1)}, bf16[2,320,1024]{2,1,0:T(8,128)(2,1)}, bf16[2,320...) custom-call(bf16[4,320,256]{2,1,0:T(8,128)(2,1)} %get-tuple-element.82.o_ref, ...), custom_call_target="tpu_custom_call" | custom-call | flops 6039797760 | bytes 31457280 | tf_op jit(solution)/shard_map/pallas_call | solution.py:921
  77.5 45.9 %shard_map.273 = (bf16[4,320,256]{2,1,0:T(8,128)(2,1)}, f32[1280,128]{1,0:T(8,128)}, bf16[1280,1024]{1,0:T(8,128)(2,1)}, bf16[1280,256]{1,0:T(8,128)(2,1)}, bf16...) custom-call(bf16[320,1024]{1,0:T(8,128)(2,1)} %get-tuple-element.86., ...), custom_call_target="tpu_custom_call" | custom-call | flops 40000000000 | bytes 20971520 | tf_op jit(solution)/shard_map/pallas_call | solution.py:777
  123.3 2.0 slice_bitcast_fusion.4.refs_3_
  125.3 27.4 %shard_map.274 = (f32[320,1024]{1,0:T(8,128)}, f32[320,4096]{1,0:T(8,128)}, bf16[320,1024]{1,0:T(8,128)(2,1)}, bf16[2,320,1024]{2,1,0:T(8,128)(2,1)}, bf16[2,320...) custom-call(bf16[4,320,256]{2,1,0:T(8,128)(2,1)} %get-tuple-element.89.o_ref, ...), custom_call_target="tpu_custom_call" | custom-call | flops 6039797760 | bytes 31457280 | tf_op jit(solution)/shard_map/pallas_call | solution.py:921
  152.7 6.8 %bitcast_convert_fusion.1 = bf16[1024,2048]{1,0:T(8,128)(2,1)} fusion(bf16[2,320,1024]{2,1,0:T(8,128)(2,1)S(1)} %copy-done.6, bf16[2,320,2048]{2,1,0:T(8,128)(2,1)} %get-tuple-element.101), kind=kOutput, calls=%fused_computation.1 | convolution fusion | flops 2686451712 | bytes 8126464 | tf_op jit(solution)/shard_map/dot_general | solution.py:42
  159.5 117.5 %shard_map.275 = (f32[1,4096]{1,0:T(1,128)}, f32[8,1024]{1,0:T(8,128)}, f32[8,1024]{1,0:T(8,128)}, f32[8,256]{1,0:T(8,128)}, bf16[2,2,2,2,128,1024]{5,4,3,2,1,0:...) custom-call(f32[320,4096]{1,0:T(8,128)} %get-tuple-element.90.refs_0, ...), custom_call_target="tpu_custom_call" | custom-call | flops 99999997952 | bytes 62914560 | tf_op jit(solution)/shard_map/pallas_call | solution.py:1310
  277.0 0.8 fusion.10
  277.8 0.8 slice.57
  278.6 2.0 slice_bitcast_fusion.3.refs_3_.refs_12_
  280.6 7.7 %bitcast_convert_fusion = bf16[1024,2048]{1,0:T(8,128)(2,1)} fusion(bf16[2,320,1024]{2,1,0:T(8,128)(2,1)} %get-tuple-element.104, bf16[2,320,2048]{2,1,0:T(8,128)(2,1)} %get-tuple-element.119), kind=kOutput, calls=%fused_computation | convolution fusion | flops 2686451712 | bytes 8126464 | tf_op jit(solution)/shard_map/dot_general | solution.py:42
  288.2 0.7 broadcast_select_fusion.6
  289.3 0.8 slice.54
  290.8 0.7 reduce.6
  292.2 159.7 %shard_map.276 = (f32[1,4096]{1,0:T(1,128)}, f32[8,1024]{1,0:T(8,128)}, f32[8,1024]{1,0:T(8,128)}, f32[8,256]{1,0:T(8,128)}, bf16[2,2,2,2,128,1024]{5,4,3,2,1,0:...) custom-call(f32[320,4096]{1,0:T(8,128)} %get-tuple-element.103.refs_, ...), custom_call_target="tpu_custom_call" | custom-call | flops 99999997952 | bytes 62914560 | tf_op jit(solution)/shard_map/pallas_call | solution.py:1310
  451.9 0.8 fusion.9
  452.8 0.8 slice.62
  453.5 2.0 slice_bitcast_fusion.2.refs_10_
  455.5 0.7 broadcast_select_fusion.5
  456.6 0.8 slice.59
  457.6 0.7 reduce.7
  459.0 47.6 %shard_map.277 = (f32[1024,256]{1,0:T(8,128)}, f32[4096,64]{1,0:T(8,128)}, f32[1024,64]{1,0:T(8,128)}, f32[1024,192]{1,0:T(8,128)}, f32[1,64]{1,0:T(1,128)}, /*i...) custom-call(bf16[2,2,2,2,64,512]{5,4,3,2,1,0:T(8,128)(2,1)} %bitcast, ...), custom_call_target="tpu_custom_call" | custom-call | flops 1000000000 | bytes 62914560 | tf_op jit(solution)/shard_map/pallas_call | solution.py:1507
  506.5 3.2 copy.54
  509.7 2.6 copy.52
  512.3 0.9 copy.53
  513.3 3.4 select_bitcast_fusion
  520.3 1.0 copy.76
  (86 shorter events, 8.0 us)
Async XLA Ops:
  0.6 4.0 copy-start
  0.7 54.9 %collective-permute-start = (bf16[1024,4096]{1,0:T(8,128)(2,1)}, bf16[1024,4096]{1,0:T(8,128)(2,1)}, u32[]{:S(2)}, u32[]{:S(2)}) collective-permute-start(bf16[1024,4096]{1,0:T(8,128)(2,1)} %bitcast.56), channel_id=1, source_target_pairs={{0,16},{16,0},{1,17},{17,1},{2,18},{18,2},{3,19},{19,3},{4,20},{20... | collective-permute-start | bytes 25165832 | tf_op jit(solution)/shard_map/ppermute | solution.py:1538
  1.4 54.2 %collective-permute-start.1 = (bf16[4096,1024]{1,0:T(8,128)(2,1)}, bf16[4096,1024]{1,0:T(8,128)(2,1)}, u32[]{:S(2)}, u32[]{:S(2)}) collective-permute-start(bf16[4096,1024]{1,0:T(8,128)(2,1)} %bitcast.61), channel_id=1, source_target_pairs={{0,16},{16,0},{1,17},{17,1},{2,18},{18,2},{3,19},{19,3},{4,20},{20... | collective-permute-start | bytes 25165832 | tf_op jit(solution)/shard_map/ppermute | solution.py:1538
  125.3 27.4 %copy-start.6 = (bf16[2,320,1024]{2,1,0:T(8,128)(2,1)S(1)}, bf16[2,320,1024]{2,1,0:T(8,128)(2,1)}, u32[]{:S(2)}) copy-start(bf16[2,320,1024]{2,1,0:T(8,128)(2,1)} %get-tuple-element.91) | copy-start | bytes 3932164
  280.6 10.3 %copy-start.8 = (f32[1,4096]{1,0:T(1,128)S(1)}, f32[1,4096]{1,0:T(1,128)}, u32[]{:S(2)}) copy-start(f32[1,4096]{1,0:T(1,128)} %get-tuple-element.118) | copy-start | bytes 49156
  451.9 5.7 %copy-start.7 = (f32[1,4096]{1,0:T(1,128)S(1)}, f32[1,4096]{1,0:T(1,128)}, u32[]{:S(2)}) copy-start(f32[1,4096]{1,0:T(1,128)} %get-tuple-element.125) | copy-start | bytes 49156
  506.5 5.8 %copy-start.5 = (f32[1024,64]{1,0:T(8,128)S(1)}, f32[1024,64]{1,0:T(8,128)}, u32[]{:S(2)}) copy-start(f32[1024,64]{1,0:T(8,128)} %get-tuple-element.141) | copy-start | bytes 786436
  509.7 3.5 copy-start.2
  509.7 3.5 copy-start.3
  513.2 3.5 copy-start.17
  513.2 4.0 copy-start.16
  513.2 4.5 copy-start.15
  513.2 5.0 copy-start.14
  513.2 5.5 %copy-start.13 = (f32[1,64]{1,0:T(1,128)S(1)}, f32[1,64]{1,0:T(1,128)}, u32[]{:S(2)}) copy-start(f32[1,64]{1,0:T(1,128)} %get-tuple-element.218) | copy-start | bytes 772
  513.3 6.0 %copy-start.12 = (f32[1,64]{1,0:T(1,128)S(1)}, f32[1,64]{1,0:T(1,128)}, u32[]{:S(2)}) copy-start(f32[1,64]{1,0:T(1,128)} %get-tuple-element.219) | copy-start | bytes 772
  513.3 6.5 %copy-start.11 = (f32[1,64]{1,0:T(1,128)S(1)}, f32[1,64]{1,0:T(1,128)}, u32[]{:S(2)}) copy-start(f32[1,64]{1,0:T(1,128)} %get-tuple-element.220) | copy-start | bytes 772
  513.3 7.0 %copy-start.4 = (f32[1024,256]{1,0:T(8,128)S(1)}, f32[1024,256]{1,0:T(8,128)}, u32[]{:S(2)}) copy-start(f32[1024,256]{1,0:T(8,128)} %get-tuple-element.145) | copy-start | bytes 3145732
  513.3 9.0 %copy-start.1 = (s32[2,1,6]{2,1,0:T(1,128)S(1)}, s32[2,1,6]{2,1,0:T(1,128)}, u32[]{:S(2)}) copy-start(s32[2,1,6]{2,1,0:T(1,128)} %param.18) | copy-start | bytes 148
  516.7 4.6 copy-start.9
  516.7 5.1 copy-start.10
